TPU v7x, 32 devices: a whole 2x2x4 slice. The times are simulated.
32 devices in a mesh: groups: 1, tensor: 16 (over z, y, core), adapter: 2 (over x).
Axes of the slice: x: 2, y: 2, z: 4, core: 2. Of those that a mesh axis runs over, the one named last changes fastest.
Arguments:
- hidden_input: bfloat16 [4096, 8192], P(('groups', 'tensor'), 'adapter'), may hold values from -6 to 6
- value_matrix: bfloat16 [8192, 1024], P('adapter', 'tensor'), may hold values from -0.0625 to 0.0625
- adapter_down_weight: bfloat16 [16, 8192, 16], P('tensor', 'adapter'), may hold values from -0.0625 to 0.0625
- adapter_up_weight: bfloat16 [16, 16, 1024], P('tensor'), may hold values from -1.5 to 1.5
- adapter_per_block: int32 [32], P(('groups', 'tensor')), may hold values from 0 to 15
- live_block_rows: int32 [32], P(('groups', 'tensor')), may hold values from 1 to 128
Outputs:
- values_out: bfloat16 [4096, 1024], P(('groups', 'tensor'), 'adapter')
All inputs are finite; a program needn't handle non-finite values.
Results may differ from a plain program's by a relative error of at most 0.0038.
Values may be sent and summed in bfloat16 or wider, within the bound.
No kernel may reach another device: no remote copies, remote signals or barrier semaphores. Data moves between devices by JAX's collectives and lax.ppermute only.
A program may use at most 64 MiB of HBM per device.

v0:
```python
import jax
import jax.numpy as jnp
from jax import lax
from jax.sharding import PartitionSpec as P

ADAPTER_RANK = 16
BLK = 128


def body(
    hidden_input,
    value_matrix,
    adapter_down_weight,
    adapter_up_weight,
    adapter_per_block,
    live_block_rows,
):
    rows_here, quarter = hidden_input.shape
    blocks_here = rows_here // BLK
    output_width = adapter_up_weight.shape[2]
    input_blocks = hidden_input.reshape(blocks_here, BLK, quarter)
    base_part = jnp.dot(
        hidden_input,
        lax.all_gather(value_matrix, "tensor", axis=1, tiled=True),
        preferred_element_type=jnp.float32,
    )
    down_portion = lax.all_gather(adapter_down_weight, "tensor", axis=0, tiled=True)
    up_portion = lax.all_gather(adapter_up_weight, "tensor", axis=0, tiled=True)
    wanted = jnp.arange(down_portion.shape[0], dtype=jnp.int32)
    onehot = (adapter_per_block[:, None] == wanted[None, :]).astype(jnp.bfloat16)
    chosen_down = jnp.einsum(
        "bn,ndr->bdr", onehot, down_portion, preferred_element_type=jnp.float32
    )
    chosen_up = jnp.einsum("bn,nrv->brv", onehot, up_portion, preferred_element_type=jnp.float32)
    collected_rows, chosen_up = (chosen_down, chosen_up)
    shrink = jnp.einsum(
        "fiu,fun->fin",
        input_blocks,
        collected_rows.astype(jnp.bfloat16),
        preferred_element_type=jnp.float32,
    )
    live_mask = jnp.arange(BLK, dtype=jnp.int32)[None, :, None] < live_block_rows[:, None, None]
    shrink = jnp.where(live_mask, shrink, jnp.zeros_like(shrink))
    up_bf = chosen_up.astype(jnp.bfloat16)
    base_own, shrink_own = (
        lax.psum_scatter(base_part, "adapter", scatter_dimension=0, tiled=True),
        lax.psum_scatter(
            shrink.reshape(rows_here, ADAPTER_RANK), "adapter", scatter_dimension=0, tiled=True
        ),
    )
    own_rows = base_own.shape[0]
    own_blocks = own_rows // BLK
    up_own = lax.dynamic_slice_in_dim(up_bf, lax.axis_index("adapter") * own_blocks, own_blocks, 0)
    shrink_bf = shrink_own.astype(jnp.bfloat16).reshape(own_blocks, BLK, ADAPTER_RANK)
    low_rank = jnp.einsum("bkr,brv->bkv", shrink_bf, up_own, preferred_element_type=jnp.float32)
    owned = (base_own + low_rank.reshape(own_rows, output_width)).astype(jnp.bfloat16)
    return lax.all_to_all(owned, "adapter", split_axis=1, concat_axis=0, tiled=True)


def solution(mesh):
    in_specs = (
        P(("groups", "tensor"), "adapter"),
        P("adapter", "tensor"),
        P("tensor", "adapter", None),
        P("tensor", None, None),
        P(("groups", "tensor")),
        P(("groups", "tensor")),
    )
    out_specs = P(("groups", "tensor"), "adapter")
    return jax.shard_map(body, mesh=mesh, in_specs=in_specs, out_specs=out_specs, check_vma=False)
```

profile of v0, /device:TPU:0, one launch (start us, length us, event | category | flops | bytes accessed | tf_op | source)
XLA Modules:
  0.0 178.6 jit_solution(10084196100375000641)
XLA Ops:
  6.5 0.0 copy-start
  6.5 0.0 all-gather.5.cloned.1.call-start
  6.5 0.7 all-gather.5.cloned.1.call-update
  7.3 0.0 all-gather.3.cloned.1.call-start
  7.3 0.7 all-gather.3.cloned.1.call-update
  8.0 0.0 reduce-scatter.5.cloned.1.call-start
  8.1 0.7 iota_compare_fusion.3
  8.8 44.9 %all-gather.5.cloned.1.call-done = bf16[16,4096,16]{1,2,0:T(8,128)(2,1)} async-done(((bf16[1,4096,16]{1,2,0:T(8,128)(2,1)}), bf16[16,4096,16]{1,2,0:T(8,128)(2,1)}) %all-gather.5.cloned.1.call-update) | async-done | bytes 2097168 | tf_op jit(solution)/shard_map/all_gather | solution.py:27
  53.7 4.0 %convolution_convert_fusion = bf16[2,4096,16]{1,0,2:T(2,128)(2,1)S(1)} fusion(bf16[16,4096,16]{1,2,0:T(8,128)(2,1)} %all-gather.5.cloned.1.call-done, s32[2]{0:T(128)} %param.10), kind=kOutput, calls=%fused_computation | convolution fusion | flops 4325408 | bytes 2359304 | tf_op jit(solution)/shard_map/bn,ndr->bdr/dot_general | solution.py:31
  57.6 0.0 copy-done
  57.6 0.7 fusion.2
  58.3 0.6 copy.33
  58.9 0.0 reduce-scatter.5.cloned.1.call-update
  58.9 0.0 copy-start.1
  59.0 0.0 copy-start.2
  59.0 0.0 reduce-scatter.3.cloned.1.call-start
  59.0 70.5 %all-gather.3.cloned.1.call-done = bf16[4096,1024]{0,1:T(8,128)(2,1)} async-done(((bf16[4096,64]{0,1:T(8,128)(2,1)}), bf16[4096,1024]{0,1:T(8,128)(2,1)}) %all-gather.3.cloned.1.call-update) | async-done | bytes 8388624 | tf_op jit(solution)/shard_map/all_gather | solution.py:24
  129.5 6.8 %fusion.13 = f32[256,1024]{1,0:T(8,128)} fusion(bf16[256,4096]{1,0:T(8,128)(2,1)S(1)} %copy-done, bf16[4096,1024]{0,1:T(8,128)(2,1)} %all-gather.3.cloned.1.call-done), kind=kOutput, calls=%fused_computation.21 | convolution fusion | flops 2147483648 | bytes 11534336 | tf_op jit(solution)/shard_map/dot_general | solution.py:22
  136.3 0.0 reduce-scatter.3.cloned.1.call-update
  136.3 0.0 copy-done.1
  136.3 20.2 %all_gather.11 = bf16[16,16,1024]{2,1,0:T(8,128)(2,1)S(1)} all-gather(bf16[1,16,1024]{2,1,0:T(8,128)(2,1)S(1)} %copy-done.1), channel_id=1, replica_groups=mesh['groups'=1,'tensor'=16,'adapter'=2] {'tensor'}, dimensions={0}, use_global_device_ids=true | all-gather | bytes 557056 | tf_op jit(solution)/shard_map/all_gather | solution.py:28
  156.5 0.0 copy-done.2
  156.5 0.4 fusion.3
  156.9 0.1 dynamic-slice_convert_fusion
  157.0 0.0 reduce-scatter.5.cloned.1.call-done
  157.0 5.2 %reduce-scatter.3.cloned.1.call-done = f32[128,1024]{1,0:T(8,128)} async-done(((f32[256,1024]{1,0:T(8,128)}), f32[128,1024]{1,0:T(8,128)}) %reduce-scatter.3.cloned.1.call-update) | async-done | bytes 524304 | tf_op jit(solution)/shard_map/reduce_scatter | solution.py:46
  162.2 1.3 fusion.1
  163.5 7.8 %all_to_all.19 = bf16[128,2,512]{2,0,1:T(8,128)(2,1)S(1)} all-to-all(bf16[128,2,512]{2,0,1:T(8,128)(2,1)S(1)} %bitcast.27), channel_id=1, replica_groups=mesh['groups'=1,'tensor'=16,'adapter'=2] {'adapter'}, dimensions={1} | all-to-all | bytes 524288 | tf_op jit(solution)/shard_map/all_to_all | solution.py:57
  171.4 0.7 copy.35
  (1 shorter events, 0.0 us)
Async XLA Ops:
  6.5 51.1 %copy-start = (bf16[256,4096]{1,0:T(8,128)(2,1)S(1)}, bf16[256,4096]{1,0:T(8,128)(2,1)}, u32[]{:S(2)}) copy-start(bf16[256,4096]{1,0:T(8,128)(2,1)} %param.6) | copy-start | bytes 6291460
  6.5 47.1 %all-gather.5.cloned.1.call-start = ((), (), s32[]{:S(2)}) async-start(), calls=%async_computation.5 | async-start | bytes 2228224 | tf_op jit(solution)/shard_map/all_gather | solution.py:27
  7.3 122.3 %all-gather.3.cloned.1.call-start = ((), (), s32[]{:S(2)}) async-start(), calls=%async_computation.3 | async-start | bytes 8912896 | tf_op jit(solution)/shard_map/all_gather | solution.py:24
  8.0 149.0 %reduce-scatter.5.cloned.1.call-start = ((), (), s32[]{:S(2)}) async-start(), calls=%async_computation.6 | async-start | bytes 24576 | tf_op jit(solution)/shard_map/reduce_scatter | solution.py:47
  58.9 77.4 %copy-start.1 = (bf16[1,16,1024]{2,1,0:T(8,128)(2,1)S(1)}, bf16[1,16,1024]{2,1,0:T(8,128)(2,1)}, u32[]{:S(2)}) copy-start(bf16[1,16,1024]{2,1,0:T(8,128)(2,1)} %param.9) | copy-start | bytes 98308
  59.0 97.6 %copy-start.2 = (s32[2]{0:T(128)S(1)}, s32[2]{0:T(128)}, u32[]{:S(2)}) copy-start(s32[2]{0:T(128)} %param.10) | copy-start | bytes 28
  59.0 103.2 %reduce-scatter.3.cloned.1.call-start = ((), (), s32[]{:S(2)}) async-start(), calls=%async_computation.4 | async-start | bytes 1572864 | tf_op jit(solution)/shard_map/reduce_scatter | solution.py:46
Sparse Core Ops, SparseCore 0:
  9.5 44.0 all-gather.4
  55.8 73.6 all-gather.2
  131.7 8.0 reduce-scatter.4
  141.9 20.2 reduce-scatter.2
where the time goes:
time: 179 us
  waiting for transfers between devices  122 us (68%)
  blocking collectives  28 us (16%)
  between operations  13.2 us (7%)
  matrix products  13.1 us (7%)
    all_gather x1, waiting for transfers between devices, body(): lax.all_gather(value_matrix, 'tensor', axis=1, tiled=True)  70.5 us
    all_gather x1, waiting for transfers between devices, body(): lax.all_gather(adapter_down_weight, 'tensor', axis=0, tiled=True)  44.9 us
    all_gather x1, blocking collectives, body(): up_portion = lax.all_gather(adapter_up_weight, 'tensor', axis=0, tiled=True)  20.2 us
    all_to_all x1, blocking collectives, body(): lax.all_to_all(owned, 'adapter', split_axis=1, concat_axis=0, tiled=True)  7.84 us
    dot_general x1, matrix products, body(): jnp.dot(hidden_input, lax.all_gather(value_matrix, 'tensor', axis=1, tile...  6.79 us
    reduce_scatter x1, waiting for transfers between devices, body(): lax.psum_scatter(base_part, 'adapter', scatter_dimension=0, tiled=True)  5.16 us
    dot_general x1, matrix products, body(): jnp.einsum('bn,ndr->bdr', onehot, down_portion, preferred_element_type=jn...  3.97 us
  transfers between devices with their start and end apart: 4, of which 3 were waited for; matrix products, arithmetic and copies ran while one was open for 7% of the time, Pallas kernels for 0%

commit v1 on v0

v1 whole, which is shorter than its diff:
```python
import jax
import jax.numpy as jnp
from jax import lax
from jax.sharding import PartitionSpec as P

BLK = 128
F32 = jnp.float32
BF16 = jnp.bfloat16


def dot_nt(a, b):
    return lax.dot_general(a, b, (((1,), (1,)), ((), ())), preferred_element_type=F32)


def make_body(tensor, adapters):
    depth = tensor // 4
    low = depth // adapters

    def over_tensor(array, flip):
        return lax.ppermute(array, "tensor", perm=[(i, i ^ flip) for i in range(tensor)])

    def over_adapter(array, flip):
        return lax.ppermute(array, "adapter", perm=[(i, i ^ flip) for i in range(adapters)])

    def over_both(array, flip_t, flip_a):
        pairs = [
            (i * adapters + j, (i ^ flip_t) * adapters + (j ^ flip_a))
            for i in range(tensor)
            for j in range(adapters)
        ]
        return lax.ppermute(array, ("tensor", "adapter"), perm=pairs)

    def body(hidden, value, down, up, chosen, live):
        t, x = lax.axis_index("tensor"), lax.axis_index("adapter")
        z, y, core = t // 4, (t // 2) % 2, t % 2
        rows, features = hidden.shape
        width = value.shape[1]
        homes, rank, wide = up.shape
        blocks = rows // BLK
        first = (blocks // 2) * BLK

        theirs = [over_tensor(hidden[:first], 2), over_tensor(hidden[first:], 2)]
        packet = jnp.concatenate([value.T, down.transpose(0, 2, 1).reshape(homes * rank, features)])
        units = {0: packet}
        bit = depth // 2
        while bit:
            units.update({a ^ bit: over_tensor(u, 4 * bit) for a, u in units.items()})
            bit //= 2
        pairs = {a: (u, over_tensor(u, 1)) for a, u in units.items()}

        ids = jnp.stack([chosen, live])
        ids = jnp.concatenate([ids, over_tensor(ids, 2)], axis=1)
        ups = lax.dynamic_slice_in_dim(up, x * (wide // adapters), wide // adapters, 2)[None]
        bit = 1
        while bit < tensor:
            ups = jnp.concatenate([ups, over_tensor(ups, bit)])
            bit *= 2

        w_all = jnp.concatenate([u[:width] for a in range(depth) for u in pairs[a]])
        d_all = jnp.concatenate([u[width:] for a in range(depth) for u in pairs[a]])

        relative = (ids[0] // homes) ^ t
        here = (relative & 2) == 0
        slot = (relative // 4) * 2 + relative % 2
        which = slot * homes + ids[0] % homes

        ups = ups.reshape(tensor, homes, rank, low, 2, 2, width)
        ups = lax.dynamic_index_in_dim(ups, y, 4, keepdims=False)
        z_low = z % low
        order = [
            lax.dynamic_index_in_dim(ups, z_low ^ a, 3, keepdims=False) for a in range(low)
        ]
        ups = jnp.stack(order, axis=3)
        ups = jnp.where(core == 1, ups[..., ::-1, :], ups)
        ups = ups.reshape(tensor * homes, rank, low * 2 * width)
        up_index = relative * homes + ids[0] % homes

        mine_part = (z // low) ^ x

        def work(x_rows, b0):
            count = x_rows.shape[0] // BLK
            base = dot_nt(x_rows, w_all).reshape(-1, adapters, low * 2 * width)
            kept = lax.dynamic_index_in_dim(base, mine_part, 1, keepdims=False)
            sent = [
                lax.dynamic_index_in_dim(base, mine_part ^ k, 1, keepdims=False)
                for k in range(1, adapters)
            ]
            for k in range(1, adapters):
                kept = kept + over_adapter(sent[k - 1], k)
            shrink = dot_nt(x_rows, d_all).reshape(count, BLK, -1, rank)
            spots = jnp.arange(shrink.shape[2], dtype=jnp.int32)
            hot = (which[b0 : b0 + count, None] == spots) & here[b0 : b0 + count, None]
            alive = jnp.arange(BLK, dtype=jnp.int32) < ids[1, b0 : b0 + count, None]
            mask = hot[:, None, :, None] & alive[:, :, None, None]
            shrink = jnp.where(mask, shrink, 0.0).sum(axis=2)
            return kept, shrink

        def finish(kept, shrink, b0):
            count = shrink.shape[0]
            mid = shrink.astype(BF16)
            picked = jnp.stack(
                [
                    lax.dynamic_index_in_dim(ups, up_index[b], 0, keepdims=False)
                    for b in range(b0, b0 + count)
                ]
            )
            extra = jnp.einsum("bir,brv->biv", mid, picked, preferred_element_type=F32)
            return (kept + extra.reshape(kept.shape)).astype(BF16)

        half = blocks // 2
        kept_own, m_own = work(hidden, 0)
        kept_a, m_a = work(theirs[0], blocks)
        kept_b, m_b = work(theirs[1], blocks + half)
        m = jnp.concatenate([m_own, m_a, m_b])
        for k in range(1, adapters):
            m = m + over_adapter(m, k)
        swapped = over_tensor(m.astype(BF16), 2)
        swapped = jnp.concatenate([swapped[blocks:], swapped[:blocks]])
        m = m.astype(BF16) + swapped

        out_a = over_tensor(finish(kept_a, m[blocks : blocks + half], blocks), 2)
        out_b = over_tensor(finish(kept_b, m[blocks + half :], blocks + half), 2)
        out_own = finish(kept_own, m[:blocks], 0)
        pair = jnp.stack([out_own, jnp.concatenate([out_a, out_b])], axis=1)
        pair = pair.reshape(rows, 2, low, 2, width)
        pair = jnp.where(y == 1, pair[:, ::-1], pair)
        pair = jnp.where(core == 1, pair[:, :, :, ::-1], pair)
        pair = jnp.stack(
            [lax.dynamic_index_in_dim(pair, z_low ^ a, 2, keepdims=False) for a in range(low)],
            axis=1,
        )
        return pair.reshape(rows, wide // adapters)

    return body


def solution(mesh):
    in_specs = (
        P(("groups", "tensor"), "adapter"),
        P("adapter", "tensor"),
        P("tensor", "adapter", None),
        P("tensor", None, None),
        P(("groups", "tensor")),
        P(("groups", "tensor")),
    )
    out_specs = P(("groups", "tensor"), "adapter")
    body = make_body(mesh.shape["tensor"], mesh.shape["adapter"])
    return jax.shard_map(body, mesh=mesh, in_specs=in_specs, out_specs=out_specs, check_vma=False)
```

time: 179 us -> 124 us (0.69)
  waiting for transfers between devices: 122 us -> 48.7 us
  blocking collectives: 28 us -> 0 us
  local copies, waits for them, and re-layouts: 1.43 us -> 25.5 us
  starting transfers between devices: 0.12 us -> 20.3 us
  other arithmetic: 0.73 us -> 7.63 us
  between operations: 13.2 us -> 8.11 us
    all_gather x2 -> x0, waiting for transfers between devices: 115 us -> none  [the longest x1 70.5 us: body(): lax.all_gather(value_matrix, 'tensor', axis=1, tiled=True)]
    ppermute x0 -> x21, waiting for transfers between devices: none -> 48.7 us  [the longest x17 48 us: over_tensor(): lax.ppermute(array, 'tensor', perm=[(i, i ^ flip) for i in range(tensor)])]
    ppermute x0 -> x21, starting transfers between devices: none -> 20.3 us  [the longest x17 16 us: over_tensor(): lax.ppermute(array, 'tensor', perm=[(i, i ^ flip) for i in range(tensor)])]
    all_gather x1 -> x0, blocking collectives: 20.2 us -> none  [body(): up_portion = lax.all_gather(adapter_up_weight, 'tensor', axis=0, tiled=True)]
    unnamed x7 -> x38, local copies, waits for them, and re-layouts: 0.72 us -> 13.4 us
    all_to_all x1 -> x0, blocking collectives: 7.84 us -> none  [body(): lax.all_to_all(owned, 'adapter', split_axis=1, concat_axis=0, tiled=True)]
    slice x0 -> x6, local copies, waits for them, and re-layouts: none -> 5.61 us  [the longest x1 3.08 us: body(): theirs = [over_tensor(hidden[:first], 2), over_tensor(hidden[first:], 2)]]
    reduce_scatter x2 -> x0, waiting for transfers between devices: 5.18 us -> none  [the longest x1 5.16 us: body(): lax.psum_scatter(base_part, 'adapter', scatter_dimension=0, tiled=True)]
  transfers between devices with their start and end apart: 4 -> 21, of which waited for: 3 -> 8; matrix products, arithmetic and copies ran while one was open for 7% -> 32% of each run, Pallas kernels for 0% -> 0%
where the time goes in v1:
time: 124 us; the launch traced here: 123 us
  waiting for transfers between devices  48.7 us (39%)
  local copies, waits for them, and re-layouts  25.5 us (21%)
  starting transfers between devices  20.3 us (16%)
  matrix products  12.6 us (10%)
  between operations  8.11 us (7%)
  other arithmetic  7.63 us (6%)
    ppermute x17, waiting for transfers between devices, over_tensor(): lax.ppermute(array, 'tensor', perm=[(i, i ^ flip) for i in range(tensor)])  48 us
    ppermute x17, starting transfers between devices, over_tensor(): lax.ppermute(array, 'tensor', perm=[(i, i ^ flip) for i in range(tensor)])  16 us
    unnamed x38, local copies, waits for them, and re-layouts  13.4 us
    dot_general x6, matrix products, dot_nt(): lax.dot_general(a, b, (((1,), (1,)), ((), ())), preferred_element_type=F32)  10.6 us
    ppermute x4, starting transfers between devices, over_adapter(): lax.ppermute(array, 'adapter', perm=[(i, i ^ flip) for i in range(adapter...  4.31 us
    slice x1, local copies, waits for them, and re-layouts, body(): theirs = [over_tensor(hidden[:first], 2), over_tensor(hidden[first:], 2)]  3.08 us
    and x3, other arithmetic, work(): hot = (which[b0:b0 + count, None] == spots) & here[b0:b0 + count, None]  2.56 us
  transfers between devices with their start and end apart: 21, of which 8 were waited for; matrix products, arithmetic and copies ran while one was open for 32% of the time, Pallas kernels for 0%

profile of v1, /device:TPU:0, one launch (start us, length us, event | category | flops | bytes accessed | tf_op | source)
XLA Modules:
  0.0 122.8 jit_solution(673381416147639989)
XLA Ops:
  0.0 2.1 %pad_maximum_fusion = bf16[80,4096]{1,0:T(8,128)(2,1)} fusion(bf16[16,4096]{1,0:T(8,128)(2,1)} %bitcast.147, bf16[64,4096]{1,0:T(8,128)(2,1)} %bitcast.142), kind=kLoop, calls=%fused_computation.1 | loop fusion | flops 1310720 | bytes 1310720 | tf_op jit(solution)/shard_map/concatenate | solution.py:43
  2.5 2.6 %collective-permute-start.1 = (bf16[80,4096]{1,0:T(8,128)(2,1)}, bf16[80,4096]{1,0:T(8,128)(2,1)}, u32[]{:S(2)}, u32[]{:S(2)}) collective-permute-start(bf16[80,4096]{1,0:T(8,128)(2,1)} %pad_maximum_fusion), channel_id=1, source_target_pairs={{0,8},{2,10},{4,12},{6,14},{8,0},{10,2},{12,4},{14,6},{16,24},{18,... | collective-permute-start | bytes 1966088 | tf_op jit(solution)/shard_map/ppermute | solution.py:20
  5.1 2.6 %collective-permute-start.3 = (bf16[80,4096]{1,0:T(8,128)(2,1)}, bf16[80,4096]{1,0:T(8,128)(2,1)}, u32[]{:S(2)}, u32[]{:S(2)}) collective-permute-start(bf16[80,4096]{1,0:T(8,128)(2,1)} %pad_maximum_fusion), channel_id=1, source_target_pairs={{0,16},{2,18},{4,20},{6,22},{8,24},{10,26},{12,28},{14,30},{16,0},... | collective-permute-start | bytes 1966088 | tf_op jit(solution)/shard_map/ppermute | solution.py:20
  7.7 3.1 %fusion.25 = (bf16[128,4096]{1,0:T(8,128)(2,1)}, bf16[128,4096]{1,0:T(8,128)(2,1)}) fusion(bf16[256,4096]{1,0:T(8,128)(2,1)} %param.6), kind=kLoop, calls=%fused_computation.99 | loop fusion | bytes 4194304 | tf_op jit(solution)/shard_map/slice | solution.py:42
  10.8 1.5 %collective-permute-start.10 = (bf16[128,4096]{1,0:T(8,128)(2,1)}, bf16[128,4096]{1,0:T(8,128)(2,1)}, u32[]{:S(2)}, u32[]{:S(2)}) collective-permute-start(bf16[128,4096]{1,0:T(8,128)(2,1)} %get-tuple-element.8), channel_id=1, source_target_pairs={{0,4},{2,6},{4,0},{6,2},{8,12},{10,14},{12,8},{14,10},{16,20},{18,... | collective-permute-start | bytes 3145736 | tf_op jit(solution)/shard_map/ppermute | solution.py:20
  14.0 22.1 %collective-permute-done.8 = s32[2,2]{1,0:T(2,128)S(1)} collective-permute-done((s32[2,2]{1,0:T(2,128)S(1)}, s32[2,2]{1,0:T(2,128)S(1)}, u32[]{:S(2)}, u32[]{:S(2)}) %collective-permute-start.8) | collective-permute-done | bytes 48 | tf_op jit(solution)/shard_map/ppermute | solution.py:20
  39.4 1.2 %compare_and_fusion = pred[8]{0:T(512)(128)(4,1)S(1)} fusion(pred[]{:T(512)} %bitcast.20, s32[]{:T(128)} %bitcast.19), kind=kLoop, calls=%fused_computation.79 | loop fusion | flops 16 | bytes 13 | tf_op jit(solution)/shard_map/and | solution.py:92
  40.7 1.3 %compare_and_fusion.1 = pred[8]{0:T(512)(128)(4,1)S(1)} fusion(pred[]{:T(512)} %bitcast.14, s32[]{:T(128)} %bitcast.13), kind=kLoop, calls=%fused_computation.81 | loop fusion | flops 16 | bytes 13 | tf_op jit(solution)/shard_map/and | solution.py:92
  42.2 1.6 %collective-permute-start.14 = (bf16[2,1,16,512]{3,2,0,1:T(8,128)(2,1)S(1)}, bf16[2,1,16,512]{3,2,0,1:T(8,128)(2,1)S(1)}, u32[]{:S(2)}, u32[]{:S(2)}) collective-permute-start(bf16[2,1,16,512]{3,2,0,1:T(8,128)(2,1)S(1)} %pad_maximum_fusion.8), channel_id=1, source_target_pairs={{0,4},{2,6},{4,0},{6,2},{8,12},{10,14},{12,8},{14,10},{16,20},{18,... | collective-permute-start | bytes 98312 | tf_op jit(solution)/shard_map/ppermute | solution.py:20
  52.8 3.7 %collective-permute-done.15 = bf16[4,1,16,512]{3,2,0,1:T(8,128)(2,1)S(1)} collective-permute-done((bf16[4,1,16,512]{3,2,0,1:T(8,128)(2,1)S(1)}, bf16[4,1,16,512]{3,2,0,1:T(8,128)(2,1)S(1)}, u32[]{:S(2)}, u32[]{:S(2)}) %collective-permute-start.15) | collective-permute-done | bytes 65568 | tf_op jit(solution)/shard_map/ppermute | solution.py:20
  57.2 7.4 %collective-permute-done.16 = bf16[8,1,16,512]{3,2,0,1:T(8,128)(2,1)S(1)} collective-permute-done((bf16[8,1,16,512]{3,2,0,1:T(8,128)(2,1)S(1)}, bf16[8,1,16,512]{3,2,0,1:T(8,128)(2,1)S(1)}, u32[]{:S(2)}, u32[]{:S(2)}) %collective-permute-start.16) | collective-permute-done | bytes 131104 | tf_op jit(solution)/shard_map/ppermute | solution.py:20
  66.2 1.4 %rev.9 = bf16[16,1,16,2,2,64]{5,4,3,2,0,1:T(2,128)(2,1)S(1)} reverse(bf16[16,1,16,2,2,64]{5,4,3,2,0,1:T(2,128)(2,1)S(1)} %pad_maximum_fusion.1), dimensions={4} | reverse | bytes 262144 | tf_op jit(solution)/shard_map/rev | solution.py:74
  70.3 1.9 %slice_dynamic-update-slice_fusion.6 = bf16[512,4096]{1,0:T(8,128)(2,1)} fusion(bf16[512,4096]{1,0:T(8,128)(2,1)} %constant_dynamic-update-slice_fusion, bf16[80,4096]{1,0:T(8,128)(2,1)} %collective-permute-done), kind=kLoop, calls=%fused_computation.8 | loop fusion | bytes 1048576
  72.2 1.9 %slice_dynamic-update-slice_fusion.5 = bf16[512,4096]{1,0:T(8,128)(2,1)} fusion(bf16[512,4096]{1,0:T(8,128)(2,1)} %slice_dynamic-update-slice_fusion.6, bf16[80,4096]{1,0:T(8,128)(2,1)} %collective-permute-done.1), kind=kLoop, calls=%fused_computation.7 | loop fusion | bytes 1048576
  74.1 0.9 slice_dynamic-update-slice_fusion.13
  75.0 0.9 slice_dynamic-update-slice_fusion.12
  75.9 11.2 %collective-permute-done.5 = bf16[80,4096]{1,0:T(8,128)(2,1)S(1)} collective-permute-done((bf16[80,4096]{1,0:T(8,128)(2,1)}, bf16[80,4096]{1,0:T(8,128)(2,1)S(1)}, u32[]{:S(2)}, u32[]{:S(2)}) %collective-permute-start.5) | collective-permute-done | bytes 655392 | tf_op jit(solution)/shard_map/ppermute | solution.py:20
  87.9 1.9 %slice_dynamic-update-slice_fusion.3 = bf16[512,4096]{1,0:T(8,128)(2,1)} fusion(bf16[512,4096]{1,0:T(8,128)(2,1)} %slice_dynamic-update-slice_fusion.4, bf16[80,4096]{1,0:T(8,128)(2,1)} %collective-permute-done.3), kind=kLoop, calls=%fused_computation.5 | loop fusion | bytes 1048576
  91.5 0.9 slice_dynamic-update-slice_fusion.10
  94.4 1.8 %fusion.33 = f32[128,128]{1,0:T(8,128)S(1)} fusion(bf16[128,4096]{1,0:T(8,128)(2,1)S(1)} %slice_dynamic-update-slice_fusion.7, bf16[128,4096]{1,0:T(8,128)(2,1)} %collective-permute-done.10), kind=kOutput, calls=%fused_computation.107 | convolution fusion | flops 134217728 | bytes 2162688 | tf_op jit(solution)/shard_map/dot_general | solution.py:12
  96.3 1.7 %fusion.32 = f32[128,128]{1,0:T(8,128)S(1)} fusion(bf16[128,4096]{1,0:T(8,128)(2,1)S(1)} %slice_dynamic-update-slice_fusion.7, bf16[128,4096]{1,0:T(8,128)(2,1)} %collective-permute-done.9), kind=kOutput, calls=%fused_computation.106 | convolution fusion | flops 134217728 | bytes 2162688 | tf_op jit(solution)/shard_map/dot_general | solution.py:12
  98.0 1.6 %collective-permute-start.11 = (f32[4,128,16]{1,2,0:T(8,128)S(1)}, f32[4,128,16]{1,2,0:T(8,128)S(1)}, u32[]{:S(2)}, u32[]{:S(2)}) collective-permute-start(f32[4,128,16]{1,2,0:T(8,128)S(1)} %pad_maximum_fusion.7), channel_id=1, source_target_pairs={{0,1},{1,0},{2,3},{3,2},{4,5},{5,4},{6,7},{7,6},{8,9},{9,8},{10,11... | collective-permute-start | bytes 98312 | tf_op jit(solution)/shard_map/ppermute | solution.py:23
  99.5 1.1 slice_dynamic-update-slice_fusion
  100.6 1.3 %fusion.31 = f32[512,256]{1,0:T(8,128)S(1)} fusion(bf16[512,4096]{1,0:T(8,128)(2,1)S(1)} %slice_dynamic-update-slice_fusion, bf16[256,4096]{1,0:T(8,128)(2,1)S(1)} %copy-done.2), kind=kOutput, calls=%fused_computation.105 | convolution fusion | flops 1073741824 | bytes 6815744 | tf_op jit(solution)/shard_map/dot_general | solution.py:12
  101.9 2.5 %fusion.35 = f32[512,128]{1,0:T(8,128)S(1)} fusion(bf16[512,4096]{1,0:T(8,128)(2,1)S(1)} %slice_dynamic-update-slice_fusion, bf16[128,4096]{1,0:T(8,128)(2,1)} %collective-permute-done.10), kind=kOutput, calls=%fused_computation.109 | convolution fusion | flops 536870912 | bytes 5505024 | tf_op jit(solution)/shard_map/dot_general | solution.py:12
  104.4 2.5 %fusion.34 = f32[512,128]{1,0:T(8,128)S(1)} fusion(bf16[512,4096]{1,0:T(8,128)(2,1)S(1)} %slice_dynamic-update-slice_fusion, bf16[128,4096]{1,0:T(8,128)(2,1)} %collective-permute-done.9), kind=kOutput, calls=%fused_computation.108 | convolution fusion | flops 536870912 | bytes 5505024 | tf_op jit(solution)/shard_map/dot_general | solution.py:12
  107.8 1.6 %collective-permute-start.17 = (f32[128,256]{1,0:T(8,128)S(1)}, f32[128,256]{1,0:T(8,128)S(1)}, u32[]{:S(2)}, u32[]{:S(2)}) collective-permute-start(f32[128,256]{1,0:T(8,128)S(1)} %bitcast.153), channel_id=1, source_target_pairs={{0,1},{1,0},{2,3},{3,2},{4,5},{5,4},{6,7},{7,6},{8,9},{9,8},{10,11... | collective-permute-start | bytes 393224 | tf_op jit(solution)/shard_map/ppermute | solution.py:23
  109.3 1.6 %collective-permute-start.12 = (bf16[4,128,16]{1,2,0:T(8,128)(2,1)S(1)}, bf16[4,128,16]{1,2,0:T(8,128)(2,1)S(1)}, u32[]{:S(2)}, u32[]{:S(2)}) collective-permute-start(bf16[4,128,16]{1,2,0:T(8,128)(2,1)S(1)} %add_convert_fusion), channel_id=1, source_target_pairs={{0,4},{2,6},{4,0},{6,2},{8,12},{10,14},{12,8},{14,10},{16,20},{18,... | collective-permute-start | bytes 49160 | tf_op jit(solution)/shard_map/ppermute | solution.py:20
  112.0 1.1 collective-permute-done.12
  114.3 1.6 %collective-permute-start.20 = (bf16[128,256]{1,0:T(8,128)(2,1)S(1)}, bf16[128,256]{1,0:T(8,128)(2,1)S(1)}, u32[]{:S(2)}, u32[]{:S(2)}) collective-permute-start(bf16[128,256]{1,0:T(8,128)(2,1)S(1)} %fusion.2), channel_id=1, source_target_pairs={{0,4},{2,6},{4,0},{6,2},{8,12},{10,14},{12,8},{14,10},{16,20},{18,... | collective-permute-start | bytes 196616 | tf_op jit(solution)/shard_map/ppermute | solution.py:20
  117.2 1.6 %collective-permute-start.18 = (bf16[128,256]{1,0:T(8,128)(2,1)S(1)}, bf16[128,256]{1,0:T(8,128)(2,1)S(1)}, u32[]{:S(2)}, u32[]{:S(2)}) collective-permute-start(bf16[128,256]{1,0:T(8,128)(2,1)S(1)} %fusion.4), channel_id=1, source_target_pairs={{0,4},{2,6},{4,0},{6,2},{8,12},{10,14},{12,8},{14,10},{16,20},{18,... | collective-permute-start | bytes 196616 | tf_op jit(solution)/shard_map/ppermute | solution.py:20
  119.0 2.5 %collective-permute-done.18 = bf16[128,256]{1,0:T(8,128)(2,1)S(1)} collective-permute-done((bf16[128,256]{1,0:T(8,128)(2,1)S(1)}, bf16[128,256]{1,0:T(8,128)(2,1)S(1)}, u32[]{:S(2)}, u32[]{:S(2)}) %collective-permute-start.18) | collective-permute-done | bytes 65568 | tf_op jit(solution)/shard_map/ppermute | solution.py:20
  (118 shorter events, 22.3 us)
Async XLA Ops:
  0.0 13.7 %copy-start = (bf16[1,16,1024]{2,1,0:T(8,128)(2,1)S(1)}, bf16[1,16,1024]{2,1,0:T(8,128)(2,1)}, u32[]{:S(2)}) copy-start(bf16[1,16,1024]{2,1,0:T(8,128)(2,1)} %param.9) | copy-start | bytes 98308
  0.0 13.8 %copy-start.5 = (bf16[1,4096,16]{1,2,0:T(8,128)(2,1)S(1)}, bf16[1,4096,16]{1,2,0:T(8,128)(2,1)}, u32[]{:S(2)}) copy-start(bf16[1,4096,16]{1,2,0:T(8,128)(2,1)} %param.8) | copy-start | bytes 393220
  0.0 12.9 %copy-start.3 = (bf16[4096,64]{0,1:T(8,128)(2,1)S(1)}, bf16[4096,64]{0,1:T(8,128)(2,1)}, u32[]{:S(2)}) copy-start(bf16[4096,64]{0,1:T(8,128)(2,1)} %param.7) | copy-start | bytes 1572868
  0.0 12.3 %copy-start.6 = (s32[2]{0:T(128)S(1)}, s32[2]{0:T(128)}, u32[]{:S(2)}) copy-start(s32[2]{0:T(128)} %param.11) | copy-start | bytes 28
  0.0 12.3 %copy-start.7 = (s32[2]{0:T(128)S(1)}, s32[2]{0:T(128)}, u32[]{:S(2)}) copy-start(s32[2]{0:T(128)} %param.10) | copy-start | bytes 28
  2.1 67.6 %collective-permute-start = (bf16[80,4096]{1,0:T(8,128)(2,1)}, bf16[80,4096]{1,0:T(8,128)(2,1)}, u32[]{:S(2)}, u32[]{:S(2)}) collective-permute-start(bf16[80,4096]{1,0:T(8,128)(2,1)} %pad_maximum_fusion), channel_id=1, source_target_pairs={{0,2},{2,0},{4,6},{6,4},{8,10},{10,8},{12,14},{14,12},{16,18},{18,... | collective-permute-start | bytes 1966088 | tf_op jit(solution)/shard_map/ppermute | solution.py:20
  2.5 67.2 %collective-permute-start.1 = (bf16[80,4096]{1,0:T(8,128)(2,1)}, bf16[80,4096]{1,0:T(8,128)(2,1)}, u32[]{:S(2)}, u32[]{:S(2)}) collective-permute-start(bf16[80,4096]{1,0:T(8,128)(2,1)} %pad_maximum_fusion), channel_id=1, source_target_pairs={{0,8},{2,10},{4,12},{6,14},{8,0},{10,2},{12,4},{14,6},{16,24},{18,... | collective-permute-start | bytes 1966088 | tf_op jit(solution)/shard_map/ppermute | solution.py:20
  5.1 64.6 %collective-permute-start.3 = (bf16[80,4096]{1,0:T(8,128)(2,1)}, bf16[80,4096]{1,0:T(8,128)(2,1)}, u32[]{:S(2)}, u32[]{:S(2)}) collective-permute-start(bf16[80,4096]{1,0:T(8,128)(2,1)} %pad_maximum_fusion), channel_id=1, source_target_pairs={{0,16},{2,18},{4,20},{6,22},{8,24},{10,26},{12,28},{14,30},{16,0},... | collective-permute-start | bytes 1966088 | tf_op jit(solution)/shard_map/ppermute | solution.py:20
  10.8 83.6 %collective-permute-start.10 = (bf16[128,4096]{1,0:T(8,128)(2,1)}, bf16[128,4096]{1,0:T(8,128)(2,1)}, u32[]{:S(2)}, u32[]{:S(2)}) collective-permute-start(bf16[128,4096]{1,0:T(8,128)(2,1)} %get-tuple-element.8), channel_id=1, source_target_pairs={{0,4},{2,6},{4,0},{6,2},{8,12},{10,14},{12,8},{14,10},{16,20},{18,... | collective-permute-start | bytes 3145736 | tf_op jit(solution)/shard_map/ppermute | solution.py:20
  12.3 23.8 %collective-permute-start.8 = (s32[2,2]{1,0:T(2,128)S(1)}, s32[2,2]{1,0:T(2,128)S(1)}, u32[]{:S(2)}, u32[]{:S(2)}) collective-permute-start(s32[2,2]{1,0:T(2,128)S(1)} %pad_add_fusion), channel_id=1, source_target_pairs={{0,4},{2,6},{4,0},{6,2},{8,12},{10,14},{12,8},{14,10},{16,20},{18,... | collective-permute-start | bytes 56 | tf_op jit(solution)/shard_map/ppermute | solution.py:20
  36.1 6.1 %collective-permute-start.13 = (bf16[1,1,16,512]{3,2,0,1:T(8,128)(2,1)S(1)}, bf16[1,1,16,512]{3,2,0,1:T(8,128)(2,1)S(1)}, u32[]{:S(2)}, u32[]{:S(2)}) collective-permute-start(bf16[1,1,16,512]{3,2,0,1:T(8,128)(2,1)S(1)} %fusion.49), channel_id=1, source_target_pairs={{0,2},{2,0},{4,6},{6,4},{8,10},{10,8},{12,14},{14,12},{16,18},{18,... | collective-permute-start | bytes 49160 | tf_op jit(solution)/shard_map/ppermute | solution.py:20
  42.2 9.9 %collective-permute-start.14 = (bf16[2,1,16,512]{3,2,0,1:T(8,128)(2,1)S(1)}, bf16[2,1,16,512]{3,2,0,1:T(8,128)(2,1)S(1)}, u32[]{:S(2)}, u32[]{:S(2)}) collective-permute-start(bf16[2,1,16,512]{3,2,0,1:T(8,128)(2,1)S(1)} %pad_maximum_fusion.8), channel_id=1, source_target_pairs={{0,4},{2,6},{4,0},{6,2},{8,12},{10,14},{12,8},{14,10},{16,20},{18,... | collective-permute-start | bytes 98312 | tf_op jit(solution)/shard_map/ppermute | solution.py:20
  52.1 4.3 %collective-permute-start.15 = (bf16[4,1,16,512]{3,2,0,1:T(8,128)(2,1)S(1)}, bf16[4,1,16,512]{3,2,0,1:T(8,128)(2,1)S(1)}, u32[]{:S(2)}, u32[]{:S(2)}) collective-permute-start(bf16[4,1,16,512]{3,2,0,1:T(8,128)(2,1)S(1)} %pad_maximum_fusion.6), channel_id=1, source_target_pairs={{0,8},{2,10},{4,12},{6,14},{8,0},{10,2},{12,4},{14,6},{16,24},{18,... | collective-permute-start | bytes 196616 | tf_op jit(solution)/shard_map/ppermute | solution.py:20
  56.5 8.1 %collective-permute-start.16 = (bf16[8,1,16,512]{3,2,0,1:T(8,128)(2,1)S(1)}, bf16[8,1,16,512]{3,2,0,1:T(8,128)(2,1)S(1)}, u32[]{:S(2)}, u32[]{:S(2)}) collective-permute-start(bf16[8,1,16,512]{3,2,0,1:T(8,128)(2,1)S(1)} %pad_maximum_fusion.4), channel_id=1, source_target_pairs={{0,16},{2,18},{4,20},{6,22},{8,24},{10,26},{12,28},{14,30},{16,0},... | collective-permute-start | bytes 393224 | tf_op jit(solution)/shard_map/ppermute | solution.py:20
  64.6 31.6 %collective-permute-start.9 = (bf16[128,4096]{1,0:T(8,128)(2,1)}, bf16[128,4096]{1,0:T(8,128)(2,1)}, u32[]{:S(2)}, u32[]{:S(2)}) collective-permute-start(bf16[128,4096]{1,0:T(8,128)(2,1)} %get-tuple-element.7), channel_id=1, source_target_pairs={{0,4},{2,6},{4,0},{6,2},{8,12},{10,14},{12,8},{14,10},{16,20},{18,... | collective-permute-start | bytes 3145736 | tf_op jit(solution)/shard_map/ppermute | solution.py:20
  68.1 25.3 %copy-start.2 = (bf16[256,4096]{1,0:T(8,128)(2,1)S(1)}, bf16[256,4096]{1,0:T(8,128)(2,1)}, u32[]{:S(2)}) copy-start(bf16[256,4096]{1,0:T(8,128)(2,1)} %param.6) | copy-start | bytes 6291460
  69.7 20.1 %collective-permute-start.4 = (bf16[80,4096]{1,0:T(8,128)(2,1)}, bf16[80,4096]{1,0:T(8,128)(2,1)S(1)}, u32[]{:S(2)}, u32[]{:S(2)}) collective-permute-start(bf16[80,4096]{1,0:T(8,128)(2,1)} %collective-permute-done.3), channel_id=1, source_target_pairs={{0,2},{2,0},{4,6},{6,4},{8,10},{10,8},{12,14},{14,12},{16,18},{18,... | collective-permute-start | bytes 1966088 | tf_op jit(solution)/shard_map/ppermute | solution.py:20
  69.7 17.4 %collective-permute-start.5 = (bf16[80,4096]{1,0:T(8,128)(2,1)}, bf16[80,4096]{1,0:T(8,128)(2,1)S(1)}, u32[]{:S(2)}, u32[]{:S(2)}) collective-permute-start(bf16[80,4096]{1,0:T(8,128)(2,1)} %collective-permute-done.3), channel_id=1, source_target_pairs={{0,8},{2,10},{4,12},{6,14},{8,0},{10,2},{12,4},{14,6},{16,24},{18,... | collective-permute-start | bytes 1966088 | tf_op jit(solution)/shard_map/ppermute | solution.py:20
  69.8 17.3 %collective-permute-start.2 = (bf16[80,4096]{1,0:T(8,128)(2,1)}, bf16[80,4096]{1,0:T(8,128)(2,1)S(1)}, u32[]{:S(2)}, u32[]{:S(2)}) collective-permute-start(bf16[80,4096]{1,0:T(8,128)(2,1)} %collective-permute-done.1), channel_id=1, source_target_pairs={{0,2},{2,0},{4,6},{6,4},{8,10},{10,8},{12,14},{14,12},{16,18},{18,... | collective-permute-start | bytes 1966088 | tf_op jit(solution)/shard_map/ppermute | solution.py:20
  87.1 5.4 %collective-permute-start.6 = (bf16[80,4096]{1,0:T(8,128)(2,1)S(1)}, bf16[80,4096]{1,0:T(8,128)(2,1)S(1)}, u32[]{:S(2)}, u32[]{:S(2)}) collective-permute-start(bf16[80,4096]{1,0:T(8,128)(2,1)S(1)} %collective-permute-done.5), channel_id=1, source_target_pairs={{0,2},{2,0},{4,6},{6,4},{8,10},{10,8},{12,14},{14,12},{16,18},{18,... | collective-permute-start | bytes 1966088 | tf_op jit(solution)/shard_map/ppermute | solution.py:20
  92.5 0.9 copy-start.4
  94.3 5.2 %copy-start.1 = (bf16[512,4096]{1,0:T(8,128)(2,1)S(1)}, bf16[512,4096]{1,0:T(8,128)(2,1)}, u32[]{:S(2)}) copy-start(bf16[512,4096]{1,0:T(8,128)(2,1)} %slice_dynamic-update-slice_fusion.1) | copy-start | bytes 12582916
  98.0 11.3 %collective-permute-start.11 = (f32[4,128,16]{1,2,0:T(8,128)S(1)}, f32[4,128,16]{1,2,0:T(8,128)S(1)}, u32[]{:S(2)}, u32[]{:S(2)}) collective-permute-start(f32[4,128,16]{1,2,0:T(8,128)S(1)} %pad_maximum_fusion.7), channel_id=1, source_target_pairs={{0,1},{1,0},{2,3},{3,2},{4,5},{5,4},{6,7},{7,6},{8,9},{9,8},{10,11... | collective-permute-start | bytes 98312 | tf_op jit(solution)/shard_map/ppermute | solution.py:23
  107.1 6.4 %collective-permute-start.19 = (f32[128,256]{1,0:T(8,128)S(1)}, f32[128,256]{1,0:T(8,128)S(1)}, u32[]{:S(2)}, u32[]{:S(2)}) collective-permute-start(f32[128,256]{1,0:T(8,128)S(1)} %bitcast.154), channel_id=1, source_target_pairs={{0,1},{1,0},{2,3},{3,2},{4,5},{5,4},{6,7},{7,6},{8,9},{9,8},{10,11... | collective-permute-start | bytes 393224 | tf_op jit(solution)/shard_map/ppermute | solution.py:23
  107.8 8.5 %collective-permute-start.17 = (f32[128,256]{1,0:T(8,128)S(1)}, f32[128,256]{1,0:T(8,128)S(1)}, u32[]{:S(2)}, u32[]{:S(2)}) collective-permute-start(f32[128,256]{1,0:T(8,128)S(1)} %bitcast.153), channel_id=1, source_target_pairs={{0,1},{1,0},{2,3},{3,2},{4,5},{5,4},{6,7},{7,6},{8,9},{9,8},{10,11... | collective-permute-start | bytes 393224 | tf_op jit(solution)/shard_map/ppermute | solution.py:23
  109.3 3.8 %collective-permute-start.12 = (bf16[4,128,16]{1,2,0:T(8,128)(2,1)S(1)}, bf16[4,128,16]{1,2,0:T(8,128)(2,1)S(1)}, u32[]{:S(2)}, u32[]{:S(2)}) collective-permute-start(bf16[4,128,16]{1,2,0:T(8,128)(2,1)S(1)} %add_convert_fusion), channel_id=1, source_target_pairs={{0,4},{2,6},{4,0},{6,2},{8,12},{10,14},{12,8},{14,10},{16,20},{18,... | collective-permute-start | bytes 49160 | tf_op jit(solution)/shard_map/ppermute | solution.py:20
  111.3 10.3 %collective-permute-start.7 = (f32[256,256]{1,0:T(8,128)S(1)}, f32[256,256]{1,0:T(8,128)S(1)}, u32[]{:S(2)}, u32[]{:S(2)}) collective-permute-start(f32[256,256]{1,0:T(8,128)S(1)} %bitcast.152), channel_id=1, source_target_pairs={{0,1},{1,0},{2,3},{3,2},{4,5},{5,4},{6,7},{7,6},{8,9},{9,8},{10,11... | collective-permute-start | bytes 786440 | tf_op jit(solution)/shard_map/ppermute | solution.py:23
  114.3 4.6 %collective-permute-start.20 = (bf16[128,256]{1,0:T(8,128)(2,1)S(1)}, bf16[128,256]{1,0:T(8,128)(2,1)S(1)}, u32[]{:S(2)}, u32[]{:S(2)}) collective-permute-start(bf16[128,256]{1,0:T(8,128)(2,1)S(1)} %fusion.2), channel_id=1, source_target_pairs={{0,4},{2,6},{4,0},{6,2},{8,12},{10,14},{12,8},{14,10},{16,20},{18,... | collective-permute-start | bytes 196616 | tf_op jit(solution)/shard_map/ppermute | solution.py:20
  117.2 4.3 %collective-permute-start.18 = (bf16[128,256]{1,0:T(8,128)(2,1)S(1)}, bf16[128,256]{1,0:T(8,128)(2,1)S(1)}, u32[]{:S(2)}, u32[]{:S(2)}) collective-permute-start(bf16[128,256]{1,0:T(8,128)(2,1)S(1)} %fusion.4), channel_id=1, source_target_pairs={{0,4},{2,6},{4,0},{6,2},{8,12},{10,14},{12,8},{14,10},{16,20},{18,... | collective-permute-start | bytes 196616 | tf_op jit(solution)/shard_map/ppermute | solution.py:20

commit v2 on v1

v2 whole, which is shorter than its diff:
```python
import functools

import jax
import jax.numpy as jnp
from jax import lax
from jax.experimental import pallas as pl
from jax.experimental.pallas import tpu as pltpu
from jax.sharding import PartitionSpec as P

BLK = 128
LANES = 128
F32 = jnp.float32
BF16 = jnp.bfloat16
MIB = 1 << 20


def dot_nt(a, b):
    return lax.dot_general(a, b, (((1,), (1,)), ((), ())), preferred_element_type=F32)


def swaps(tensor, adapters):
    def over_tensor(array, flip):
        return lax.ppermute(array, "tensor", perm=[(i, i ^ flip) for i in range(tensor)])

    def over_adapter(array, flip):
        return lax.ppermute(array, "adapter", perm=[(i, i ^ flip) for i in range(adapters)])

    return over_tensor, over_adapter


def make_general_body(tensor, adapters):
    depth = tensor // 4
    low = depth // adapters
    over_tensor, over_adapter = swaps(tensor, adapters)

    def body(hidden, value, down, up, chosen, live):
        t, x = lax.axis_index("tensor"), lax.axis_index("adapter")
        z, y, core = t // 4, (t // 2) % 2, t % 2
        rows, features = hidden.shape
        width = value.shape[1]
        homes, rank, wide = up.shape
        blocks = rows // BLK

        theirs = over_tensor(hidden, 2)
        packet = jnp.concatenate([value.T, down.transpose(0, 2, 1).reshape(homes * rank, features)])
        units = {0: packet}
        bit = depth // 2
        while bit:
            units.update({a ^ bit: over_tensor(u, 4 * bit) for a, u in units.items()})
            bit //= 2
        pairs = {a: (u, over_tensor(u, 1)) for a, u in units.items()}

        ids = jnp.stack([chosen, live])
        ids = jnp.concatenate([ids, over_tensor(ids, 2)], axis=1)
        ups = lax.dynamic_slice_in_dim(up, x * (wide // adapters), wide // adapters, 2)[None]
        bit = 1
        while bit < tensor:
            ups = jnp.concatenate([ups, over_tensor(ups, bit)])
            bit *= 2

        w_all = jnp.concatenate([u[:width] for a in range(depth) for u in pairs[a]])
        d_all = jnp.concatenate([u[width:] for a in range(depth) for u in pairs[a]])

        relative = (ids[0] // homes) ^ t
        here = (relative & 2) == 0
        slot = (relative // 4) * 2 + relative % 2
        which = slot * homes + ids[0] % homes

        ups = ups.reshape(tensor, homes, rank, low, 2, 2, width)
        ups = lax.dynamic_index_in_dim(ups, y, 4, keepdims=False)
        z_low = z % low
        order = [lax.dynamic_index_in_dim(ups, z_low ^ a, 3, keepdims=False) for a in range(low)]
        ups = jnp.stack(order, axis=3)
        ups = jnp.where(core == 1, ups[..., ::-1, :], ups)
        ups = ups.reshape(tensor * homes, rank, low * 2 * width)
        up_index = relative * homes + ids[0] % homes

        part = (z // low) ^ x

        def work(x_rows, b0):
            count = x_rows.shape[0] // BLK
            base = dot_nt(x_rows, w_all).reshape(-1, adapters, low * 2 * width)
            kept = lax.dynamic_index_in_dim(base, part, 1, keepdims=False)
            for k in range(1, adapters):
                sent = lax.dynamic_index_in_dim(base, part ^ k, 1, keepdims=False)
                kept = kept + over_adapter(sent, k)
            shrink = dot_nt(x_rows, d_all).reshape(count, BLK, -1, rank)
            spots = jnp.arange(shrink.shape[2], dtype=jnp.int32)
            hot = (which[b0 : b0 + count, None] == spots) & here[b0 : b0 + count, None]
            alive = jnp.arange(BLK, dtype=jnp.int32) < ids[1, b0 : b0 + count, None]
            mask = hot[:, None, :, None] & alive[:, :, None, None]
            return kept, jnp.where(mask, shrink, 0.0).sum(axis=2)

        def finish(kept, shrink, b0):
            mid = shrink.astype(BF16)
            picked = [
                lax.dynamic_index_in_dim(ups, up_index[b], 0, keepdims=False)
                for b in range(b0, b0 + shrink.shape[0])
            ]
            extra = jnp.einsum("bir,brv->biv", mid, jnp.stack(picked), preferred_element_type=F32)
            return (kept + extra.reshape(kept.shape)).astype(BF16)

        kept_own, m_own = work(hidden, 0)
        kept_their, m_their = work(theirs, blocks)
        m = jnp.concatenate([m_own, m_their])
        total = m
        for k in range(1, adapters):
            total = total + over_adapter(m, k)
        m = total.astype(BF16)
        swapped = over_tensor(m, 2)
        m = m + jnp.concatenate([swapped[blocks:], swapped[:blocks]])
        out_their = over_tensor(finish(kept_their, m[blocks:], blocks), 2)
        out_own = finish(kept_own, m[:blocks], 0)
        pair = jnp.stack([out_own, out_their], axis=1)
        pair = pair.reshape(rows, 2, low, 2, width)
        pair = jnp.where(y == 1, pair[:, ::-1], pair)
        pair = jnp.where(core == 1, pair[:, :, :, ::-1], pair)
        pair = jnp.stack(
            [lax.dynamic_index_in_dim(pair, z_low ^ a, 2, keepdims=False) for a in range(low)],
            axis=1,
        )
        return pair.reshape(rows, wide // adapters)

    return body


RANK = 16
WIDTH = 64
DEPTH = 4
TILE = 2 * WIDTH
HALF = 2 * TILE
UP_TILES = 4


def place():
    t = lax.axis_index("tensor")
    z, y, core = t // 4, (t // 2) % 2, t % 2
    part = (z // 2) ^ lax.axis_index("adapter")
    return t, z % 2, y, core, part


def prep_kernel(chosen, live, value, down, up, packet, ids):
    x = lax.axis_index("adapter")
    features = value.shape[1]
    packet[:WIDTH, :features] = value[...]
    packet[pl.ds(WIDTH, RANK), :features] = down[...]
    packet[pl.ds(WIDTH, RANK), pl.ds(features, LANES)] = jnp.zeros((RANK, LANES), BF16)
    for j in range(UP_TILES):
        start = pl.multiple_of((x * UP_TILES + j) * LANES, LANES)
        packet[pl.ds(j * RANK, RANK), pl.ds(features, LANES)] = up[:, pl.ds(start, LANES)]
    lane = lax.broadcasted_iota(jnp.int32, ids.shape, 1)
    line = jnp.zeros(ids.shape, jnp.int32)
    for b in range(2):
        line = jnp.where(lane == b, chosen[b], line)
        line = jnp.where(lane == 2 + b, live[b], line)
    ids[...] = line


def prep(chosen, live, value, down, up):
    features = value.shape[1]
    vmem, smem = pl.BlockSpec(memory_space=pltpu.VMEM), pl.BlockSpec(memory_space=pltpu.SMEM)
    return pl.pallas_call(
        prep_kernel,
        out_shape=[
            jax.ShapeDtypeStruct((WIDTH + RANK, features + LANES), BF16),
            jax.ShapeDtypeStruct((8, LANES), jnp.int32),
        ],
        in_specs=[smem] * 2 + [vmem] * 3,
        out_specs=[vmem] * 2,
    )(chosen, live, value, down, up)


def compute_kernel(chosen, live, ids_p, mine, theirs, *refs):
    units, (kept, to_x, to_y, to_xy, up_own, w, d) = refs[: 2 * DEPTH], refs[2 * DEPTH :]
    t, _, _, core, part = place()
    rows, features = mine.shape
    for a in range(DEPTH):
        base = ((a // 2) ^ part) * HALF + (a % 2) * TILE
        for k in range(2):
            start = pl.multiple_of(base + (core ^ k) * WIDTH, WIDTH)
            w[pl.ds(start, WIDTH), :] = units[2 * a + k][:WIDTH, :features]
    up_own[...] = jnp.zeros_like(up_own)
    to_y[pl.ds(rows + RANK, WIDTH), :] = jnp.zeros((WIDTH, HALF), F32)
    for b in range(4):
        relative = (chosen[b] if b < 2 else ids_p[0, b - 2]) ^ t
        spot = (relative // 4) * 2 + relative % 2
        here = ((relative // 2) % 2) == 0
        lanes = pl.ds(b % 2 * LANES, LANES)
        d[b] = jnp.zeros_like(d[b])
        for u in range(2 * DEPTH):

            @pl.when(here & (spot == u))
            def _():
                d[b] = units[u][pl.ds(WIDTH, RANK), :features]
                up = units[u][:WIDTH, pl.ds(features, LANES)].astype(F32)
                if b < 2:
                    up_own[:, lanes] = up
                else:
                    to_y[pl.ds(rows + RANK, WIDTH), lanes] = up

    w_kept, w_sent = w[pl.ds(0, HALF), :], w[pl.ds(HALF, HALF), :]
    kept[:rows, :] = dot_nt(mine[...], w_kept)
    to_x[:rows, :] = dot_nt(mine[...], w_sent)
    to_y[:rows, :] = dot_nt(theirs[...], w_kept)
    to_xy[:rows, :] = dot_nt(theirs[...], w_sent)
    line = pl.ds(rows, RANK)
    for b in range(4):
        at = pl.ds(b % 2 * BLK, BLK)
        m = dot_nt(d[b], (mine if b < 2 else theirs)[at, :])
        limit = live[b] if b < 2 else ids_p[0, b]
        m = jnp.where(lax.broadcasted_iota(jnp.int32, m.shape, 1) < limit, m, 0.0)
        if b < 2:
            kept[line, at] = m
            to_x[line, at] = m
        else:
            to_y[line, at] = m
            to_xy[line, at] = m


def compute(scalars, rows, units):
    count, features = rows[0].shape
    vmem, smem = pl.BlockSpec(memory_space=pltpu.VMEM), pl.BlockSpec(memory_space=pltpu.SMEM)
    short = jax.ShapeDtypeStruct((count + RANK, HALF), F32)
    long = jax.ShapeDtypeStruct((count + RANK + WIDTH, HALF), F32)
    return pl.pallas_call(
        compute_kernel,
        out_shape=[short, short, long, short, jax.ShapeDtypeStruct((WIDTH, HALF), F32)],
        in_specs=[smem] * 3 + [vmem] * (2 + len(units)),
        out_specs=[vmem] * 5,
        scratch_shapes=[
            pltpu.VMEM((2 * HALF, features), BF16),
            pltpu.VMEM((4, RANK, features), BF16),
        ],
        compiler_params=pltpu.CompilerParams(vmem_limit_bytes=48 * MIB),
        cost_estimate=pl.CostEstimate(
            flops=4 * count * features * 2 * HALF, bytes_accessed=10 * MIB, transcendentals=0
        ),
    )(*scalars, *rows, *units)


def final_kernel(kept, up_own, from_x, from_y, from_xy, out):
    _, z_low, y, _, _ = place()
    rows = out.shape[0]
    line = pl.ds(rows, RANK)
    m = (kept[line, :] + from_x[line, :]) + (from_y[line, :] + from_xy[line, :])
    mid = m.T.astype(BF16)
    up = (up_own[...] + from_y[pl.ds(rows + RANK, WIDTH), :]).astype(BF16)
    for tile in range(2):
        cols = pl.ds(tile * LANES, LANES)
        for side in range(2):
            j = 2 * (z_low ^ tile) + (y ^ side)
            lanes = pl.ds(pl.multiple_of(j * LANES, LANES), LANES)
            for b in range(2):
                span = pl.ds(b * BLK, BLK)
                if side == 0:
                    base = kept[span, cols] + from_x[span, cols]
                else:
                    base = from_y[span, cols] + from_xy[span, cols]
                picked = jnp.zeros((RANK, LANES), BF16)
                for i in range(UP_TILES):
                    piece = up[i * RANK : (i + 1) * RANK, b * LANES : (b + 1) * LANES]
                    picked = jnp.where(j == i, piece, picked)
                extra = jnp.dot(
                    mid[b * BLK : (b + 1) * BLK], picked, preferred_element_type=F32
                )
                out[span, lanes] = (base + extra).astype(BF16)


def final(rows, *args):
    vmem = pl.BlockSpec(memory_space=pltpu.VMEM)
    return pl.pallas_call(
        final_kernel,
        out_shape=jax.ShapeDtypeStruct((rows, 2 * HALF), BF16),
        in_specs=[vmem] * len(args),
        out_specs=vmem,
    )(*args)


def make_body(tensor, adapters):
    over_tensor, over_adapter = swaps(tensor, adapters)
    tie = lax.optimization_barrier

    def over_both(array):
        pairs = [
            (i * adapters + j, (i ^ 2) * adapters + (j ^ 1))
            for i in range(tensor)
            for j in range(adapters)
        ]
        return lax.ppermute(array, ("tensor", "adapter"), perm=pairs)

    def body(hidden, value, down, up, chosen, live):
        rows, features = hidden.shape
        theirs = over_tensor(hidden, 2)
        packet, ids = prep(
            chosen, live, value.T, down.transpose(0, 2, 1).reshape(RANK, features), up[0]
        )
        ids_p = over_tensor(ids, 2)
        u2 = over_tensor(packet, 8)
        u1 = over_tensor(packet, 4)
        v0 = over_tensor(packet, 1)
        u2, u1, v0 = tie((u2, u1, v0))
        u3 = over_tensor(u2, 4)
        v2, v1 = over_tensor(u2, 1), over_tensor(u1, 1)
        v3 = over_tensor(u3, 1)
        units = (packet, v0, u1, v1, u2, v2, u3, v3)
        kept, to_x, to_y, to_xy, up_own = compute((chosen, live, ids_p), (hidden, theirs), units)
        from_xy = over_both(to_xy)
        from_x = over_adapter(to_x, 1)
        from_y = over_tensor(to_y, 2)
        return final(rows, kept, up_own, from_x, from_y, from_xy)

    return body


def solution(mesh):
    in_specs = (
        P(("groups", "tensor"), "adapter"),
        P("adapter", "tensor"),
        P("tensor", "adapter", None),
        P("tensor", None, None),
        P(("groups", "tensor")),
        P(("groups", "tensor")),
    )
    out_specs = P(("groups", "tensor"), "adapter")
    tensor, adapters = mesh.shape["tensor"], mesh.shape["adapter"]

    def run(hidden, value, down, up, chosen, live):
        blocks = chosen.shape[0] // (mesh.shape["groups"] * tensor)
        fits = (tensor, adapters, blocks) == (4 * DEPTH, 2, 2)
        fits = fits and up.shape == (tensor, RANK, tensor * WIDTH)
        make = make_body if fits else make_general_body
        body = make(tensor, adapters)
        mapped = jax.shard_map(
            body, mesh=mesh, in_specs=in_specs, out_specs=out_specs, check_vma=False
        )
        return mapped(hidden, value, down, up, chosen, live)

    return run
```

time: 124 us -> 89.6 us (0.72)
  local copies, waits for them, and re-layouts: 25.5 us -> 6.64 us
  matrix products: 12.6 us -> 0 us
  waiting for transfers between devices: 48.7 us -> 60 us
  Pallas kernels: 0 us -> 10.6 us
  starting transfers between devices: 20.3 us -> 12.1 us
  between operations: 8.11 us -> 0.04 us
  other arithmetic: 7.63 us -> 0 us
    dot_general x9 -> x0, matrix products: 12.6 us -> none  [the longest x6 10.6 us: dot_nt(): lax.dot_general(a, b, (((1,), (1,)), ((), ())), preferred_element_type=F32)]
    pallas_call x0 -> x3, Pallas kernels: none -> 10.6 us  [the longest x1 6.32 us: compute(): pl.pallas_call(compute_kernel, out_shape=[short, short, long, short, jax....]
    ppermute x17 -> x10, starting transfers between devices: 16 us -> 9.08 us  [over_tensor(): lax.ppermute(array, 'tensor', perm=[(i, i ^ flip) for i in range(tensor)])]
    unnamed x38 -> x20, local copies, waits for them, and re-layouts: 13.4 us -> 6.64 us
    ppermute x4 -> x1, waiting for transfers between devices: 0.65 us -> 6.6 us  [over_adapter(): lax.ppermute(array, 'adapter', perm=[(i, i ^ flip) for i in range(adapter...]
    slice x6 -> x0, local copies, waits for them, and re-layouts: 5.61 us -> none  [the longest x1 3.08 us: body(): theirs = [over_tensor(hidden[:first], 2), over_tensor(hidden[first:], 2)]]
    ppermute x0 -> x1, waiting for transfers between devices: none -> 5.07 us  [over_both(): return lax.ppermute(array, ('tensor', 'adapter'), perm=pairs)]
    ppermute x4 -> x1, starting transfers between devices: 4.31 us -> 1.49 us  [over_adapter(): lax.ppermute(array, 'adapter', perm=[(i, i ^ flip) for i in range(adapter...]
  transfers between devices with their start and end apart: 21 -> 12, of which waited for: 8 -> 7; matrix products, arithmetic and copies ran while one was open for 32% -> 0% of each run, Pallas kernels for 0% -> 2%
where the time goes in v2:
time: 89.6 us; the launch traced here: 89.3 us
  waiting for transfers between devices  60 us (67%)
  starting transfers between devices  12.1 us (14%)
  Pallas kernels  10.6 us (12%)
  local copies, waits for them, and re-layouts  6.64 us (7%)
    ppermute x10, waiting for transfers between devices, over_tensor(): lax.ppermute(array, 'tensor', perm=[(i, i ^ flip) for i in range(tensor)])  48.3 us
    ppermute x10, starting transfers between devices, over_tensor(): lax.ppermute(array, 'tensor', perm=[(i, i ^ flip) for i in range(tensor)])  9.08 us
    unnamed x20, local copies, waits for them, and re-layouts  6.64 us
    ppermute x1, waiting for transfers between devices, over_adapter(): lax.ppermute(array, 'adapter', perm=[(i, i ^ flip) for i in range(adapter...  6.6 us
    pallas_call x1, Pallas kernels, compute(): pl.pallas_call(compute_kernel, out_shape=[short, short, long, short, jax....  6.32 us
    ppermute x1, waiting for transfers between devices, over_both(): return lax.ppermute(array, ('tensor', 'adapter'), perm=pairs)  5.07 us
    pallas_call x1, Pallas kernels, final(): pl.pallas_call(final_kernel, out_shape=jax.ShapeDtypeStruct((rows, 2 * HA...  2.26 us
    pallas_call x1, Pallas kernels, prep(): pl.pallas_call(prep_kernel, out_shape=[jax.ShapeDtypeStruct((WIDTH + RANK...  2.03 us
  transfers between devices with their start and end apart: 12, of which 7 were waited for; matrix products, arithmetic and copies ran while one was open for 0% of the time, Pallas kernels for 2%

profile of v2, /device:TPU:0, one launch (start us, length us, event | category | flops | bytes accessed | tf_op | source)
XLA Modules:
  0.0 89.3 jit_solution(4829655239275799719)
XLA Ops:
  0.0 3.0 %collective-permute-start.1 = (bf16[256,4096]{1,0:T(8,128)(2,1)}, bf16[256,4096]{1,0:T(8,128)(2,1)S(1)}, u32[]{:S(2)}, u32[]{:S(2)}) collective-permute-start(bf16[256,4096]{1,0:T(8,128)(2,1)} %mine.1), channel_id=1, source_target_pairs={{0,4},{2,6},{4,0},{6,2},{8,12},{10,14},{12,8},{14,10},{16,20},{18,... | collective-permute-start | bytes 6291464 | tf_op jit(solution)/shard_map/ppermute | solution.py:23
  3.0 2.0 %shard_map.64 = (bf16[80,4224]{1,0:T(8,128)(2,1)}, s32[8,128]{1,0:T(8,128)}) custom-call(s32[2]{0:T(128)} %chosen.3, s32[2]{0:T(128)} %live.3, bf16[64,4096]{1,0:T(8,128)(2,1)} %bitcast.5, bf16[16,4096]{1,0:T(8,128)(2,1)} %bitcast.6, bf16[16,1024]{1,0:T(8,128)(2,1)} %bitcast.7), custom_call_target="tpu_custom_call" | custom-call | tf_op jit(solution)/shard_map/pallas_call | solution.py:162
  5.0 0.0 collective-permute-start.4
  5.0 1.6 %collective-permute-start.3 = (bf16[80,4224]{1,0:T(8,128)(2,1)}, bf16[80,4224]{1,0:T(8,128)(2,1)S(1)}, u32[]{:S(2)}, u32[]{:S(2)}) collective-permute-start(bf16[80,4224]{1,0:T(8,128)(2,1)} %get-tuple-element.16.refs_0_), channel_id=1, source_target_pairs={{0,8},{2,10},{4,12},{6,14},{8,0},{10,2},{12,4},{14,6},{16,24},{18,... | collective-permute-start | bytes 2027528 | tf_op jit(solution)/shard_map/ppermute | solution.py:23
  6.6 2.6 %collective-permute-start.2 = (bf16[80,4224]{1,0:T(8,128)(2,1)}, bf16[80,4224]{1,0:T(8,128)(2,1)S(1)}, u32[]{:S(2)}, u32[]{:S(2)}) collective-permute-start(bf16[80,4224]{1,0:T(8,128)(2,1)} %get-tuple-element.16.refs_0_), channel_id=1, source_target_pairs={{0,16},{2,18},{4,20},{6,22},{8,24},{10,26},{12,28},{14,30},{16,0},... | collective-permute-start | bytes 2027528 | tf_op jit(solution)/shard_map/ppermute | solution.py:23
  9.2 0.0 collective-permute-done.4.refs_1_
  9.2 28.0 %collective-permute-done.3.refs_2_ = bf16[80,4224]{1,0:T(8,128)(2,1)S(1)} collective-permute-done((bf16[80,4224]{1,0:T(8,128)(2,1)}, bf16[80,4224]{1,0:T(8,128)(2,1)S(1)}, u32[]{:S(2)}, u32[]{:S(2)}) %collective-permute-start.3) | collective-permute-done | bytes 675872 | tf_op jit(solution)/shard_map/ppermute | solution.py:23
  37.1 2.4 %collective-permute-done.2.refs_4_ = bf16[80,4224]{1,0:T(8,128)(2,1)S(1)} collective-permute-done((bf16[80,4224]{1,0:T(8,128)(2,1)}, bf16[80,4224]{1,0:T(8,128)(2,1)S(1)}, u32[]{:S(2)}, u32[]{:S(2)}) %collective-permute-start.2) | collective-permute-done | bytes 675872 | tf_op jit(solution)/shard_map/ppermute | solution.py:23
  39.5 0.4 collective-permute-start.7
  40.0 0.5 collective-permute-start.5
  40.5 14.5 %collective-permute-done.7.refs_6_ = bf16[80,4224]{1,0:T(8,128)(2,1)S(1)} collective-permute-done((bf16[80,4224]{1,0:T(8,128)(2,1)S(1)}, bf16[80,4224]{1,0:T(8,128)(2,1)S(1)}, u32[]{:S(2)}, u32[]{:S(2)}) %collective-permute-start.7) | collective-permute-done | bytes 675872 | tf_op jit(solution)/shard_map/ppermute | solution.py:23
  55.0 0.0 collective-permute-start.8
  55.0 0.5 collective-permute-start
  55.5 3.3 %collective-permute-done.ids_p = s32[8,128]{1,0:T(8,128)S(1)} collective-permute-done((s32[8,128]{1,0:T(8,128)}, s32[8,128]{1,0:T(8,128)S(1)}, u32[]{:S(2)}, u32[]{:S(2)}) %collective-permute-start) | collective-permute-done | bytes 4128 | tf_op jit(solution)/shard_map/ppermute | solution.py:23
  58.8 0.0 collective-permute-done.5.refs_3_
  58.8 0.8 copy-done.6
  59.7 1.3 %copy-done.5 = bf16[256,4096]{1,0:T(8,128)(2,1)} copy-done((bf16[256,4096]{1,0:T(8,128)(2,1)}, bf16[256,4096]{1,0:T(8,128)(2,1)S(1)}, u32[]{:S(2)}) %copy-start.5) | copy-done | bytes 2097176
  61.0 1.1 %copy-done = bf16[80,4224]{1,0:T(8,128)(2,1)S(1)} copy-done((bf16[80,4224]{1,0:T(8,128)(2,1)S(1)}, bf16[80,4224]{1,0:T(8,128)(2,1)}, u32[]{:S(2)}) %copy-start) | copy-done | bytes 675864
  62.1 0.7 copy-done.3
  62.7 0.7 copy-done.4
  63.4 6.3 %shard_map.65 = (f32[272,256]{1,0:T(8,128)S(1)}, f32[272,256]{1,0:T(8,128)S(1)}, f32[336,256]{1,0:T(8,128)S(1)}, f32[272,256]{1,0:T(8,128)S(1)}, f32[64,256]{1,0:T(8,128)S(1)}) custom-call(s32[2]{0:T(128)S(1)} %copy-done.3, s32[2]{0:T(128)S(1)} %copy-done.4, s32[8,128]{1,0:T(8,128)S(1)} %collective-permute-done.ids_p, bf16[256,4096]{1,0:T(8,128)(2,1)} %mine.1, ...), custom_call_target="tpu_custom_call" | custom-call | flops 2147483648 | bytes 10485760 | tf_op jit(solution)/shard_map/pallas_call | solution.py:225
  69.7 0.7 copy-done.1
  70.4 0.6 copy-done.2
  71.1 0.5 collective-permute-start.10
  71.6 1.5 %collective-permute-start.9 = (f32[272,256]{1,0:T(8,128)S(1)}, f32[272,256]{1,0:T(8,128)S(1)}, u32[]{:S(2)}, u32[]{:S(2)}) collective-permute-start(f32[272,256]{1,0:T(8,128)S(1)} %get-tuple-element.22), channel_id=1, source_target_pairs={{0,1},{1,0},{2,3},{3,2},{4,5},{5,4},{6,7},{7,6},{8,9},{9,8},{10,11... | collective-permute-start | bytes 835592 | tf_op jit(solution)/shard_map/ppermute | solution.py:26
  73.0 1.5 %collective-permute-start.11 = (f32[272,256]{1,0:T(8,128)S(1)}, f32[272,256]{1,0:T(8,128)S(1)}, u32[]{:S(2)}, u32[]{:S(2)}) collective-permute-start(f32[272,256]{1,0:T(8,128)S(1)} %get-tuple-element.24), channel_id=1, source_target_pairs={{0,5},{1,4},{2,7},{3,6},{4,1},{5,0},{6,3},{7,2},{8,13},{9,12},{10,... | collective-permute-start | bytes 835592 | tf_op jit(solution)/shard_map/ppermute | solution.py:289
  74.6 6.6 %collective-permute-done.9.from_x = f32[272,256]{1,0:T(8,128)S(1)} collective-permute-done((f32[272,256]{1,0:T(8,128)S(1)}, f32[272,256]{1,0:T(8,128)S(1)}, u32[]{:S(2)}, u32[]{:S(2)}) %collective-permute-start.9) | collective-permute-done | bytes 278560 | tf_op jit(solution)/shard_map/ppermute | solution.py:26
  81.2 5.1 %collective-permute-done.11.from_xy = f32[272,256]{1,0:T(8,128)S(1)} collective-permute-done((f32[272,256]{1,0:T(8,128)S(1)}, f32[272,256]{1,0:T(8,128)S(1)}, u32[]{:S(2)}, u32[]{:S(2)}) %collective-permute-start.11) | collective-permute-done | bytes 278560 | tf_op jit(solution)/shard_map/ppermute | solution.py:289
  86.2 0.1 collective-permute-done.10.from_y
  86.3 0.6 copy-done.9
  86.9 0.1 copy-done.7
  87.1 2.3 %shard_map.66 = bf16[256,512]{1,0:T(8,128)(2,1)} custom-call(f32[272,256]{1,0:T(8,128)} %copy-done.1, f32[64,256]{1,0:T(8,128)} %copy-done.2, f32[272,256]{1,0:T(8,128)} %copy-done.8, f32[336,256]{1,0:T(8,128)} %copy-done.7, f32[272,256]{1,0:T(8,128)} %copy-done.9), custom_call_target="tpu_custom_call" | custom-call | tf_op jit(solution)/shard_map/pallas_call | solution.py:271
  (15 shorter events, 0.0 us)
Async XLA Ops:
  0.0 58.8 %collective-permute-start.1 = (bf16[256,4096]{1,0:T(8,128)(2,1)}, bf16[256,4096]{1,0:T(8,128)(2,1)S(1)}, u32[]{:S(2)}, u32[]{:S(2)}) collective-permute-start(bf16[256,4096]{1,0:T(8,128)(2,1)} %mine.1), channel_id=1, source_target_pairs={{0,4},{2,6},{4,0},{6,2},{8,12},{10,14},{12,8},{14,10},{16,20},{18,... | collective-permute-start | bytes 6291464 | tf_op jit(solution)/shard_map/ppermute | solution.py:23
  5.0 4.2 %collective-permute-start.4 = (bf16[80,4224]{1,0:T(8,128)(2,1)}, bf16[80,4224]{1,0:T(8,128)(2,1)S(1)}, u32[]{:S(2)}, u32[]{:S(2)}) collective-permute-start(bf16[80,4224]{1,0:T(8,128)(2,1)} %get-tuple-element.16.refs_0_), channel_id=1, source_target_pairs={{0,2},{2,0},{4,6},{6,4},{8,10},{10,8},{12,14},{14,12},{16,18},{18,... | collective-permute-start | bytes 2027528 | tf_op jit(solution)/shard_map/ppermute | solution.py:23
  5.0 32.1 %collective-permute-start.3 = (bf16[80,4224]{1,0:T(8,128)(2,1)}, bf16[80,4224]{1,0:T(8,128)(2,1)S(1)}, u32[]{:S(2)}, u32[]{:S(2)}) collective-permute-start(bf16[80,4224]{1,0:T(8,128)(2,1)} %get-tuple-element.16.refs_0_), channel_id=1, source_target_pairs={{0,8},{2,10},{4,12},{6,14},{8,0},{10,2},{12,4},{14,6},{16,24},{18,... | collective-permute-start | bytes 2027528 | tf_op jit(solution)/shard_map/ppermute | solution.py:23
  6.6 33.0 %collective-permute-start.2 = (bf16[80,4224]{1,0:T(8,128)(2,1)}, bf16[80,4224]{1,0:T(8,128)(2,1)S(1)}, u32[]{:S(2)}, u32[]{:S(2)}) collective-permute-start(bf16[80,4224]{1,0:T(8,128)(2,1)} %get-tuple-element.16.refs_0_), channel_id=1, source_target_pairs={{0,16},{2,18},{4,20},{6,22},{8,24},{10,26},{12,28},{14,30},{16,0},... | collective-permute-start | bytes 2027528 | tf_op jit(solution)/shard_map/ppermute | solution.py:23
  39.5 15.4 %collective-permute-start.7 = (bf16[80,4224]{1,0:T(8,128)(2,1)S(1)}, bf16[80,4224]{1,0:T(8,128)(2,1)S(1)}, u32[]{:S(2)}, u32[]{:S(2)}) collective-permute-start(bf16[80,4224]{1,0:T(8,128)(2,1)S(1)} %collective-permute-done.2.refs_4_), channel_id=1, source_target_pairs={{0,8},{2,10},{4,12},{6,14},{8,0},{10,2},{12,4},{14,6},{16,24},{18,... | collective-permute-start | bytes 2027528 | tf_op jit(solution)/shard_map/ppermute | solution.py:23
  40.0 18.8 %collective-permute-start.6 = (bf16[80,4224]{1,0:T(8,128)(2,1)S(1)}, bf16[80,4224]{1,0:T(8,128)(2,1)S(1)}, u32[]{:S(2)}, u32[]{:S(2)}) collective-permute-start(bf16[80,4224]{1,0:T(8,128)(2,1)S(1)} %collective-permute-done.2.refs_4_), channel_id=1, source_target_pairs={{0,2},{2,0},{4,6},{6,4},{8,10},{10,8},{12,14},{14,12},{16,18},{18,... | collective-permute-start | bytes 2027528 | tf_op jit(solution)/shard_map/ppermute | solution.py:23
  40.0 18.8 %collective-permute-start.5 = (bf16[80,4224]{1,0:T(8,128)(2,1)S(1)}, bf16[80,4224]{1,0:T(8,128)(2,1)S(1)}, u32[]{:S(2)}, u32[]{:S(2)}) collective-permute-start(bf16[80,4224]{1,0:T(8,128)(2,1)S(1)} %collective-permute-done.3.refs_2_), channel_id=1, source_target_pairs={{0,2},{2,0},{4,6},{6,4},{8,10},{10,8},{12,14},{14,12},{16,18},{18,... | collective-permute-start | bytes 2027528 | tf_op jit(solution)/shard_map/ppermute | solution.py:23
  55.0 3.8 %collective-permute-start.8 = (bf16[80,4224]{1,0:T(8,128)(2,1)S(1)}, bf16[80,4224]{1,0:T(8,128)(2,1)S(1)}, u32[]{:S(2)}, u32[]{:S(2)}) collective-permute-start(bf16[80,4224]{1,0:T(8,128)(2,1)S(1)} %collective-permute-done.7.refs_6_), channel_id=1, source_target_pairs={{0,2},{2,0},{4,6},{6,4},{8,10},{10,8},{12,14},{14,12},{16,18},{18,... | collective-permute-start | bytes 2027528 | tf_op jit(solution)/shard_map/ppermute | solution.py:23
  55.0 3.8 %collective-permute-start = (s32[8,128]{1,0:T(8,128)}, s32[8,128]{1,0:T(8,128)S(1)}, u32[]{:S(2)}, u32[]{:S(2)}) collective-permute-start(s32[8,128]{1,0:T(8,128)} %get-tuple-element.15), channel_id=1, source_target_pairs={{0,4},{2,6},{4,0},{6,2},{8,12},{10,14},{12,8},{14,10},{16,20},{18,... | collective-permute-start | bytes 12296 | tf_op jit(solution)/shard_map/ppermute | solution.py:23
  58.8 0.9 copy-start.6
  59.7 1.3 %copy-start.5 = (bf16[256,4096]{1,0:T(8,128)(2,1)}, bf16[256,4096]{1,0:T(8,128)(2,1)S(1)}, u32[]{:S(2)}) copy-start(bf16[256,4096]{1,0:T(8,128)(2,1)S(1)} %collective-permute-done.1.theirs) | copy-start | bytes 6291460
  61.0 1.1 %copy-start = (bf16[80,4224]{1,0:T(8,128)(2,1)S(1)}, bf16[80,4224]{1,0:T(8,128)(2,1)}, u32[]{:S(2)}) copy-start(bf16[80,4224]{1,0:T(8,128)(2,1)} %get-tuple-element.16.refs_0_) | copy-start | bytes 2027524
  62.1 0.7 copy-start.3
  62.7 0.7 copy-start.4
  69.7 0.7 copy-start.1
  70.4 0.6 copy-start.2
  71.1 15.3 %collective-permute-start.10 = (f32[336,256]{1,0:T(8,128)S(1)}, f32[336,256]{1,0:T(8,128)S(1)}, u32[]{:S(2)}, u32[]{:S(2)}) collective-permute-start(f32[336,256]{1,0:T(8,128)S(1)} %get-tuple-element.23), channel_id=1, source_target_pairs={{0,4},{2,6},{4,0},{6,2},{8,12},{10,14},{12,8},{14,10},{16,20},{18,... | collective-permute-start | bytes 1032200 | tf_op jit(solution)/shard_map/ppermute | solution.py:23
  71.6 9.6 %collective-permute-start.9 = (f32[272,256]{1,0:T(8,128)S(1)}, f32[272,256]{1,0:T(8,128)S(1)}, u32[]{:S(2)}, u32[]{:S(2)}) collective-permute-start(f32[272,256]{1,0:T(8,128)S(1)} %get-tuple-element.22), channel_id=1, source_target_pairs={{0,1},{1,0},{2,3},{3,2},{4,5},{5,4},{6,7},{7,6},{8,9},{9,8},{10,11... | collective-permute-start | bytes 835592 | tf_op jit(solution)/shard_map/ppermute | solution.py:26
  73.0 13.2 %collective-permute-start.11 = (f32[272,256]{1,0:T(8,128)S(1)}, f32[272,256]{1,0:T(8,128)S(1)}, u32[]{:S(2)}, u32[]{:S(2)}) collective-permute-start(f32[272,256]{1,0:T(8,128)S(1)} %get-tuple-element.24), channel_id=1, source_target_pairs={{0,5},{1,4},{2,7},{3,6},{4,1},{5,0},{6,3},{7,2},{8,13},{9,12},{10,... | collective-permute-start | bytes 835592 | tf_op jit(solution)/shard_map/ppermute | solution.py:289
  81.1 5.2 %copy-start.8 = (f32[272,256]{1,0:T(8,128)}, f32[272,256]{1,0:T(8,128)S(1)}, u32[]{:S(2)}) copy-start(f32[272,256]{1,0:T(8,128)S(1)} %collective-permute-done.9.from_x) | copy-start | bytes 835588
  86.2 0.7 copy-start.9
  86.3 0.7 copy-start.7

commit v3 on v2

--- a/solution.py
+++ b/solution.py
@@ -1,5 +1,3 @@
-import functools
-
 import jax
 import jax.numpy as jnp
 from jax import lax
@@ -130,6 +128,12 @@
 TILE = 2 * WIDTH
 HALF = 2 * TILE
 UP_TILES = 4
+PAD = 24
+VMEM = 16 * MIB
+IN_SMEM = pl.BlockSpec(memory_space=pltpu.SMEM)
+IN_VMEM = pl.BlockSpec(memory_space=pltpu.VMEM)
+IN_HBM = pl.BlockSpec(memory_space=pltpu.HBM)
+IN_ANY = pl.BlockSpec(memory_space=pl.ANY)
 
 
 def place():
@@ -139,15 +143,12 @@
     return t, z % 2, y, core, part
 
 
-def prep_kernel(chosen, live, value, down, up, packet, ids):
+def prep_kernel(chosen, live, down, up, packet, ids):
     x = lax.axis_index("adapter")
-    features = value.shape[1]
-    packet[:WIDTH, :features] = value[...]
-    packet[pl.ds(WIDTH, RANK), :features] = down[...]
-    packet[pl.ds(WIDTH, RANK), pl.ds(features, LANES)] = jnp.zeros((RANK, LANES), BF16)
-    for j in range(UP_TILES):
-        start = pl.multiple_of((x * UP_TILES + j) * LANES, LANES)
-        packet[pl.ds(j * RANK, RANK), pl.ds(features, LANES)] = up[:, pl.ds(start, LANES)]
+    features = down.shape[1]
+    packet[:, :features] = down[...]
+    start = pl.multiple_of(x * 2 * HALF, LANES)
+    packet[:, pl.ds(features, 2 * HALF)] = up[:, pl.ds(start, 2 * HALF)]
     lane = lax.broadcasted_iota(jnp.int32, ids.shape, 1)
     line = jnp.zeros(ids.shape, jnp.int32)
     for b in range(2):
@@ -156,95 +157,178 @@
     ids[...] = line
 
 
-def prep(chosen, live, value, down, up):
-    features = value.shape[1]
-    vmem, smem = pl.BlockSpec(memory_space=pltpu.VMEM), pl.BlockSpec(memory_space=pltpu.SMEM)
+def prep(chosen, live, down, up):
+    features = down.shape[1]
     return pl.pallas_call(
         prep_kernel,
         out_shape=[
-            jax.ShapeDtypeStruct((WIDTH + RANK, features + LANES), BF16),
+            jax.ShapeDtypeStruct((RANK, features + 2 * HALF), BF16),
             jax.ShapeDtypeStruct((8, LANES), jnp.int32),
         ],
-        in_specs=[smem] * 2 + [vmem] * 3,
-        out_specs=[vmem] * 2,
-    )(chosen, live, value, down, up)
-
-
-def compute_kernel(chosen, live, ids_p, mine, theirs, *refs):
-    units, (kept, to_x, to_y, to_xy, up_own, w, d) = refs[: 2 * DEPTH], refs[2 * DEPTH :]
-    t, _, _, core, part = place()
-    rows, features = mine.shape
+        in_specs=[IN_SMEM] * 2 + [IN_VMEM] * 2,
+        out_specs=[IN_VMEM] * 2,
+        compiler_params=pltpu.CompilerParams(vmem_limit_bytes=60 * MIB),
+        cost_estimate=pl.CostEstimate(flops=0, bytes_accessed=MIB, transcendentals=0),
+    )(chosen, live, down, up)
+
+
+def gather_wide(wide, w, sems):
+    _, _, _, core, part = place()
+    copies = []
     for a in range(DEPTH):
         base = ((a // 2) ^ part) * HALF + (a % 2) * TILE
         for k in range(2):
             start = pl.multiple_of(base + (core ^ k) * WIDTH, WIDTH)
-            w[pl.ds(start, WIDTH), :] = units[2 * a + k][:WIDTH, :features]
-    up_own[...] = jnp.zeros_like(up_own)
-    to_y[pl.ds(rows + RANK, WIDTH), :] = jnp.zeros((WIDTH, HALF), F32)
+            i = 2 * a + k
+            copies.append(
+                pltpu.make_async_copy(wide[i], w.at[pl.ds(start, WIDTH), :], sems.at[i])
+            )
+    for c in copies:
+        c.start()
+    return copies
+
+
+def load_rows(pieces, rows_in, sems):
+    at, copies = 0, []
+    for i, ref in enumerate(pieces):
+        copies.append(
+            pltpu.make_async_copy(ref, rows_in.at[pl.ds(at, ref.shape[0])], sems.at[i])
+        )
+        at += ref.shape[0]
+    for c in copies:
+        c.start()
+    return copies
+
+
+def their_kernel(theirs, *refs):
+    wide, (to_y, to_xy, w, rows_in, w_sem, r_sem) = refs[: 2 * DEPTH], refs[2 * DEPTH :]
+    rows = rows_in.shape[0]
+    copies = load_rows((theirs,), rows_in, r_sem) + gather_wide(wide, w, w_sem)
+    for c in copies:
+        c.wait()
+    to_xy[:rows, :] = dot_nt(rows_in[...], w[pl.ds(HALF, HALF), :])
+    to_y[:rows, :] = dot_nt(rows_in[...], w[pl.ds(0, HALF), :])
+    for out in (to_y, to_xy):
+        out[pl.ds(rows, PAD), :] = jnp.zeros((PAD, HALF), F32)
+
+
+def their_sums(theirs, wide):
+    rows, features = theirs.shape
+    return pl.pallas_call(
+        their_kernel,
+        out_shape=[jax.ShapeDtypeStruct((rows + PAD, HALF), F32)] * 2,
+        in_specs=[IN_ANY] * (1 + len(wide)),
+        out_specs=[IN_VMEM] * 2,
+        scratch_shapes=[
+            pltpu.VMEM((2 * HALF, features), BF16),
+            pltpu.VMEM((rows, features), BF16),
+            pltpu.SemaphoreType.DMA((2 * DEPTH,)),
+            pltpu.SemaphoreType.DMA((1,)),
+        ],
+        compiler_params=pltpu.CompilerParams(vmem_limit_bytes=VMEM),
+        cost_estimate=pl.CostEstimate(flops=0, bytes_accessed=0, transcendentals=0),
+    )(theirs, *wide)
+
+
+def own_kernel(ids, ids_p, mine, theirs, narrow, narrow_v, *refs):
+    wide, refs = refs[: 2 * DEPTH], refs[2 * DEPTH :]
+    kept, to_x, m_y, m_xy, up_own, w, d, up, rows_in, w_sem, d_sem, r_sem = refs
+    t = lax.axis_index("tensor")
+    rows, features = mine.shape
+    cols = pl.ds(0, features)
+    copies = load_rows((mine, theirs), rows_in, r_sem) + gather_wide(wide, w, w_sem)
+
+    def fetch(b, ref, line):
+        lines = pl.ds(line, RANK)
+        return [
+            pltpu.make_async_copy(ref.at[lines, cols], d.at[b], d_sem.at[2 * b]),
+            pltpu.make_async_copy(
+                ref.at[lines, pl.ds(features, 2 * HALF)], up.at[b], d_sem.at[2 * b + 1]
+            ),
+        ]
+
+    where = []
     for b in range(4):
-        relative = (chosen[b] if b < 2 else ids_p[0, b - 2]) ^ t
-        spot = (relative // 4) * 2 + relative % 2
+        relative = (ids[0, b] if b < 2 else ids_p[0, b - 2]) ^ t
         here = ((relative // 2) % 2) == 0
-        lanes = pl.ds(b % 2 * LANES, LANES)
-        d[b] = jnp.zeros_like(d[b])
-        for u in range(2 * DEPTH):
-
-            @pl.when(here & (spot == u))
+        line, other = pl.multiple_of(relative // 4 * RANK, RANK), relative % 2
+        where.append(here)
+
+        @pl.when(jnp.logical_not(here))
+        def _():
+            d[b] = jnp.zeros_like(d[b])
+            up[b] = jnp.zeros_like(up[b])
+
+        for i, ref in enumerate((narrow, narrow_v)):
+
+            @pl.when(here & (other == i))
             def _():
-                d[b] = units[u][pl.ds(WIDTH, RANK), :features]
-                up = units[u][:WIDTH, pl.ds(features, LANES)].astype(F32)
-                if b < 2:
-                    up_own[:, lanes] = up
-                else:
-                    to_y[pl.ds(rows + RANK, WIDTH), lanes] = up
-
-    w_kept, w_sent = w[pl.ds(0, HALF), :], w[pl.ds(HALF, HALF), :]
-    kept[:rows, :] = dot_nt(mine[...], w_kept)
-    to_x[:rows, :] = dot_nt(mine[...], w_sent)
-    to_y[:rows, :] = dot_nt(theirs[...], w_kept)
-    to_xy[:rows, :] = dot_nt(theirs[...], w_sent)
-    line = pl.ds(rows, RANK)
+                for c in fetch(b, ref, line):
+                    c.start()
+
+    for c in copies:
+        c.wait()
+    to_x[:rows, :] = dot_nt(rows_in[pl.ds(0, rows), :], w[pl.ds(HALF, HALF), :])
+    kept[:rows, :] = dot_nt(rows_in[pl.ds(0, rows), :], w[pl.ds(0, HALF), :])
+    for b, here in enumerate(where):
+
+        @pl.when(here)
+        def _():
+            for c in fetch(b, narrow, 0):
+                c.wait()
+
     for b in range(4):
         at = pl.ds(b % 2 * BLK, BLK)
-        m = dot_nt(d[b], (mine if b < 2 else theirs)[at, :])
-        limit = live[b] if b < 2 else ids_p[0, b]
+        m = dot_nt(d[b], rows_in[pl.ds(b * BLK, BLK), :])
+        limit = ids[0, 2 + b] if b < 2 else ids_p[0, b]
         m = jnp.where(lax.broadcasted_iota(jnp.int32, m.shape, 1) < limit, m, 0.0)
         if b < 2:
-            kept[line, at] = m
-            to_x[line, at] = m
+            kept[pl.ds(rows, RANK), at] = m
+            to_x[pl.ds(rows, RANK), at] = m
+            up_own[b] = up[b]
         else:
-            to_y[line, at] = m
-            to_xy[line, at] = m
-
-
-def compute(scalars, rows, units):
-    count, features = rows[0].shape
-    vmem, smem = pl.BlockSpec(memory_space=pltpu.VMEM), pl.BlockSpec(memory_space=pltpu.SMEM)
-    short = jax.ShapeDtypeStruct((count + RANK, HALF), F32)
-    long = jax.ShapeDtypeStruct((count + RANK + WIDTH, HALF), F32)
+            m_y[:RANK, at] = m
+            m_xy[:, at] = m
+            for i in range(2):
+                m_y[pl.ds((b % 2 * 2 + i + 1) * RANK, RANK), :] = up[
+                    b, :, pl.ds(i * HALF, HALF)
+                ].astype(F32)
+
+
+def own_sums(scalars, mine, theirs, narrow, wide):
+    rows, features = mine.shape
+    shapes = [(rows + RANK, HALF), (rows + RANK, HALF), (5 * RANK, HALF), (RANK, HALF)]
     return pl.pallas_call(
-        compute_kernel,
-        out_shape=[short, short, long, short, jax.ShapeDtypeStruct((WIDTH, HALF), F32)],
-        in_specs=[smem] * 3 + [vmem] * (2 + len(units)),
-        out_specs=[vmem] * 5,
+        own_kernel,
+        out_shape=[jax.ShapeDtypeStruct(s, F32) for s in shapes]
+        + [jax.ShapeDtypeStruct((2, RANK, 2 * HALF), BF16)],
+        in_specs=[IN_SMEM] * 2 + [IN_ANY] * (4 + len(wide)),
+        out_specs=[IN_VMEM] * 5,
         scratch_shapes=[
             pltpu.VMEM((2 * HALF, features), BF16),
             pltpu.VMEM((4, RANK, features), BF16),
+            pltpu.VMEM((4, RANK, 2 * HALF), BF16),
+            pltpu.VMEM((2 * rows, features), BF16),
+            pltpu.SemaphoreType.DMA((2 * DEPTH,)),
+            pltpu.SemaphoreType.DMA((8,)),
+            pltpu.SemaphoreType.DMA((2,)),
         ],
-        compiler_params=pltpu.CompilerParams(vmem_limit_bytes=48 * MIB),
-        cost_estimate=pl.CostEstimate(
-            flops=4 * count * features * 2 * HALF, bytes_accessed=10 * MIB, transcendentals=0
-        ),
-    )(*scalars, *rows, *units)
-
-
-def final_kernel(kept, up_own, from_x, from_y, from_xy, out):
+        compiler_params=pltpu.CompilerParams(vmem_limit_bytes=VMEM),
+        cost_estimate=pl.CostEstimate(flops=0, bytes_accessed=0, transcendentals=0),
+    )(*scalars, mine, theirs, *narrow, *wide)
+
+
+def final_kernel(kept, up_own, from_x, from_y, from_xy, m_y, m_xy, out):
     _, z_low, y, _, _ = place()
-    rows = out.shape[0]
-    line = pl.ds(rows, RANK)
-    m = (kept[line, :] + from_x[line, :]) + (from_y[line, :] + from_xy[line, :])
+    line = pl.ds(out.shape[0], RANK)
+    m = (kept[line, :] + from_x[line, :]) + (m_y[:RANK, :] + m_xy[...])
     mid = m.T.astype(BF16)
-    up = (up_own[...] + from_y[pl.ds(rows + RANK, WIDTH), :]).astype(BF16)
+    up = []
+    for b in range(2):
+        for i in range(UP_TILES):
+            lines = pl.ds((b * 2 + i // 2 + 1) * RANK, RANK)
+            got = m_y[lines, pl.ds(i % 2 * LANES, LANES)].astype(BF16)
+            up.append(up_own[b, :, pl.ds(i * LANES, LANES)] + got)
     for tile in range(2):
         cols = pl.ds(tile * LANES, LANES)
         for side in range(2):
@@ -258,21 +342,21 @@
                     base = from_y[span, cols] + from_xy[span, cols]
                 picked = jnp.zeros((RANK, LANES), BF16)
                 for i in range(UP_TILES):
-                    piece = up[i * RANK : (i + 1) * RANK, b * LANES : (b + 1) * LANES]
-                    picked = jnp.where(j == i, piece, picked)
+                    picked = jnp.where(j == i, up[b * UP_TILES + i], picked)
                 extra = jnp.dot(
                     mid[b * BLK : (b + 1) * BLK], picked, preferred_element_type=F32
                 )
                 out[span, lanes] = (base + extra).astype(BF16)
 
 
-def final(rows, *args):
-    vmem = pl.BlockSpec(memory_space=pltpu.VMEM)
+def final(*args):
+    rows = args[0].shape[0] - RANK
     return pl.pallas_call(
         final_kernel,
         out_shape=jax.ShapeDtypeStruct((rows, 2 * HALF), BF16),
-        in_specs=[vmem] * len(args),
-        out_specs=vmem,
+        in_specs=[IN_VMEM] * len(args),
+        out_specs=IN_VMEM,
+        compiler_params=pltpu.CompilerParams(vmem_limit_bytes=VMEM),
     )(*args)
 
 
@@ -289,25 +373,33 @@
         return lax.ppermute(array, ("tensor", "adapter"), perm=pairs)
 
     def body(hidden, value, down, up, chosen, live):
-        rows, features = hidden.shape
+        features = hidden.shape[1]
+        w0, down = value.T, down.transpose(0, 2, 1).reshape(RANK, features)
         theirs = over_tensor(hidden, 2)
-        packet, ids = prep(
-            chosen, live, value.T, down.transpose(0, 2, 1).reshape(RANK, features), up[0]
+        w2, w1 = over_tensor(w0, 8), over_tensor(w0, 4)
+        v0 = over_tensor(w0, 1)
+        v0, down = tie((v0, down))
+        d0, ids = prep(chosen, live, down, up[0])
+        v1, w0 = over_tensor(w1, 1), over_tensor(v0, 1)
+        w2, v1, w0, d0, ids = tie((w2, v1, w0, d0, ids))
+        w3, v2 = over_tensor(w2, 4), over_tensor(w2, 1)
+        d2, d1 = over_tensor(d0, 8), over_tensor(d0, 4)
+        w3, v2, d2, d1, ids, theirs = tie((w3, v2, d2, d1, ids, theirs))
+        v3 = over_tensor(w3, 1)
+        d3 = over_tensor(d2, 4)
+        ids_p = over_tensor(ids, 2)
+        wide = (w0, v0, w1, v1, w2, v2, w3, v3)
+        theirs, ids_p = tie((theirs, ids_p))
+        to_y, to_xy = their_sums(theirs, wide)
+        to_y, to_xy, d3 = tie((to_y, to_xy, d3))
+        from_y, from_xy = over_tensor(to_y, 2), over_both(to_xy)
+        narrow = jnp.concatenate([d0, d1, d2, d3])
+        narrow_v = over_tensor(narrow, 1)
+        kept, to_x, m_y, m_xy, up_own = own_sums(
+            (ids, ids_p), hidden, theirs, (narrow, narrow_v), wide
         )
-        ids_p = over_tensor(ids, 2)
-        u2 = over_tensor(packet, 8)
-        u1 = over_tensor(packet, 4)
-        v0 = over_tensor(packet, 1)
-        u2, u1, v0 = tie((u2, u1, v0))
-        u3 = over_tensor(u2, 4)
-        v2, v1 = over_tensor(u2, 1), over_tensor(u1, 1)
-        v3 = over_tensor(u3, 1)
-        units = (packet, v0, u1, v1, u2, v2, u3, v3)
-        kept, to_x, to_y, to_xy, up_own = compute((chosen, live, ids_p), (hidden, theirs), units)
-        from_xy = over_both(to_xy)
-        from_x = over_adapter(to_x, 1)
-        from_y = over_tensor(to_y, 2)
-        return final(rows, kept, up_own, from_x, from_y, from_xy)
+        from_x, m_y, m_xy = over_adapter(to_x, 1), over_tensor(m_y, 2), over_both(m_xy)
+        return final(kept, up_own, from_x, from_y, from_xy, m_y, m_xy)
 
     return body
 

time: 89.6 us -> 76.6 us (0.85)
  waiting for transfers between devices: 60 us -> 47.3 us
  starting transfers between devices: 12.1 us -> 17.8 us
  local copies, waits for them, and re-layouts: 6.64 us -> 0.96 us
    ppermute x1, waiting for transfers between devices: 6.6 us -> 0.01 us  [over_adapter(): lax.ppermute(array, 'adapter', perm=[(i, i ^ flip) for i in range(adapter...]
    unnamed x20 -> x7, local copies, waits for them, and re-layouts: 6.64 us -> 0.95 us
    ppermute x1 -> x2, waiting for transfers between devices: 5.07 us -> 0.9 us  [over_both(): return lax.ppermute(array, ('tensor', 'adapter'), perm=pairs)]
    ppermute x10 -> x16, starting transfers between devices: 9.08 us -> 12.5 us  [over_tensor(): lax.ppermute(array, 'tensor', perm=[(i, i ^ flip) for i in range(tensor)])]
    ppermute x1 -> x2, starting transfers between devices: 1.51 us -> 4.74 us  [over_both(): return lax.ppermute(array, ('tensor', 'adapter'), perm=pairs)]
    ppermute x10 -> x16, waiting for transfers between devices: 48.3 us -> 46.4 us  [over_tensor(): lax.ppermute(array, 'tensor', perm=[(i, i ^ flip) for i in range(tensor)])]
    pallas_call x1, Pallas kernels: 2.26 us -> 1 us  [final(): pl.pallas_call(final_kernel, out_shape=jax.ShapeDtypeStruct((rows, 2 * HA...]
    pallas_call x2 -> x3, Pallas kernels: 8.36 us -> 9.18 us  [the longest x1 4.84 us: own_sums(): pl.pallas_call(own_kernel, out_shape=[jax.ShapeDtypeStruct(s, F32) for s...]
  transfers between devices with their start and end apart: 12 -> 19, of which waited for: 7 -> 8; matrix products, arithmetic and copies ran while one was open for 0% -> 1% of each run, Pallas kernels for 2% -> 12%
where the time goes in v3:
time: 76.6 us; the launch traced here: 76.4 us
  waiting for transfers between devices  47.3 us (62%)
  starting transfers between devices  17.8 us (23%)
  Pallas kernels  10.2 us (13%)
  local copies, waits for them, and re-layouts  0.96 us (1%)
    ppermute x16, waiting for transfers between devices, over_tensor(): lax.ppermute(array, 'tensor', perm=[(i, i ^ flip) for i in range(tensor)])  46.4 us
    ppermute x16, starting transfers between devices, over_tensor(): lax.ppermute(array, 'tensor', perm=[(i, i ^ flip) for i in range(tensor)])  12.5 us
    pallas_call x1, Pallas kernels, own_sums(): pl.pallas_call(own_kernel, out_shape=[jax.ShapeDtypeStruct(s, F32) for s...  4.84 us
    ppermute x2, starting transfers between devices, over_both(): return lax.ppermute(array, ('tensor', 'adapter'), perm=pairs)  4.74 us
    pallas_call x1, Pallas kernels, their_sums(): pl.pallas_call(their_kernel, out_shape=[jax.ShapeDtypeStruct((rows + PAD,...  2.74 us
    pallas_call x1, Pallas kernels, prep(): pl.pallas_call(prep_kernel, out_shape=[jax.ShapeDtypeStruct((RANK, featur...  1.59 us
  transfers between devices with their start and end apart: 19, of which 8 were waited for; matrix products, arithmetic and copies ran while one was open for 1% of the time, Pallas kernels for 12%

profile of v3, /device:TPU:0, one launch (start us, length us, event | category | flops | bytes accessed | tf_op | source)
XLA Modules:
  0.0 76.4 jit_solution(17675291898565704320)
XLA Ops:
  0.0 3.0 %collective-permute-start.9 = (bf16[256,4096]{1,0:T(8,128)(2,1)}, bf16[256,4096]{1,0:T(8,128)(2,1)S(1)}, u32[]{:S(2)}, u32[]{:S(2)}) collective-permute-start(bf16[256,4096]{1,0:T(8,128)(2,1)} %mine.1), channel_id=1, source_target_pairs={{0,4},{2,6},{4,0},{6,2},{8,12},{10,14},{12,8},{14,10},{16,20},{18,... | collective-permute-start | bytes 6291464 | tf_op jit(solution)/shard_map/ppermute | solution.py:21
  3.0 0.0 collective-permute-start.3
  3.0 1.6 %collective-permute-start.1 = (bf16[64,4096]{1,0:T(8,128)(2,1)}, bf16[64,4096]{1,0:T(8,128)(2,1)S(1)}, u32[]{:S(2)}, u32[]{:S(2)}) collective-permute-start(bf16[64,4096]{1,0:T(8,128)(2,1)} %bitcast.8), channel_id=1, source_target_pairs={{0,8},{2,10},{4,12},{6,14},{8,0},{10,2},{12,4},{14,6},{16,24},{18,... | collective-permute-start | bytes 1572872 | tf_op jit(solution)/shard_map/ppermute | solution.py:21
  4.5 2.6 %collective-permute-start = (bf16[64,4096]{1,0:T(8,128)(2,1)}, bf16[64,4096]{1,0:T(8,128)(2,1)S(1)}, u32[]{:S(2)}, u32[]{:S(2)}) collective-permute-start(bf16[64,4096]{1,0:T(8,128)(2,1)} %bitcast.9), channel_id=1, source_target_pairs={{0,16},{2,18},{4,20},{6,22},{8,24},{10,26},{12,28},{14,30},{16,0},... | collective-permute-start | bytes 1572872 | tf_op jit(solution)/shard_map/ppermute | solution.py:21
  7.1 21.5 %collective-permute-done.1.refs_2_ = bf16[64,4096]{1,0:T(8,128)(2,1)S(1)} collective-permute-done((bf16[64,4096]{1,0:T(8,128)(2,1)}, bf16[64,4096]{1,0:T(8,128)(2,1)S(1)}, u32[]{:S(2)}, u32[]{:S(2)}) %collective-permute-start.1) | collective-permute-done | bytes 524320 | tf_op jit(solution)/shard_map/ppermute | solution.py:21
  28.6 0.0 collective-permute-start.2
  28.6 1.6 %shard_map.64 = (bf16[16,4608]{1,0:T(8,128)(2,1)}, s32[8,128]{1,0:T(8,128)}) custom-call(s32[2]{0:T(128)} %chosen.1, s32[2]{0:T(128)} %live.1, bf16[16,4096]{1,0:T(8,128)(2,1)} %bitcast.5, bf16[16,1024]{1,0:T(8,128)(2,1)} %bitcast.6), custom_call_target="tpu_custom_call" | custom-call | bytes 1048576 | tf_op jit(solution)/shard_map/pallas_call | solution.py:162
  30.2 0.8 %collective-permute-done.refs_4_ = bf16[64,4096]{1,0:T(8,128)(2,1)S(1)} collective-permute-done((bf16[64,4096]{1,0:T(8,128)(2,1)}, bf16[64,4096]{1,0:T(8,128)(2,1)S(1)}, u32[]{:S(2)}, u32[]{:S(2)}) %collective-permute-start) | collective-permute-done | bytes 524320 | tf_op jit(solution)/shard_map/ppermute | solution.py:21
  31.0 0.0 collective-permute-done.4.refs_0_
  31.0 0.0 collective-permute-done.2.refs_3_
  31.0 0.4 collective-permute-start.8
  31.5 2.6 %collective-permute-start.7 = (bf16[16,4608]{1,0:T(8,128)(2,1)}, bf16[16,4608]{1,0:T(8,128)(2,1)S(1)}, u32[]{:S(2)}, u32[]{:S(2)}) collective-permute-start(bf16[16,4608]{1,0:T(8,128)(2,1)} %get-tuple-element.37), channel_id=1, source_target_pairs={{0,16},{2,18},{4,20},{6,22},{8,24},{10,26},{12,28},{14,30},{16,0},... | collective-permute-start | bytes 442376 | tf_op jit(solution)/shard_map/ppermute | solution.py:21
  34.0 0.1 collective-permute-start.5
  34.1 0.9 %constant_dynamic-update-slice_fusion.3 = bf16[64,4608]{1,0:T(8,128)(2,1)S(1)} fusion(bf16[16,4608]{1,0:T(8,128)(2,1)} %get-tuple-element.37), kind=kLoop, calls=%fused_computation.3 | loop fusion | bytes 294912
  35.0 6.1 %collective-permute-done.8 = bf16[16,4608]{1,0:T(8,128)(2,1)S(1)} collective-permute-done((bf16[16,4608]{1,0:T(8,128)(2,1)}, bf16[16,4608]{1,0:T(8,128)(2,1)S(1)}, u32[]{:S(2)}, u32[]{:S(2)}) %collective-permute-start.8) | collective-permute-done | bytes 147488 | tf_op jit(solution)/shard_map/ppermute | solution.py:21
  41.1 10.0 %collective-permute-done.5.refs_6_ = bf16[64,4096]{1,0:T(8,128)(2,1)S(1)} collective-permute-done((bf16[64,4096]{1,0:T(8,128)(2,1)S(1)}, bf16[64,4096]{1,0:T(8,128)(2,1)S(1)}, u32[]{:S(2)}, u32[]{:S(2)}) %collective-permute-start.5) | collective-permute-done | bytes 524320 | tf_op jit(solution)/shard_map/ppermute | solution.py:21
  51.2 0.3 collective-permute-start.10
  51.5 0.6 collective-permute-start.12
  52.2 0.0 copy-start
  52.2 2.8 %collective-permute-done.10.ids_p = s32[8,128]{1,0:T(8,128)S(1)} collective-permute-done((s32[8,128]{1,0:T(8,128)}, s32[8,128]{1,0:T(8,128)S(1)}, u32[]{:S(2)}, u32[]{:S(2)}) %collective-permute-start.10) | collective-permute-done | bytes 4128 | tf_op jit(solution)/shard_map/ppermute | solution.py:21
  55.0 2.7 %shard_map.65 = (f32[280,256]{1,0:T(8,128)S(1)}, f32[280,256]{1,0:T(8,128)S(1)}) custom-call(bf16[256,4096]{1,0:T(8,128)(2,1)S(1)} %collective-permute-done.9.theirs, bf16[64,4096]{1,0:T(8,128)(2,1)} %collective-permute-done.4.refs_0_, bf16[64,4096]{1,0:T(8,128)(2,1)S(1)} %collective-permute-done.3.refs_1_, ...), custom_call_target="tpu_custom_call" | custom-call | tf_op jit(solution)/shard_map/pallas_call | solution.py:217
  57.8 0.1 collective-permute-start.13
  57.9 0.6 collective-permute-start.15
  58.5 2.4 %collective-permute-start.16 = (f32[280,256]{1,0:T(8,128)S(1)}, f32[280,256]{1,0:T(8,128)S(1)}, u32[]{:S(2)}, u32[]{:S(2)}) collective-permute-start(f32[280,256]{1,0:T(8,128)S(1)} %get-tuple-element.56), channel_id=1, source_target_pairs={{0,5},{1,4},{2,7},{3,6},{4,1},{5,0},{6,3},{7,2},{8,13},{9,12},{10,... | collective-permute-start | bytes 860168 | tf_op jit(solution)/shard_map/ppermute | solution.py:373
  60.9 4.8 %shard_map.66 = (f32[272,256]{1,0:T(8,128)S(1)}, f32[272,256]{1,0:T(8,128)S(1)}, f32[80,256]{1,0:T(8,128)S(1)}, f32[16,256]{1,0:T(8,128)S(1)}, bf16[2,16,512]{2,1,0:T(8,128)(2,1)S(1)}) custom-call(s32[8,128]{1,0:T(8,128)S(1)} %copy-done.1, s32[8,128]{1,0:T(8,128)S(1)} %collective-permute-done.10.ids_p, bf16[256,4096]{1,0:T(8,128)(2,1)S(1)} %copy-done, ...), custom_call_target="tpu_custom_call" | custom-call | tf_op jit(solution)/shard_map/pallas_call | solution.py:301
  65.7 0.6 collective-permute-start.14
  66.3 0.6 collective-permute-start.17
  66.9 2.4 %collective-permute-start.18 = (f32[16,256]{1,0:T(8,128)S(1)}, f32[16,256]{1,0:T(8,128)S(1)}, u32[]{:S(2)}, u32[]{:S(2)}) collective-permute-start(f32[16,256]{1,0:T(8,128)S(1)} %get-tuple-element.58), channel_id=1, source_target_pairs={{0,5},{1,4},{2,7},{3,6},{4,1},{5,0},{6,3},{7,2},{8,13},{9,12},{10,... | collective-permute-start | bytes 49160 | tf_op jit(solution)/shard_map/ppermute | solution.py:373
  69.3 4.6 %collective-permute-done.15.from_y = f32[280,256]{1,0:T(8,128)S(1)} collective-permute-done((f32[280,256]{1,0:T(8,128)S(1)}, f32[280,256]{1,0:T(8,128)S(1)}, u32[]{:S(2)}, u32[]{:S(2)}) %collective-permute-start.15) | collective-permute-done | bytes 286752 | tf_op jit(solution)/shard_map/ppermute | solution.py:21
  73.9 0.9 %collective-permute-done.18.m_xy = f32[16,256]{1,0:T(8,128)S(1)} collective-permute-done((f32[16,256]{1,0:T(8,128)S(1)}, f32[16,256]{1,0:T(8,128)S(1)}, u32[]{:S(2)}, u32[]{:S(2)}) %collective-permute-start.18) | collective-permute-done | bytes 16416 | tf_op jit(solution)/shard_map/ppermute | solution.py:373
  74.8 0.6 collective-permute-done.17.m_y
  75.4 1.0 %shard_map.67 = bf16[256,512]{1,0:T(8,128)(2,1)} custom-call(f32[272,256]{1,0:T(8,128)S(1)} %get-tuple-element.52.kept, bf16[2,16,512]{2,1,0:T(8,128)(2,1)S(1)} %get-tuple-element.53.up_own, f32[272,256]{1,0:T(8,128)S(1)} %collective-permute-done.14.from_x, f32[280,256]{1,0:T(8,128)S(1)} %collective-permute-done.15.from_y, ...), custom_call_target="tpu_custom_call" | custom-call | tf_op jit(solution)/shard_map/pallas_call | solution.py:354
  (18 shorter events, 0.1 us)
Async XLA Ops:
  0.0 51.2 %collective-permute-start.9 = (bf16[256,4096]{1,0:T(8,128)(2,1)}, bf16[256,4096]{1,0:T(8,128)(2,1)S(1)}, u32[]{:S(2)}, u32[]{:S(2)}) collective-permute-start(bf16[256,4096]{1,0:T(8,128)(2,1)} %mine.1), channel_id=1, source_target_pairs={{0,4},{2,6},{4,0},{6,2},{8,12},{10,14},{12,8},{14,10},{16,20},{18,... | collective-permute-start | bytes 6291464 | tf_op jit(solution)/shard_map/ppermute | solution.py:21
  3.0 4.2 %collective-permute-start.3 = (bf16[64,4096]{1,0:T(8,128)(2,1)}, bf16[64,4096]{1,0:T(8,128)(2,1)S(1)}, u32[]{:S(2)}, u32[]{:S(2)}) collective-permute-start(bf16[64,4096]{1,0:T(8,128)(2,1)} %bitcast.7), channel_id=1, source_target_pairs={{0,2},{2,0},{4,6},{6,4},{8,10},{10,8},{12,14},{14,12},{16,18},{18,... | collective-permute-start | bytes 1572872 | tf_op jit(solution)/shard_map/ppermute | solution.py:21
  3.0 25.7 %collective-permute-start.1 = (bf16[64,4096]{1,0:T(8,128)(2,1)}, bf16[64,4096]{1,0:T(8,128)(2,1)S(1)}, u32[]{:S(2)}, u32[]{:S(2)}) collective-permute-start(bf16[64,4096]{1,0:T(8,128)(2,1)} %bitcast.8), channel_id=1, source_target_pairs={{0,8},{2,10},{4,12},{6,14},{8,0},{10,2},{12,4},{14,6},{16,24},{18,... | collective-permute-start | bytes 1572872 | tf_op jit(solution)/shard_map/ppermute | solution.py:21
  4.5 26.5 %collective-permute-start = (bf16[64,4096]{1,0:T(8,128)(2,1)}, bf16[64,4096]{1,0:T(8,128)(2,1)S(1)}, u32[]{:S(2)}, u32[]{:S(2)}) collective-permute-start(bf16[64,4096]{1,0:T(8,128)(2,1)} %bitcast.9), channel_id=1, source_target_pairs={{0,16},{2,18},{4,20},{6,22},{8,24},{10,26},{12,28},{14,30},{16,0},... | collective-permute-start | bytes 1572872 | tf_op jit(solution)/shard_map/ppermute | solution.py:21
  7.1 23.9 %collective-permute-start.4 = (bf16[64,4096]{1,0:T(8,128)(2,1)S(1)}, bf16[64,4096]{1,0:T(8,128)(2,1)}, u32[]{:S(2)}, u32[]{:S(2)}) collective-permute-start(bf16[64,4096]{1,0:T(8,128)(2,1)S(1)} %collective-permute-done.3.refs_1_), channel_id=1, source_target_pairs={{0,2},{2,0},{4,6},{6,4},{8,10},{10,8},{12,14},{14,12},{16,18},{18,... | collective-permute-start | bytes 1572872 | tf_op jit(solution)/shard_map/ppermute | solution.py:21
  28.6 2.4 %collective-permute-start.2 = (bf16[64,4096]{1,0:T(8,128)(2,1)S(1)}, bf16[64,4096]{1,0:T(8,128)(2,1)}, u32[]{:S(2)}, u32[]{:S(2)}) collective-permute-start(bf16[64,4096]{1,0:T(8,128)(2,1)S(1)} %collective-permute-done.1.refs_2_), channel_id=1, source_target_pairs={{0,2},{2,0},{4,6},{6,4},{8,10},{10,8},{12,14},{14,12},{16,18},{18,... | collective-permute-start | bytes 1572872 | tf_op jit(solution)/shard_map/ppermute | solution.py:21
  31.0 10.1 %collective-permute-start.8 = (bf16[16,4608]{1,0:T(8,128)(2,1)}, bf16[16,4608]{1,0:T(8,128)(2,1)S(1)}, u32[]{:S(2)}, u32[]{:S(2)}) collective-permute-start(bf16[16,4608]{1,0:T(8,128)(2,1)} %get-tuple-element.37), channel_id=1, source_target_pairs={{0,8},{2,10},{4,12},{6,14},{8,0},{10,2},{12,4},{14,6},{16,24},{18,... | collective-permute-start | bytes 442376 | tf_op jit(solution)/shard_map/ppermute | solution.py:21
  31.5 9.7 %collective-permute-start.7 = (bf16[16,4608]{1,0:T(8,128)(2,1)}, bf16[16,4608]{1,0:T(8,128)(2,1)S(1)}, u32[]{:S(2)}, u32[]{:S(2)}) collective-permute-start(bf16[16,4608]{1,0:T(8,128)(2,1)} %get-tuple-element.37), channel_id=1, source_target_pairs={{0,16},{2,18},{4,20},{6,22},{8,24},{10,26},{12,28},{14,30},{16,0},... | collective-permute-start | bytes 442376 | tf_op jit(solution)/shard_map/ppermute | solution.py:21
  34.0 7.1 %collective-permute-start.6 = (bf16[64,4096]{1,0:T(8,128)(2,1)S(1)}, bf16[64,4096]{1,0:T(8,128)(2,1)S(1)}, u32[]{:S(2)}, u32[]{:S(2)}) collective-permute-start(bf16[64,4096]{1,0:T(8,128)(2,1)S(1)} %collective-permute-done.refs_4_), channel_id=1, source_target_pairs={{0,2},{2,0},{4,6},{6,4},{8,10},{10,8},{12,14},{14,12},{16,18},{18,... | collective-permute-start | bytes 1572872 | tf_op jit(solution)/shard_map/ppermute | solution.py:21
  34.0 17.1 %collective-permute-start.5 = (bf16[64,4096]{1,0:T(8,128)(2,1)S(1)}, bf16[64,4096]{1,0:T(8,128)(2,1)S(1)}, u32[]{:S(2)}, u32[]{:S(2)}) collective-permute-start(bf16[64,4096]{1,0:T(8,128)(2,1)S(1)} %collective-permute-done.refs_4_), channel_id=1, source_target_pairs={{0,8},{2,10},{4,12},{6,14},{8,0},{10,2},{12,4},{14,6},{16,24},{18,... | collective-permute-start | bytes 1572872 | tf_op jit(solution)/shard_map/ppermute | solution.py:21
  51.2 3.8 %collective-permute-start.10 = (s32[8,128]{1,0:T(8,128)}, s32[8,128]{1,0:T(8,128)S(1)}, u32[]{:S(2)}, u32[]{:S(2)}) collective-permute-start(s32[8,128]{1,0:T(8,128)} %get-tuple-element.39.ids), channel_id=1, source_target_pairs={{0,4},{2,6},{4,0},{6,2},{8,12},{10,14},{12,8},{14,10},{16,20},{18,... | collective-permute-start | bytes 12296 | tf_op jit(solution)/shard_map/ppermute | solution.py:21
  51.5 6.2 %collective-permute-start.12 = (bf16[16,4608]{1,0:T(8,128)(2,1)S(1)}, bf16[16,4608]{1,0:T(8,128)(2,1)S(1)}, u32[]{:S(2)}, u32[]{:S(2)}) collective-permute-start(bf16[16,4608]{1,0:T(8,128)(2,1)S(1)} %collective-permute-done.7), channel_id=1, source_target_pairs={{0,8},{2,10},{4,12},{6,14},{8,0},{10,2},{12,4},{14,6},{16,24},{18,... | collective-permute-start | bytes 442376 | tf_op jit(solution)/shard_map/ppermute | solution.py:21
  52.1 2.9 %collective-permute-start.11 = (bf16[64,4096]{1,0:T(8,128)(2,1)S(1)}, bf16[64,4096]{1,0:T(8,128)(2,1)S(1)}, u32[]{:S(2)}, u32[]{:S(2)}) collective-permute-start(bf16[64,4096]{1,0:T(8,128)(2,1)S(1)} %collective-permute-done.5.refs_6_), channel_id=1, source_target_pairs={{0,2},{2,0},{4,6},{6,4},{8,10},{10,8},{12,14},{14,12},{16,18},{18,... | collective-permute-start | bytes 1572872 | tf_op jit(solution)/shard_map/ppermute | solution.py:21
  52.2 8.7 %copy-start = (bf16[256,4096]{1,0:T(8,128)(2,1)S(1)}, bf16[256,4096]{1,0:T(8,128)(2,1)}, u32[]{:S(2)}) copy-start(bf16[256,4096]{1,0:T(8,128)(2,1)} %mine.1) | copy-start | bytes 6291460
  52.2 8.7 %copy-start.1 = (s32[8,128]{1,0:T(8,128)S(1)}, s32[8,128]{1,0:T(8,128)}, u32[]{:S(2)}) copy-start(s32[8,128]{1,0:T(8,128)} %get-tuple-element.39.ids) | copy-start | bytes 12292
  57.8 3.1 %collective-permute-start.13 = (bf16[64,4608]{1,0:T(8,128)(2,1)S(1)}, bf16[64,4608]{1,0:T(8,128)(2,1)S(1)}, u32[]{:S(2)}, u32[]{:S(2)}) collective-permute-start(bf16[64,4608]{1,0:T(8,128)(2,1)S(1)} %constant_dynamic-update-slice_fusion.narrow), channel_id=1, source_target_pairs={{0,2},{2,0},{4,6},{6,4},{8,10},{10,8},{12,14},{14,12},{16,18},{18,... | collective-permute-start | bytes 1769480 | tf_op jit(solution)/shard_map/ppermute | solution.py:21
  57.9 16.0 %collective-permute-start.15 = (f32[280,256]{1,0:T(8,128)S(1)}, f32[280,256]{1,0:T(8,128)S(1)}, u32[]{:S(2)}, u32[]{:S(2)}) collective-permute-start(f32[280,256]{1,0:T(8,128)S(1)} %get-tuple-element.55), channel_id=1, source_target_pairs={{0,4},{2,6},{4,0},{6,2},{8,12},{10,14},{12,8},{14,10},{16,20},{18,... | collective-permute-start | bytes 860168 | tf_op jit(solution)/shard_map/ppermute | solution.py:21
  58.5 15.4 %collective-permute-start.16 = (f32[280,256]{1,0:T(8,128)S(1)}, f32[280,256]{1,0:T(8,128)S(1)}, u32[]{:S(2)}, u32[]{:S(2)}) collective-permute-start(f32[280,256]{1,0:T(8,128)S(1)} %get-tuple-element.56), channel_id=1, source_target_pairs={{0,5},{1,4},{2,7},{3,6},{4,1},{5,0},{6,3},{7,2},{8,13},{9,12},{10,... | collective-permute-start | bytes 860168 | tf_op jit(solution)/shard_map/ppermute | solution.py:373
  65.7 9.6 %collective-permute-start.14 = (f32[272,256]{1,0:T(8,128)S(1)}, f32[272,256]{1,0:T(8,128)S(1)}, u32[]{:S(2)}, u32[]{:S(2)}) collective-permute-start(f32[272,256]{1,0:T(8,128)S(1)} %get-tuple-element.54), channel_id=1, source_target_pairs={{0,1},{1,0},{2,3},{3,2},{4,5},{5,4},{6,7},{7,6},{8,9},{9,8},{10,11... | collective-permute-start | bytes 835592 | tf_op jit(solution)/shard_map/ppermute | solution.py:24
  66.3 9.0 %collective-permute-start.17 = (f32[80,256]{1,0:T(8,128)S(1)}, f32[80,256]{1,0:T(8,128)S(1)}, u32[]{:S(2)}, u32[]{:S(2)}) collective-permute-start(f32[80,256]{1,0:T(8,128)S(1)} %get-tuple-element.57), channel_id=1, source_target_pairs={{0,4},{2,6},{4,0},{6,2},{8,12},{10,14},{12,8},{14,10},{16,20},{18,... | collective-permute-start | bytes 245768 | tf_op jit(solution)/shard_map/ppermute | solution.py:21
  66.9 7.8 %collective-permute-start.18 = (f32[16,256]{1,0:T(8,128)S(1)}, f32[16,256]{1,0:T(8,128)S(1)}, u32[]{:S(2)}, u32[]{:S(2)}) collective-permute-start(f32[16,256]{1,0:T(8,128)S(1)} %get-tuple-element.58), channel_id=1, source_target_pairs={{0,5},{1,4},{2,7},{3,6},{4,1},{5,0},{6,3},{7,2},{8,13},{9,12},{10,... | collective-permute-start | bytes 49160 | tf_op jit(solution)/shard_map/ppermute | solution.py:373

commit v4 on v3

--- a/solution.py
+++ b/solution.py
@@ -128,7 +128,6 @@
 TILE = 2 * WIDTH
 HALF = 2 * TILE
 UP_TILES = 4
-PAD = 24
 VMEM = 16 * MIB
 IN_SMEM = pl.BlockSpec(memory_space=pltpu.SMEM)
 IN_VMEM = pl.BlockSpec(memory_space=pltpu.VMEM)
@@ -143,45 +142,20 @@
     return t, z % 2, y, core, part
 
 
-def prep_kernel(chosen, live, down, up, packet, ids):
-    x = lax.axis_index("adapter")
-    features = down.shape[1]
-    packet[:, :features] = down[...]
-    start = pl.multiple_of(x * 2 * HALF, LANES)
-    packet[:, pl.ds(features, 2 * HALF)] = up[:, pl.ds(start, 2 * HALF)]
-    lane = lax.broadcasted_iota(jnp.int32, ids.shape, 1)
-    line = jnp.zeros(ids.shape, jnp.int32)
-    for b in range(2):
-        line = jnp.where(lane == b, chosen[b], line)
-        line = jnp.where(lane == 2 + b, live[b], line)
-    ids[...] = line
-
-
-def prep(chosen, live, down, up):
-    features = down.shape[1]
-    return pl.pallas_call(
-        prep_kernel,
-        out_shape=[
-            jax.ShapeDtypeStruct((RANK, features + 2 * HALF), BF16),
-            jax.ShapeDtypeStruct((8, LANES), jnp.int32),
-        ],
-        in_specs=[IN_SMEM] * 2 + [IN_VMEM] * 2,
-        out_specs=[IN_VMEM] * 2,
-        compiler_params=pltpu.CompilerParams(vmem_limit_bytes=60 * MIB),
-        cost_estimate=pl.CostEstimate(flops=0, bytes_accessed=MIB, transcendentals=0),
-    )(chosen, live, down, up)
-
-
 def gather_wide(wide, w, sems):
     _, _, _, core, part = place()
     copies = []
     for a in range(DEPTH):
         base = ((a // 2) ^ part) * HALF + (a % 2) * TILE
+        last = a == DEPTH - 1
         for k in range(2):
             start = pl.multiple_of(base + (core ^ k) * WIDTH, WIDTH)
-            i = 2 * a + k
             copies.append(
-                pltpu.make_async_copy(wide[i], w.at[pl.ds(start, WIDTH), :], sems.at[i])
+                pltpu.make_async_copy(
+                    wide[2 * k + last].at[pl.ds(0 if last else a * WIDTH, WIDTH)],
+                    w.at[pl.ds(start, WIDTH), :],
+                    sems.at[2 * a + k],
+                )
             )
     for c in copies:
         c.start()
@@ -200,23 +174,20 @@
     return copies
 
 
-def their_kernel(theirs, *refs):
-    wide, (to_y, to_xy, w, rows_in, w_sem, r_sem) = refs[: 2 * DEPTH], refs[2 * DEPTH :]
-    rows = rows_in.shape[0]
-    copies = load_rows((theirs,), rows_in, r_sem) + gather_wide(wide, w, w_sem)
+def base_kernel(rows_ref, *refs):
+    wide, (kept, sent, w, rows_in, w_sem, r_sem) = refs[:4], refs[4:]
+    copies = load_rows((rows_ref,), rows_in, r_sem) + gather_wide(wide, w, w_sem)
     for c in copies:
         c.wait()
-    to_xy[:rows, :] = dot_nt(rows_in[...], w[pl.ds(HALF, HALF), :])
-    to_y[:rows, :] = dot_nt(rows_in[...], w[pl.ds(0, HALF), :])
-    for out in (to_y, to_xy):
-        out[pl.ds(rows, PAD), :] = jnp.zeros((PAD, HALF), F32)
-
-
-def their_sums(theirs, wide):
-    rows, features = theirs.shape
+    sent[...] = dot_nt(rows_in[...], w[pl.ds(HALF, HALF), :])
+    kept[...] = dot_nt(rows_in[...], w[pl.ds(0, HALF), :])
+
+
+def base_sums(rows_in, wide):
+    rows, features = rows_in.shape
     return pl.pallas_call(
-        their_kernel,
-        out_shape=[jax.ShapeDtypeStruct((rows + PAD, HALF), F32)] * 2,
+        base_kernel,
+        out_shape=[jax.ShapeDtypeStruct((rows, HALF), F32)] * 2,
         in_specs=[IN_ANY] * (1 + len(wide)),
         out_specs=[IN_VMEM] * 2,
         scratch_shapes=[
@@ -225,13 +196,13 @@
             pltpu.SemaphoreType.DMA((2 * DEPTH,)),
             pltpu.SemaphoreType.DMA((1,)),
         ],
-        compiler_params=pltpu.CompilerParams(vmem_limit_bytes=VMEM),
+        compiler_params=pltpu.CompilerParams(vmem_limit_bytes=9 * MIB),
         cost_estimate=pl.CostEstimate(flops=0, bytes_accessed=0, transcendentals=0),
-    )(theirs, *wide)
-
-
-def own_kernel(ids, ids_p, mine, theirs, narrow, narrow_v, *refs):
-    wide, refs = refs[: 2 * DEPTH], refs[2 * DEPTH :]
+    )(rows_in, *wide)
+
+
+def own_kernel(ids, ids_p, mine, theirs, *refs):
+    wide, narrow, refs = refs[:4], refs[4:8], refs[8:]
     kept, to_x, m_y, m_xy, up_own, w, d, up, rows_in, w_sem, d_sem, r_sem = refs
     t = lax.axis_index("tensor")
     rows, features = mine.shape
@@ -249,9 +220,9 @@
 
     where = []
     for b in range(4):
-        relative = (ids[0, b] if b < 2 else ids_p[0, b - 2]) ^ t
+        relative = (ids[b] if b < 2 else ids_p[b - 2]) ^ t
         here = ((relative // 2) % 2) == 0
-        line, other = pl.multiple_of(relative // 4 * RANK, RANK), relative % 2
+        unit, other = relative // 4, relative % 2
         where.append(here)
 
         @pl.when(jnp.logical_not(here))
@@ -259,10 +230,12 @@
             d[b] = jnp.zeros_like(d[b])
             up[b] = jnp.zeros_like(up[b])
 
-        for i, ref in enumerate((narrow, narrow_v)):
-
-            @pl.when(here & (other == i))
+        for i, ref in enumerate(narrow):
+            last = i >= 2
+
+            @pl.when(here & (other == i % 2) & ((unit == DEPTH - 1) == last))
             def _():
+                line = 0 if last else pl.multiple_of(unit * RANK, RANK)
                 for c in fetch(b, ref, line):
                     c.start()
 
@@ -274,13 +247,13 @@
 
         @pl.when(here)
         def _():
-            for c in fetch(b, narrow, 0):
+            for c in fetch(b, narrow[2], 0):
                 c.wait()
 
     for b in range(4):
         at = pl.ds(b % 2 * BLK, BLK)
         m = dot_nt(d[b], rows_in[pl.ds(b * BLK, BLK), :])
-        limit = ids[0, 2 + b] if b < 2 else ids_p[0, b]
+        limit = ids[2 + b] if b < 2 else ids_p[b]
         m = jnp.where(lax.broadcasted_iota(jnp.int32, m.shape, 1) < limit, m, 0.0)
         if b < 2:
             kept[pl.ds(rows, RANK), at] = m
@@ -302,7 +275,7 @@
         own_kernel,
         out_shape=[jax.ShapeDtypeStruct(s, F32) for s in shapes]
         + [jax.ShapeDtypeStruct((2, RANK, 2 * HALF), BF16)],
-        in_specs=[IN_SMEM] * 2 + [IN_ANY] * (4 + len(wide)),
+        in_specs=[IN_SMEM] * 2 + [IN_ANY] * (2 + len(wide) + len(narrow)),
         out_specs=[IN_VMEM] * 5,
         scratch_shapes=[
             pltpu.VMEM((2 * HALF, features), BF16),
@@ -313,12 +286,27 @@
             pltpu.SemaphoreType.DMA((8,)),
             pltpu.SemaphoreType.DMA((2,)),
         ],
-        compiler_params=pltpu.CompilerParams(vmem_limit_bytes=VMEM),
+        compiler_params=pltpu.CompilerParams(vmem_limit_bytes=13 * MIB),
         cost_estimate=pl.CostEstimate(flops=0, bytes_accessed=0, transcendentals=0),
-    )(*scalars, mine, theirs, *narrow, *wide)
-
-
-def final_kernel(kept, up_own, from_x, from_y, from_xy, m_y, m_xy, out):
+    )(*scalars, mine, theirs, *wide, *narrow)
+
+
+def add_kernel(a, b, out):
+    out[...] = a[...] + b[...]
+
+
+def add(a, b):
+    return pl.pallas_call(
+        add_kernel,
+        out_shape=jax.ShapeDtypeStruct(a.shape, F32),
+        in_specs=[IN_VMEM] * 2,
+        out_specs=IN_VMEM,
+        compiler_params=pltpu.CompilerParams(vmem_limit_bytes=4 * MIB),
+        cost_estimate=pl.CostEstimate(flops=1 << 34, bytes_accessed=32 * MIB, transcendentals=0),
+    )(a, b)
+
+
+def final_kernel(kept, up_own, from_x, other, m_y, m_xy, out):
     _, z_low, y, _, _ = place()
     line = pl.ds(out.shape[0], RANK)
     m = (kept[line, :] + from_x[line, :]) + (m_y[:RANK, :] + m_xy[...])
@@ -339,7 +327,7 @@
                 if side == 0:
                     base = kept[span, cols] + from_x[span, cols]
                 else:
-                    base = from_y[span, cols] + from_xy[span, cols]
+                    base = other[span, cols]
                 picked = jnp.zeros((RANK, LANES), BF16)
                 for i in range(UP_TILES):
                     picked = jnp.where(j == i, up[b * UP_TILES + i], picked)
@@ -356,7 +344,7 @@
         out_shape=jax.ShapeDtypeStruct((rows, 2 * HALF), BF16),
         in_specs=[IN_VMEM] * len(args),
         out_specs=IN_VMEM,
-        compiler_params=pltpu.CompilerParams(vmem_limit_bytes=VMEM),
+        compiler_params=pltpu.CompilerParams(vmem_limit_bytes=6 * MIB),
     )(*args)
 
 
@@ -377,29 +365,31 @@
         w0, down = value.T, down.transpose(0, 2, 1).reshape(RANK, features)
         theirs = over_tensor(hidden, 2)
         w2, w1 = over_tensor(w0, 8), over_tensor(w0, 4)
-        v0 = over_tensor(w0, 1)
-        v0, down = tie((v0, down))
-        d0, ids = prep(chosen, live, down, up[0])
-        v1, w0 = over_tensor(w1, 1), over_tensor(v0, 1)
-        w2, v1, w0, d0, ids = tie((w2, v1, w0, d0, ids))
-        w3, v2 = over_tensor(w2, 4), over_tensor(w2, 1)
+        half = lax.dynamic_slice_in_dim(up[0], lax.axis_index("adapter") * 2 * HALF, 2 * HALF, 1)
+        d0 = jnp.concatenate([down, half], axis=1)
+        ids = jnp.concatenate([chosen, live])
+        w2, w1, w0 = tie((w2, w1, w0))
+        w3 = over_tensor(w2, 4)
+        w = jnp.concatenate([w0, w1, w2])
+        v = over_tensor(w, 1)
+        w3, d0, ids = tie((w3, d0, ids))
+        v3 = over_tensor(w3, 1)
         d2, d1 = over_tensor(d0, 8), over_tensor(d0, 4)
-        w3, v2, d2, d1, ids, theirs = tie((w3, v2, d2, d1, ids, theirs))
-        v3 = over_tensor(w3, 1)
+        ids_p = over_tensor(ids, 2)
+        d2, v3 = tie((d2, v3))
         d3 = over_tensor(d2, 4)
-        ids_p = over_tensor(ids, 2)
-        wide = (w0, v0, w1, v1, w2, v2, w3, v3)
-        theirs, ids_p = tie((theirs, ids_p))
-        to_y, to_xy = their_sums(theirs, wide)
-        to_y, to_xy, d3 = tie((to_y, to_xy, d3))
-        from_y, from_xy = over_tensor(to_y, 2), over_both(to_xy)
-        narrow = jnp.concatenate([d0, d1, d2, d3])
-        narrow_v = over_tensor(narrow, 1)
+        early = jnp.concatenate([d0, d1, d2])
+        wide = (w, w3, v, v3)
+        to_y, to_xy = base_sums(theirs, wide)
+        to_y, to_xy, ids_p = tie((to_y, to_xy, ids_p))
+        other = add(over_tensor(to_y, 2), over_both(to_xy))
+        _, d3 = tie((to_y, d3))
+        narrow = (early, over_tensor(early, 1), d3, over_tensor(d3, 1))
         kept, to_x, m_y, m_xy, up_own = own_sums(
-            (ids, ids_p), hidden, theirs, (narrow, narrow_v), wide
+            (ids, ids_p), hidden, theirs, narrow, wide
         )
         from_x, m_y, m_xy = over_adapter(to_x, 1), over_tensor(m_y, 2), over_both(m_xy)
-        return final(kept, up_own, from_x, from_y, from_xy, m_y, m_xy)
+        return final(kept, up_own, from_x, other, m_y, m_xy)
 
     return body
 

time: 76.6 us -> 75.6 us (0.987)
  starting transfers between devices: 17.8 us -> 23 us
  waiting for transfers between devices: 47.3 us -> 42.4 us
  Pallas kernels: 10.2 us -> 6.94 us
  other arithmetic: 0 us -> 1.66 us
    ppermute x16 -> x14, waiting for transfers between devices: 46.4 us -> 38.4 us  [over_tensor(): lax.ppermute(array, 'tensor', perm=[(i, i ^ flip) for i in range(tensor)])]
    ppermute x16 -> x14, starting transfers between devices: 12.5 us -> 19.7 us  [over_tensor(): lax.ppermute(array, 'tensor', perm=[(i, i ^ flip) for i in range(tensor)])]
    ppermute x2, waiting for transfers between devices: 0.9 us -> 3.98 us  [over_both(): return lax.ppermute(array, ('tensor', 'adapter'), perm=pairs)]
    pallas_call x2, Pallas kernels: 4.34 us -> 1.86 us  [the longest x1 1.83 us: base_sums(): pl.pallas_call(base_kernel, out_shape=[jax.ShapeDtypeStruct((rows, HALF),...]
    ppermute x2, starting transfers between devices: 4.74 us -> 2.68 us  [over_both(): return lax.ppermute(array, ('tensor', 'adapter'), perm=pairs)]
    concatenate x0 -> x2, other arithmetic: none -> 1.66 us  [the longest x1 0.91 us: body(): d0 = jnp.concatenate([down, half], axis=1)]
  transfers between devices with their start and end apart: 19 -> 17, of which waited for: 8 -> 8; matrix products, arithmetic and copies ran while one was open for 1% -> 4% of each run, Pallas kernels for 12% -> 8%
where the time goes in v4:
time: 75.6 us; the launch traced here: 75.3 us
  waiting for transfers between devices  42.4 us (56%)
  starting transfers between devices  23 us (30%)
  Pallas kernels  6.94 us (9%)
  other arithmetic  1.66 us (2%)
  local copies, waits for them, and re-layouts  1.19 us (2%)
    ppermute x14, waiting for transfers between devices, over_tensor(): lax.ppermute(array, 'tensor', perm=[(i, i ^ flip) for i in range(tensor)])  38.4 us
    ppermute x14, starting transfers between devices, over_tensor(): lax.ppermute(array, 'tensor', perm=[(i, i ^ flip) for i in range(tensor)])  19.7 us
    pallas_call x1, Pallas kernels, own_sums(): pl.pallas_call(own_kernel, out_shape=[jax.ShapeDtypeStruct(s, F32) for s...  4.08 us
    ppermute x2, waiting for transfers between devices, over_both(): return lax.ppermute(array, ('tensor', 'adapter'), perm=pairs)  3.98 us
    ppermute x2, starting transfers between devices, over_both(): return lax.ppermute(array, ('tensor', 'adapter'), perm=pairs)  2.68 us
    pallas_call x1, Pallas kernels, base_sums(): pl.pallas_call(base_kernel, out_shape=[jax.ShapeDtypeStruct((rows, HALF),...  1.83 us
  transfers between devices with their start and end apart: 17, of which 8 were waited for; matrix products, arithmetic and copies ran while one was open for 4% of the time, Pallas kernels for 8%

profile of v4, /device:TPU:0, one launch (start us, length us, event | category | flops | bytes accessed | tf_op | source)
XLA Modules:
  0.0 75.3 jit_solution(1827320623194142294)
XLA Ops:
  0.0 4.0 %collective-permute-start = (bf16[64,4096]{1,0:T(8,128)(2,1)}, bf16[64,4096]{1,0:T(8,128)(2,1)S(1)}, u32[]{:S(2)}, u32[]{:S(2)}) collective-permute-start(bf16[64,4096]{1,0:T(8,128)(2,1)} %bitcast.6), channel_id=1, source_target_pairs={{0,16},{2,18},{4,20},{6,22},{8,24},{10,26},{12,28},{14,30},{16,0},... | collective-permute-start | bytes 1572872 | tf_op jit(solution)/shard_map/ppermute | solution.py:21
  4.0 1.6 %collective-permute-start.1 = (bf16[64,4096]{1,0:T(8,128)(2,1)}, bf16[64,4096]{1,0:T(8,128)(2,1)S(1)}, u32[]{:S(2)}, u32[]{:S(2)}) collective-permute-start(bf16[64,4096]{1,0:T(8,128)(2,1)} %bitcast.7), channel_id=1, source_target_pairs={{0,8},{2,10},{4,12},{6,14},{8,0},{10,2},{12,4},{14,6},{16,24},{18,... | collective-permute-start | bytes 1572872 | tf_op jit(solution)/shard_map/ppermute | solution.py:21
  5.6 1.5 %collective-permute-start.3 = (bf16[256,4096]{1,0:T(8,128)(2,1)}, bf16[256,4096]{1,0:T(8,128)(2,1)S(1)}, u32[]{:S(2)}, u32[]{:S(2)}) collective-permute-start(bf16[256,4096]{1,0:T(8,128)(2,1)} %mine.1), channel_id=1, source_target_pairs={{0,4},{2,6},{4,0},{6,2},{8,12},{10,14},{12,8},{14,10},{16,20},{18,... | collective-permute-start | bytes 6291464 | tf_op jit(solution)/shard_map/ppermute | solution.py:21
  7.1 0.7 pad_add_fusion.ids
  7.9 0.9 %pad_maximum_fusion = bf16[16,4608]{1,0:T(8,128)(2,1)S(1)} fusion(bf16[16,512]{1,0:T(8,128)(2,1)S(1)} %dynamic-slice_bitcast_fusion, bf16[16,4096]{1,0:T(8,128)(2,1)} %bitcast.9), kind=kLoop, calls=%fused_computation | loop fusion | flops 294912 | bytes 294912 | tf_op jit(solution)/shard_map/concatenate | solution.py:369
  8.8 18.7 %collective-permute-done = bf16[64,4096]{1,0:T(8,128)(2,1)S(1)} collective-permute-done((bf16[64,4096]{1,0:T(8,128)(2,1)}, bf16[64,4096]{1,0:T(8,128)(2,1)S(1)}, u32[]{:S(2)}, u32[]{:S(2)}) %collective-permute-start) | collective-permute-done | bytes 524320 | tf_op jit(solution)/shard_map/ppermute | solution.py:21
  27.5 0.2 collective-permute-done.1
  27.7 1.5 %collective-permute-start.2 = (bf16[64,4096]{1,0:T(8,128)(2,1)S(1)}, bf16[64,4096]{1,0:T(8,128)(2,1)S(1)}, u32[]{:S(2)}, u32[]{:S(2)}) collective-permute-start(bf16[64,4096]{1,0:T(8,128)(2,1)S(1)} %collective-permute-done), channel_id=1, source_target_pairs={{0,8},{2,10},{4,12},{6,14},{8,0},{10,2},{12,4},{14,6},{16,24},{18,... | collective-permute-start | bytes 1572872 | tf_op jit(solution)/shard_map/ppermute | solution.py:21
  29.2 1.1 %constant_dynamic-update-slice_fusion.2 = bf16[192,4096]{1,0:T(8,128)(2,1)S(1)} fusion(bf16[64,4096]{1,0:T(8,128)(2,1)} %bitcast.8), kind=kLoop, calls=%fused_computation.4 | loop fusion | bytes 1048576
  30.4 0.1 collective-permute-start.4
  30.4 10.1 %collective-permute-done.2.refs_1_ = bf16[64,4096]{1,0:T(8,128)(2,1)S(1)} collective-permute-done((bf16[64,4096]{1,0:T(8,128)(2,1)S(1)}, bf16[64,4096]{1,0:T(8,128)(2,1)S(1)}, u32[]{:S(2)}, u32[]{:S(2)}) %collective-permute-start.2) | collective-permute-done | bytes 524320 | tf_op jit(solution)/shard_map/ppermute | solution.py:21
  40.6 3.0 %collective-permute-start.5 = (bf16[16,4608]{1,0:T(8,128)(2,1)S(1)}, bf16[16,4608]{1,0:T(8,128)(2,1)S(1)}, u32[]{:S(2)}, u32[]{:S(2)}) collective-permute-start(bf16[16,4608]{1,0:T(8,128)(2,1)S(1)} %pad_maximum_fusion), channel_id=1, source_target_pairs={{0,16},{2,18},{4,20},{6,22},{8,24},{10,26},{12,28},{14,30},{16,0},... | collective-permute-start | bytes 442376 | tf_op jit(solution)/shard_map/ppermute | solution.py:21
  43.6 1.7 %collective-permute-start.8 = (bf16[16,4608]{1,0:T(8,128)(2,1)S(1)}, bf16[16,4608]{1,0:T(8,128)(2,1)S(1)}, u32[]{:S(2)}, u32[]{:S(2)}) collective-permute-start(bf16[16,4608]{1,0:T(8,128)(2,1)S(1)} %pad_maximum_fusion), channel_id=1, source_target_pairs={{0,8},{2,10},{4,12},{6,14},{8,0},{10,2},{12,4},{14,6},{16,24},{18,... | collective-permute-start | bytes 442376 | tf_op jit(solution)/shard_map/ppermute | solution.py:21
  45.4 0.1 collective-permute-start.6
  45.5 5.3 %collective-permute-done.8 = bf16[16,4608]{1,0:T(8,128)(2,1)S(1)} collective-permute-done((bf16[16,4608]{1,0:T(8,128)(2,1)S(1)}, bf16[16,4608]{1,0:T(8,128)(2,1)S(1)}, u32[]{:S(2)}, u32[]{:S(2)}) %collective-permute-start.8) | collective-permute-done | bytes 147488 | tf_op jit(solution)/shard_map/ppermute | solution.py:21
  50.8 0.0 collective-permute-done.5
  50.8 0.0 copy-start.1
  50.8 0.1 collective-permute-start.9
  50.9 1.3 %collective-permute-start.10 = (bf16[16,4608]{1,0:T(8,128)(2,1)S(1)}, bf16[16,4608]{1,0:T(8,128)(2,1)S(1)}, u32[]{:S(2)}, u32[]{:S(2)}) collective-permute-start(bf16[16,4608]{1,0:T(8,128)(2,1)S(1)} %collective-permute-done.5), channel_id=1, source_target_pairs={{0,8},{2,10},{4,12},{6,14},{8,0},{10,2},{12,4},{14,6},{16,24},{18,... | collective-permute-start | bytes 442376 | tf_op jit(solution)/shard_map/ppermute | solution.py:21
  52.3 1.5 %collective-permute-start.7 = (s32[4]{0:T(128)S(1)}, s32[4]{0:T(128)S(1)}, u32[]{:S(2)}, u32[]{:S(2)}) collective-permute-start(s32[4]{0:T(128)S(1)} %pad_add_fusion.ids), channel_id=1, source_target_pairs={{0,4},{2,6},{4,0},{6,2},{8,12},{10,14},{12,8},{14,10},{16,20},{18,... | collective-permute-start | bytes 56 | tf_op jit(solution)/shard_map/ppermute | solution.py:21
  53.8 1.8 %shard_map.64 = (f32[256,256]{1,0:T(8,128)S(1)}, f32[256,256]{1,0:T(8,128)S(1)}) custom-call(bf16[256,4096]{1,0:T(8,128)(2,1)S(1)} %collective-permute-done.3.rows_ref.theirs, bf16[192,4096]{1,0:T(8,128)(2,1)S(1)} %constant_dynamic-update-slice_fusion.refs_0_, bf16[64,4096]{1,0:T(8,128)(2,1)S(1)} %collective-permute-done.2.refs_1_, ...), custom_call_target="tpu_custom_call" | custom-call | tf_op jit(solution)/shard_map/pallas_call | solution.py:188
  55.6 0.2 collective-permute-done.7.ids_p
  55.8 1.5 %collective-permute-start.13 = (f32[256,256]{1,0:T(8,128)S(1)}, f32[256,256]{1,0:T(8,128)S(1)}, u32[]{:S(2)}, u32[]{:S(2)}) collective-permute-start(f32[256,256]{1,0:T(8,128)S(1)} %get-tuple-element.35), channel_id=1, source_target_pairs={{0,4},{2,6},{4,0},{6,2},{8,12},{10,14},{12,8},{14,10},{16,20},{18,... | collective-permute-start | bytes 786440 | tf_op jit(solution)/shard_map/ppermute | solution.py:21
  57.3 1.4 %collective-permute-start.14 = (f32[256,256]{1,0:T(8,128)S(1)}, f32[256,256]{1,0:T(8,128)S(1)}, u32[]{:S(2)}, u32[]{:S(2)}) collective-permute-start(f32[256,256]{1,0:T(8,128)S(1)} %get-tuple-element.40), channel_id=1, source_target_pairs={{0,5},{1,4},{2,7},{3,6},{4,1},{5,0},{6,3},{7,2},{8,13},{9,12},{10,... | collective-permute-start | bytes 786440 | tf_op jit(solution)/shard_map/ppermute | solution.py:361
  58.8 1.4 %collective-permute-done.11.refs_7_ = bf16[16,4608]{1,0:T(8,128)(2,1)S(1)} collective-permute-done((bf16[16,4608]{1,0:T(8,128)(2,1)S(1)}, bf16[16,4608]{1,0:T(8,128)(2,1)S(1)}, u32[]{:S(2)}, u32[]{:S(2)}) %collective-permute-start.11) | collective-permute-done | bytes 147488 | tf_op jit(solution)/shard_map/ppermute | solution.py:21
  60.2 4.1 %shard_map.65 = (f32[272,256]{1,0:T(8,128)S(1)}, f32[272,256]{1,0:T(8,128)S(1)}, f32[80,256]{1,0:T(8,128)S(1)}, f32[16,256]{1,0:T(8,128)S(1)}, bf16[2,16,512]{2,1,0:T(8,128)(2,1)S(1)}) custom-call(s32[4]{0:T(128)S(1)} %pad_add_fusion.ids, s32[4]{0:T(128)S(1)} %collective-permute-done.7.ids_p, bf16[256,4096]{1,0:T(8,128)(2,1)S(1)} %copy-done.1, ...), custom_call_target="tpu_custom_call" | custom-call | tf_op jit(solution)/shard_map/pallas_call | solution.py:274
  64.2 0.6 collective-permute-start.12
  64.8 1.7 %collective-permute-start.15 = (f32[80,256]{1,0:T(8,128)S(1)}, f32[80,256]{1,0:T(8,128)S(1)}, u32[]{:S(2)}, u32[]{:S(2)}) collective-permute-start(f32[80,256]{1,0:T(8,128)S(1)} %get-tuple-element.41), channel_id=1, source_target_pairs={{0,4},{2,6},{4,0},{6,2},{8,12},{10,14},{12,8},{14,10},{16,20},{18,... | collective-permute-start | bytes 245768 | tf_op jit(solution)/shard_map/ppermute | solution.py:21
  66.5 1.2 %collective-permute-start.16 = (f32[16,256]{1,0:T(8,128)S(1)}, f32[16,256]{1,0:T(8,128)S(1)}, u32[]{:S(2)}, u32[]{:S(2)}) collective-permute-start(f32[16,256]{1,0:T(8,128)S(1)} %get-tuple-element.42), channel_id=1, source_target_pairs={{0,5},{1,4},{2,7},{3,6},{4,1},{5,0},{6,3},{7,2},{8,13},{9,12},{10,... | collective-permute-start | bytes 49160 | tf_op jit(solution)/shard_map/ppermute | solution.py:361
  67.8 2.5 %collective-permute-done.13.a = f32[256,256]{1,0:T(8,128)S(1)} collective-permute-done((f32[256,256]{1,0:T(8,128)S(1)}, f32[256,256]{1,0:T(8,128)S(1)}, u32[]{:S(2)}, u32[]{:S(2)}) %collective-permute-start.13) | collective-permute-done | bytes 262176 | tf_op jit(solution)/shard_map/ppermute | solution.py:21
  70.3 4.0 %collective-permute-done.16.m_xy = f32[16,256]{1,0:T(8,128)S(1)} collective-permute-done((f32[16,256]{1,0:T(8,128)S(1)}, f32[16,256]{1,0:T(8,128)S(1)}, u32[]{:S(2)}, u32[]{:S(2)}) %collective-permute-start.16) | collective-permute-done | bytes 16416 | tf_op jit(solution)/shard_map/ppermute | solution.py:361
  74.3 1.0 %shard_map.67 = bf16[256,512]{1,0:T(8,128)(2,1)} custom-call(f32[272,256]{1,0:T(8,128)S(1)} %get-tuple-element.37.kept, bf16[2,16,512]{2,1,0:T(8,128)(2,1)S(1)} %get-tuple-element.38.up_own, f32[272,256]{1,0:T(8,128)S(1)} %collective-permute-done.12.from_x, f32[256,256]{1,0:T(8,128)S(1)} %shard_map.66.other, f32[80,256]{1,0:T(8,128)S(1)} %collective-permute-done.15.m_y, ...), custom_call_target="tpu_custom_call" | custom-call | tf_op jit(solution)/shard_map/pallas_call | solution.py:342
  (19 shorter events, 0.2 us)
Async XLA Ops:
  0.0 7.1 %copy-start = (bf16[1,16,1024]{2,1,0:T(8,128)(2,1)S(1)}, bf16[1,16,1024]{2,1,0:T(8,128)(2,1)}, u32[]{:S(2)}) copy-start(bf16[1,16,1024]{2,1,0:T(8,128)(2,1)} %param.9) | copy-start | bytes 98308
  0.0 27.5 %collective-permute-start = (bf16[64,4096]{1,0:T(8,128)(2,1)}, bf16[64,4096]{1,0:T(8,128)(2,1)S(1)}, u32[]{:S(2)}, u32[]{:S(2)}) collective-permute-start(bf16[64,4096]{1,0:T(8,128)(2,1)} %bitcast.6), channel_id=1, source_target_pairs={{0,16},{2,18},{4,20},{6,22},{8,24},{10,26},{12,28},{14,30},{16,0},... | collective-permute-start | bytes 1572872 | tf_op jit(solution)/shard_map/ppermute | solution.py:21
  4.0 23.7 %collective-permute-start.1 = (bf16[64,4096]{1,0:T(8,128)(2,1)}, bf16[64,4096]{1,0:T(8,128)(2,1)S(1)}, u32[]{:S(2)}, u32[]{:S(2)}) collective-permute-start(bf16[64,4096]{1,0:T(8,128)(2,1)} %bitcast.7), channel_id=1, source_target_pairs={{0,8},{2,10},{4,12},{6,14},{8,0},{10,2},{12,4},{14,6},{16,24},{18,... | collective-permute-start | bytes 1572872 | tf_op jit(solution)/shard_map/ppermute | solution.py:21
  5.6 48.2 %collective-permute-start.3 = (bf16[256,4096]{1,0:T(8,128)(2,1)}, bf16[256,4096]{1,0:T(8,128)(2,1)S(1)}, u32[]{:S(2)}, u32[]{:S(2)}) collective-permute-start(bf16[256,4096]{1,0:T(8,128)(2,1)} %mine.1), channel_id=1, source_target_pairs={{0,4},{2,6},{4,0},{6,2},{8,12},{10,14},{12,8},{14,10},{16,20},{18,... | collective-permute-start | bytes 6291464 | tf_op jit(solution)/shard_map/ppermute | solution.py:21
  27.7 12.9 %collective-permute-start.2 = (bf16[64,4096]{1,0:T(8,128)(2,1)S(1)}, bf16[64,4096]{1,0:T(8,128)(2,1)S(1)}, u32[]{:S(2)}, u32[]{:S(2)}) collective-permute-start(bf16[64,4096]{1,0:T(8,128)(2,1)S(1)} %collective-permute-done), channel_id=1, source_target_pairs={{0,8},{2,10},{4,12},{6,14},{8,0},{10,2},{12,4},{14,6},{16,24},{18,... | collective-permute-start | bytes 1572872 | tf_op jit(solution)/shard_map/ppermute | solution.py:21
  30.4 23.4 %collective-permute-start.4 = (bf16[192,4096]{1,0:T(8,128)(2,1)S(1)}, bf16[192,4096]{1,0:T(8,128)(2,1)S(1)}, u32[]{:S(2)}, u32[]{:S(2)}) collective-permute-start(bf16[192,4096]{1,0:T(8,128)(2,1)S(1)} %constant_dynamic-update-slice_fusion.refs_0_), channel_id=1, source_target_pairs={{0,2},{2,0},{4,6},{6,4},{8,10},{10,8},{12,14},{14,12},{16,18},{18,... | collective-permute-start | bytes 4718600 | tf_op jit(solution)/shard_map/ppermute | solution.py:21
  40.6 10.2 %collective-permute-start.5 = (bf16[16,4608]{1,0:T(8,128)(2,1)S(1)}, bf16[16,4608]{1,0:T(8,128)(2,1)S(1)}, u32[]{:S(2)}, u32[]{:S(2)}) collective-permute-start(bf16[16,4608]{1,0:T(8,128)(2,1)S(1)} %pad_maximum_fusion), channel_id=1, source_target_pairs={{0,16},{2,18},{4,20},{6,22},{8,24},{10,26},{12,28},{14,30},{16,0},... | collective-permute-start | bytes 442376 | tf_op jit(solution)/shard_map/ppermute | solution.py:21
  43.6 7.2 %collective-permute-start.8 = (bf16[16,4608]{1,0:T(8,128)(2,1)S(1)}, bf16[16,4608]{1,0:T(8,128)(2,1)S(1)}, u32[]{:S(2)}, u32[]{:S(2)}) collective-permute-start(bf16[16,4608]{1,0:T(8,128)(2,1)S(1)} %pad_maximum_fusion), channel_id=1, source_target_pairs={{0,8},{2,10},{4,12},{6,14},{8,0},{10,2},{12,4},{14,6},{16,24},{18,... | collective-permute-start | bytes 442376 | tf_op jit(solution)/shard_map/ppermute | solution.py:21
  45.4 5.4 %collective-permute-start.6 = (bf16[64,4096]{1,0:T(8,128)(2,1)S(1)}, bf16[64,4096]{1,0:T(8,128)(2,1)S(1)}, u32[]{:S(2)}, u32[]{:S(2)}) collective-permute-start(bf16[64,4096]{1,0:T(8,128)(2,1)S(1)} %collective-permute-done.2.refs_1_), channel_id=1, source_target_pairs={{0,2},{2,0},{4,6},{6,4},{8,10},{10,8},{12,14},{14,12},{16,18},{18,... | collective-permute-start | bytes 1572872 | tf_op jit(solution)/shard_map/ppermute | solution.py:21
  50.8 9.3 %copy-start.1 = (bf16[256,4096]{1,0:T(8,128)(2,1)S(1)}, bf16[256,4096]{1,0:T(8,128)(2,1)}, u32[]{:S(2)}) copy-start(bf16[256,4096]{1,0:T(8,128)(2,1)} %mine.1) | copy-start | bytes 6291460
  50.8 7.9 %collective-permute-start.9 = (bf16[48,4608]{1,0:T(8,128)(2,1)S(1)}, bf16[48,4608]{1,0:T(8,128)(2,1)S(1)}, u32[]{:S(2)}, u32[]{:S(2)}) collective-permute-start(bf16[48,4608]{1,0:T(8,128)(2,1)S(1)} %constant_dynamic-update-slice_fusion.3.refs_4_), channel_id=1, source_target_pairs={{0,2},{2,0},{4,6},{6,4},{8,10},{10,8},{12,14},{14,12},{16,18},{18,... | collective-permute-start | bytes 1327112 | tf_op jit(solution)/shard_map/ppermute | solution.py:21
  50.9 7.8 %collective-permute-start.10 = (bf16[16,4608]{1,0:T(8,128)(2,1)S(1)}, bf16[16,4608]{1,0:T(8,128)(2,1)S(1)}, u32[]{:S(2)}, u32[]{:S(2)}) collective-permute-start(bf16[16,4608]{1,0:T(8,128)(2,1)S(1)} %collective-permute-done.5), channel_id=1, source_target_pairs={{0,8},{2,10},{4,12},{6,14},{8,0},{10,2},{12,4},{14,6},{16,24},{18,... | collective-permute-start | bytes 442376 | tf_op jit(solution)/shard_map/ppermute | solution.py:21
  52.3 3.5 %collective-permute-start.7 = (s32[4]{0:T(128)S(1)}, s32[4]{0:T(128)S(1)}, u32[]{:S(2)}, u32[]{:S(2)}) collective-permute-start(s32[4]{0:T(128)S(1)} %pad_add_fusion.ids), channel_id=1, source_target_pairs={{0,4},{2,6},{4,0},{6,2},{8,12},{10,14},{12,8},{14,10},{16,20},{18,... | collective-permute-start | bytes 56 | tf_op jit(solution)/shard_map/ppermute | solution.py:21
  55.8 14.5 %collective-permute-start.13 = (f32[256,256]{1,0:T(8,128)S(1)}, f32[256,256]{1,0:T(8,128)S(1)}, u32[]{:S(2)}, u32[]{:S(2)}) collective-permute-start(f32[256,256]{1,0:T(8,128)S(1)} %get-tuple-element.35), channel_id=1, source_target_pairs={{0,4},{2,6},{4,0},{6,2},{8,12},{10,14},{12,8},{14,10},{16,20},{18,... | collective-permute-start | bytes 786440 | tf_op jit(solution)/shard_map/ppermute | solution.py:21
  57.3 13.0 %collective-permute-start.14 = (f32[256,256]{1,0:T(8,128)S(1)}, f32[256,256]{1,0:T(8,128)S(1)}, u32[]{:S(2)}, u32[]{:S(2)}) collective-permute-start(f32[256,256]{1,0:T(8,128)S(1)} %get-tuple-element.40), channel_id=1, source_target_pairs={{0,5},{1,4},{2,7},{3,6},{4,1},{5,0},{6,3},{7,2},{8,13},{9,12},{10,... | collective-permute-start | bytes 786440 | tf_op jit(solution)/shard_map/ppermute | solution.py:361
  58.8 1.4 %collective-permute-start.11 = (bf16[16,4608]{1,0:T(8,128)(2,1)S(1)}, bf16[16,4608]{1,0:T(8,128)(2,1)S(1)}, u32[]{:S(2)}, u32[]{:S(2)}) collective-permute-start(bf16[16,4608]{1,0:T(8,128)(2,1)S(1)} %collective-permute-done.10.refs_6_), channel_id=1, source_target_pairs={{0,2},{2,0},{4,6},{6,4},{8,10},{10,8},{12,14},{14,12},{16,18},{18,... | collective-permute-start | bytes 442376 | tf_op jit(solution)/shard_map/ppermute | solution.py:21
  64.2 10.1 %collective-permute-start.12 = (f32[272,256]{1,0:T(8,128)S(1)}, f32[272,256]{1,0:T(8,128)S(1)}, u32[]{:S(2)}, u32[]{:S(2)}) collective-permute-start(f32[272,256]{1,0:T(8,128)S(1)} %get-tuple-element.39), channel_id=1, source_target_pairs={{0,1},{1,0},{2,3},{3,2},{4,5},{5,4},{6,7},{7,6},{8,9},{9,8},{10,11... | collective-permute-start | bytes 835592 | tf_op jit(solution)/shard_map/ppermute | solution.py:24
  64.8 9.5 %collective-permute-start.15 = (f32[80,256]{1,0:T(8,128)S(1)}, f32[80,256]{1,0:T(8,128)S(1)}, u32[]{:S(2)}, u32[]{:S(2)}) collective-permute-start(f32[80,256]{1,0:T(8,128)S(1)} %get-tuple-element.41), channel_id=1, source_target_pairs={{0,4},{2,6},{4,0},{6,2},{8,12},{10,14},{12,8},{14,10},{16,20},{18,... | collective-permute-start | bytes 245768 | tf_op jit(solution)/shard_map/ppermute | solution.py:21
  66.5 7.8 %collective-permute-start.16 = (f32[16,256]{1,0:T(8,128)S(1)}, f32[16,256]{1,0:T(8,128)S(1)}, u32[]{:S(2)}, u32[]{:S(2)}) collective-permute-start(f32[16,256]{1,0:T(8,128)S(1)} %get-tuple-element.42), channel_id=1, source_target_pairs={{0,5},{1,4},{2,7},{3,6},{4,1},{5,0},{6,3},{7,2},{8,13},{9,12},{10,... | collective-permute-start | bytes 49160 | tf_op jit(solution)/shard_map/ppermute | solution.py:361

commit v5 on v4

--- a/solution.py
+++ b/solution.py
@@ -202,7 +202,7 @@
 
 
 def own_kernel(ids, ids_p, mine, theirs, *refs):
-    wide, narrow, refs = refs[:4], refs[4:8], refs[8:]
+    wide, narrow, refs = refs[:4], refs[4:6], refs[6:]
     kept, to_x, m_y, m_xy, up_own, w, d, up, rows_in, w_sem, d_sem, r_sem = refs
     t = lax.axis_index("tensor")
     rows, features = mine.shape
@@ -231,12 +231,10 @@
             up[b] = jnp.zeros_like(up[b])
 
         for i, ref in enumerate(narrow):
-            last = i >= 2
-
-            @pl.when(here & (other == i % 2) & ((unit == DEPTH - 1) == last))
+
+            @pl.when(here & (other == i))
             def _():
-                line = 0 if last else pl.multiple_of(unit * RANK, RANK)
-                for c in fetch(b, ref, line):
+                for c in fetch(b, ref, pl.multiple_of(unit * RANK, RANK)):
                     c.start()
 
     for c in copies:
@@ -247,7 +245,7 @@
 
         @pl.when(here)
         def _():
-            for c in fetch(b, narrow[2], 0):
+            for c in fetch(b, narrow[0], 0):
                 c.wait()
 
     for b in range(4):
@@ -368,23 +366,21 @@
         half = lax.dynamic_slice_in_dim(up[0], lax.axis_index("adapter") * 2 * HALF, 2 * HALF, 1)
         d0 = jnp.concatenate([down, half], axis=1)
         ids = jnp.concatenate([chosen, live])
-        w2, w1, w0 = tie((w2, w1, w0))
+        w2, w1, w0, d0 = tie((w2, w1, w0, d0))
         w3 = over_tensor(w2, 4)
+        d2, d1 = over_tensor(d0, 8), over_tensor(d0, 4)
         w = jnp.concatenate([w0, w1, w2])
         v = over_tensor(w, 1)
-        w3, d0, ids = tie((w3, d0, ids))
-        v3 = over_tensor(w3, 1)
-        d2, d1 = over_tensor(d0, 8), over_tensor(d0, 4)
-        ids_p = over_tensor(ids, 2)
-        d2, v3 = tie((d2, v3))
-        d3 = over_tensor(d2, 4)
-        early = jnp.concatenate([d0, d1, d2])
+        d3 = over_tensor(d0, 12)
+        w3, d2, d1, d3, ids = tie((w3, d2, d1, d3, ids))
+        v3, ids_p = over_tensor(w3, 1), over_tensor(ids, 2)
+        narrow = jnp.concatenate([d0, d1, d2, d3])
+        narrow_v = over_tensor(narrow, 1)
         wide = (w, w3, v, v3)
         to_y, to_xy = base_sums(theirs, wide)
         to_y, to_xy, ids_p = tie((to_y, to_xy, ids_p))
         other = add(over_tensor(to_y, 2), over_both(to_xy))
-        _, d3 = tie((to_y, d3))
-        narrow = (early, over_tensor(early, 1), d3, over_tensor(d3, 1))
+        narrow = (narrow, narrow_v)
         kept, to_x, m_y, m_xy, up_own = own_sums(
             (ids, ids_p), hidden, theirs, narrow, wide
         )

time: 75.6 us -> 73.1 us (0.967)
  starting transfers between devices: 23 us -> 20.8 us
    ppermute x14 -> x13, starting transfers between devices: 19.7 us -> 17.5 us  [over_tensor(): lax.ppermute(array, 'tensor', perm=[(i, i ^ flip) for i in range(tensor)])]
    ppermute x2, waiting for transfers between devices: 3.98 us -> 1.97 us  [over_both(): return lax.ppermute(array, ('tensor', 'adapter'), perm=pairs)]
    ppermute x14 -> x13, waiting for transfers between devices: 38.4 us -> 40.3 us  [over_tensor(): lax.ppermute(array, 'tensor', perm=[(i, i ^ flip) for i in range(tensor)])]
  transfers between devices with their start and end apart: 17 -> 16, of which waited for: 8 -> 8; matrix products, arithmetic and copies ran while one was open for 4% -> 4% of each run, Pallas kernels for 8% -> 8%
where the time goes in v5:
time: 73.1 us; the launch traced here: 72.9 us
  waiting for transfers between devices  42.3 us (58%)
  starting transfers between devices  20.8 us (28%)
  Pallas kernels  6.9 us (9%)
  other arithmetic  1.66 us (2%)
  local copies, waits for them, and re-layouts  1.21 us (2%)
    ppermute x13, waiting for transfers between devices, over_tensor(): lax.ppermute(array, 'tensor', perm=[(i, i ^ flip) for i in range(tensor)])  40.3 us
    ppermute x13, starting transfers between devices, over_tensor(): lax.ppermute(array, 'tensor', perm=[(i, i ^ flip) for i in range(tensor)])  17.5 us
    pallas_call x1, Pallas kernels, own_sums(): pl.pallas_call(own_kernel, out_shape=[jax.ShapeDtypeStruct(s, F32) for s...  4.04 us
    ppermute x2, starting transfers between devices, over_both(): return lax.ppermute(array, ('tensor', 'adapter'), perm=pairs)  2.68 us
    ppermute x2, waiting for transfers between devices, over_both(): return lax.ppermute(array, ('tensor', 'adapter'), perm=pairs)  1.97 us
    pallas_call x1, Pallas kernels, base_sums(): pl.pallas_call(base_kernel, out_shape=[jax.ShapeDtypeStruct((rows, HALF),...  1.84 us
  transfers between devices with their start and end apart: 16, of which 8 were waited for; matrix products, arithmetic and copies ran while one was open for 4% of the time, Pallas kernels for 8%

profile of v5, /device:TPU:0, one launch (start us, length us, event | category | flops | bytes accessed | tf_op | source)
XLA Modules:
  0.0 72.9 jit_solution(17342668332205412344)
XLA Ops:
  0.0 4.0 %collective-permute-start = (bf16[64,4096]{1,0:T(8,128)(2,1)}, bf16[64,4096]{1,0:T(8,128)(2,1)S(1)}, u32[]{:S(2)}, u32[]{:S(2)}) collective-permute-start(bf16[64,4096]{1,0:T(8,128)(2,1)} %bitcast.6), channel_id=1, source_target_pairs={{0,16},{2,18},{4,20},{6,22},{8,24},{10,26},{12,28},{14,30},{16,0},... | collective-permute-start | bytes 1572872 | tf_op jit(solution)/shard_map/ppermute | solution.py:21
  4.0 1.6 %collective-permute-start.1 = (bf16[64,4096]{1,0:T(8,128)(2,1)}, bf16[64,4096]{1,0:T(8,128)(2,1)S(1)}, u32[]{:S(2)}, u32[]{:S(2)}) collective-permute-start(bf16[64,4096]{1,0:T(8,128)(2,1)} %bitcast.7), channel_id=1, source_target_pairs={{0,8},{2,10},{4,12},{6,14},{8,0},{10,2},{12,4},{14,6},{16,24},{18,... | collective-permute-start | bytes 1572872 | tf_op jit(solution)/shard_map/ppermute | solution.py:21
  5.6 1.5 %collective-permute-start.6 = (bf16[256,4096]{1,0:T(8,128)(2,1)}, bf16[256,4096]{1,0:T(8,128)(2,1)S(1)}, u32[]{:S(2)}, u32[]{:S(2)}) collective-permute-start(bf16[256,4096]{1,0:T(8,128)(2,1)} %mine.1), channel_id=1, source_target_pairs={{0,4},{2,6},{4,0},{6,2},{8,12},{10,14},{12,8},{14,10},{16,20},{18,... | collective-permute-start | bytes 6291464 | tf_op jit(solution)/shard_map/ppermute | solution.py:21
  7.1 0.7 %pad_add_fusion.ids = s32[4]{0:T(128)S(1)} fusion(s32[2]{0:T(128)} %param.11, s32[2]{0:T(128)} %param.10), kind=kLoop, calls=%fused_computation.9 | loop fusion | flops 4 | bytes 32 | tf_op jit(solution)/shard_map/concatenate | solution.py:368
  7.9 0.9 %pad_maximum_fusion = bf16[16,4608]{1,0:T(8,128)(2,1)S(1)} fusion(bf16[16,512]{1,0:T(8,128)(2,1)S(1)} %dynamic-slice_bitcast_fusion, bf16[16,4096]{1,0:T(8,128)(2,1)} %bitcast.9), kind=kLoop, calls=%fused_computation | loop fusion | flops 294912 | bytes 294912 | tf_op jit(solution)/shard_map/concatenate | solution.py:367
  8.8 18.7 %collective-permute-done = bf16[64,4096]{1,0:T(8,128)(2,1)S(1)} collective-permute-done((bf16[64,4096]{1,0:T(8,128)(2,1)}, bf16[64,4096]{1,0:T(8,128)(2,1)S(1)}, u32[]{:S(2)}, u32[]{:S(2)}) %collective-permute-start) | collective-permute-done | bytes 524320 | tf_op jit(solution)/shard_map/ppermute | solution.py:21
  27.5 0.2 collective-permute-done.1
  27.7 1.4 %collective-permute-start.3 = (bf16[16,4608]{1,0:T(8,128)(2,1)S(1)}, bf16[16,4608]{1,0:T(8,128)(2,1)S(1)}, u32[]{:S(2)}, u32[]{:S(2)}) collective-permute-start(bf16[16,4608]{1,0:T(8,128)(2,1)S(1)} %pad_maximum_fusion), channel_id=1, source_target_pairs={{0,16},{2,18},{4,20},{6,22},{8,24},{10,26},{12,28},{14,30},{16,0},... | collective-permute-start | bytes 442376 | tf_op jit(solution)/shard_map/ppermute | solution.py:21
  29.1 2.4 %collective-permute-start.4 = (bf16[16,4608]{1,0:T(8,128)(2,1)S(1)}, bf16[16,4608]{1,0:T(8,128)(2,1)S(1)}, u32[]{:S(2)}, u32[]{:S(2)}) collective-permute-start(bf16[16,4608]{1,0:T(8,128)(2,1)S(1)} %pad_maximum_fusion), channel_id=1, source_target_pairs={{0,8},{2,10},{4,12},{6,14},{8,0},{10,2},{12,4},{14,6},{16,24},{18,... | collective-permute-start | bytes 442376 | tf_op jit(solution)/shard_map/ppermute | solution.py:21
  31.5 0.6 collective-permute-start.5
  32.1 0.7 collective-permute-start.2
  32.8 1.1 %constant_dynamic-update-slice_fusion.2 = bf16[192,4096]{1,0:T(8,128)(2,1)S(1)} fusion(bf16[64,4096]{1,0:T(8,128)(2,1)} %bitcast.8), kind=kLoop, calls=%fused_computation.3 | loop fusion | bytes 1048576
  33.9 5.3 %collective-permute-done.3 = bf16[16,4608]{1,0:T(8,128)(2,1)S(1)} collective-permute-done((bf16[16,4608]{1,0:T(8,128)(2,1)S(1)}, bf16[16,4608]{1,0:T(8,128)(2,1)S(1)}, u32[]{:S(2)}, u32[]{:S(2)}) %collective-permute-start.3) | collective-permute-done | bytes 147488 | tf_op jit(solution)/shard_map/ppermute | solution.py:21
  39.2 0.0 collective-permute-start.7
  39.2 0.0 collective-permute-done.4
  39.3 3.4 %collective-permute-done.5 = bf16[16,4608]{1,0:T(8,128)(2,1)S(1)} collective-permute-done((bf16[16,4608]{1,0:T(8,128)(2,1)S(1)}, bf16[16,4608]{1,0:T(8,128)(2,1)S(1)}, u32[]{:S(2)}, u32[]{:S(2)}) %collective-permute-start.5) | collective-permute-done | bytes 147488 | tf_op jit(solution)/shard_map/ppermute | solution.py:21
  42.6 8.6 %collective-permute-done.2.refs_1_ = bf16[64,4096]{1,0:T(8,128)(2,1)S(1)} collective-permute-done((bf16[64,4096]{1,0:T(8,128)(2,1)S(1)}, bf16[64,4096]{1,0:T(8,128)(2,1)S(1)}, u32[]{:S(2)}, u32[]{:S(2)}) %collective-permute-start.2) | collective-permute-done | bytes 524320 | tf_op jit(solution)/shard_map/ppermute | solution.py:21
  51.3 0.0 copy-start.1
  51.3 0.6 collective-permute-start.10
  51.9 1.5 %collective-permute-start.9 = (s32[4]{0:T(128)S(1)}, s32[4]{0:T(128)S(1)}, u32[]{:S(2)}, u32[]{:S(2)}) collective-permute-start(s32[4]{0:T(128)S(1)} %pad_add_fusion.ids), channel_id=1, source_target_pairs={{0,4},{2,6},{4,0},{6,2},{8,12},{10,14},{12,8},{14,10},{16,20},{18,... | collective-permute-start | bytes 56 | tf_op jit(solution)/shard_map/ppermute | solution.py:21
  53.4 0.0 collective-permute-done.8.refs_3_
  53.4 1.8 %shard_map.64 = (f32[256,256]{1,0:T(8,128)S(1)}, f32[256,256]{1,0:T(8,128)S(1)}) custom-call(bf16[256,4096]{1,0:T(8,128)(2,1)S(1)} %collective-permute-done.6.rows_ref.theirs, bf16[192,4096]{1,0:T(8,128)(2,1)S(1)} %constant_dynamic-update-slice_fusion.refs_0_, bf16[64,4096]{1,0:T(8,128)(2,1)S(1)} %collective-permute-done.2.refs_1_, ...), custom_call_target="tpu_custom_call" | custom-call | tf_op jit(solution)/shard_map/pallas_call | solution.py:188
  55.3 0.2 collective-permute-done.9.ids_p
  55.4 1.5 %collective-permute-start.12 = (f32[256,256]{1,0:T(8,128)S(1)}, f32[256,256]{1,0:T(8,128)S(1)}, u32[]{:S(2)}, u32[]{:S(2)}) collective-permute-start(f32[256,256]{1,0:T(8,128)S(1)} %get-tuple-element.39), channel_id=1, source_target_pairs={{0,4},{2,6},{4,0},{6,2},{8,12},{10,14},{12,8},{14,10},{16,20},{18,... | collective-permute-start | bytes 786440 | tf_op jit(solution)/shard_map/ppermute | solution.py:21
  56.9 1.4 %collective-permute-start.13 = (f32[256,256]{1,0:T(8,128)S(1)}, f32[256,256]{1,0:T(8,128)S(1)}, u32[]{:S(2)}, u32[]{:S(2)}) collective-permute-start(f32[256,256]{1,0:T(8,128)S(1)} %get-tuple-element.40), channel_id=1, source_target_pairs={{0,5},{1,4},{2,7},{3,6},{4,1},{5,0},{6,3},{7,2},{8,13},{9,12},{10,... | collective-permute-start | bytes 786440 | tf_op jit(solution)/shard_map/ppermute | solution.py:359
  58.4 4.0 %shard_map.65 = (f32[272,256]{1,0:T(8,128)S(1)}, f32[272,256]{1,0:T(8,128)S(1)}, f32[80,256]{1,0:T(8,128)S(1)}, f32[16,256]{1,0:T(8,128)S(1)}, bf16[2,16,512]{2,1,0:T(8,128)(2,1)S(1)}) custom-call(s32[4]{0:T(128)S(1)} %pad_add_fusion.ids, s32[4]{0:T(128)S(1)} %collective-permute-done.9.ids_p, bf16[256,4096]{1,0:T(8,128)(2,1)S(1)} %copy-done.1, ...), custom_call_target="tpu_custom_call" | custom-call | tf_op jit(solution)/shard_map/pallas_call | solution.py:272
  62.4 0.6 collective-permute-start.11
  63.0 1.7 %collective-permute-start.14 = (f32[80,256]{1,0:T(8,128)S(1)}, f32[80,256]{1,0:T(8,128)S(1)}, u32[]{:S(2)}, u32[]{:S(2)}) collective-permute-start(f32[80,256]{1,0:T(8,128)S(1)} %get-tuple-element.41), channel_id=1, source_target_pairs={{0,4},{2,6},{4,0},{6,2},{8,12},{10,14},{12,8},{14,10},{16,20},{18,... | collective-permute-start | bytes 245768 | tf_op jit(solution)/shard_map/ppermute | solution.py:21
  64.7 1.3 %collective-permute-start.15 = (f32[16,256]{1,0:T(8,128)S(1)}, f32[16,256]{1,0:T(8,128)S(1)}, u32[]{:S(2)}, u32[]{:S(2)}) collective-permute-start(f32[16,256]{1,0:T(8,128)S(1)} %get-tuple-element.42), channel_id=1, source_target_pairs={{0,5},{1,4},{2,7},{3,6},{4,1},{5,0},{6,3},{7,2},{8,13},{9,12},{10,... | collective-permute-start | bytes 49160 | tf_op jit(solution)/shard_map/ppermute | solution.py:359
  66.0 3.9 %collective-permute-done.12.a = f32[256,256]{1,0:T(8,128)S(1)} collective-permute-done((f32[256,256]{1,0:T(8,128)S(1)}, f32[256,256]{1,0:T(8,128)S(1)}, u32[]{:S(2)}, u32[]{:S(2)}) %collective-permute-start.12) | collective-permute-done | bytes 262176 | tf_op jit(solution)/shard_map/ppermute | solution.py:21
  70.0 2.0 %collective-permute-done.15.m_xy = f32[16,256]{1,0:T(8,128)S(1)} collective-permute-done((f32[16,256]{1,0:T(8,128)S(1)}, f32[16,256]{1,0:T(8,128)S(1)}, u32[]{:S(2)}, u32[]{:S(2)}) %collective-permute-start.15) | collective-permute-done | bytes 16416 | tf_op jit(solution)/shard_map/ppermute | solution.py:359
  71.9 1.0 %shard_map.67 = bf16[256,512]{1,0:T(8,128)(2,1)} custom-call(f32[272,256]{1,0:T(8,128)S(1)} %get-tuple-element.36.kept, bf16[2,16,512]{2,1,0:T(8,128)(2,1)S(1)} %get-tuple-element.37.up_own, f32[272,256]{1,0:T(8,128)S(1)} %collective-permute-done.11.from_x, f32[256,256]{1,0:T(8,128)S(1)} %shard_map.66.other, f32[80,256]{1,0:T(8,128)S(1)} %collective-permute-done.14.m_y, ...), custom_call_target="tpu_custom_call" | custom-call | tf_op jit(solution)/shard_map/pallas_call | solution.py:340
  (18 shorter events, 0.2 us)
Async XLA Ops:
  0.0 7.1 %copy-start = (bf16[1,16,1024]{2,1,0:T(8,128)(2,1)S(1)}, bf16[1,16,1024]{2,1,0:T(8,128)(2,1)}, u32[]{:S(2)}) copy-start(bf16[1,16,1024]{2,1,0:T(8,128)(2,1)} %param.9) | copy-start | bytes 98308
  0.0 27.5 %collective-permute-start = (bf16[64,4096]{1,0:T(8,128)(2,1)}, bf16[64,4096]{1,0:T(8,128)(2,1)S(1)}, u32[]{:S(2)}, u32[]{:S(2)}) collective-permute-start(bf16[64,4096]{1,0:T(8,128)(2,1)} %bitcast.6), channel_id=1, source_target_pairs={{0,16},{2,18},{4,20},{6,22},{8,24},{10,26},{12,28},{14,30},{16,0},... | collective-permute-start | bytes 1572872 | tf_op jit(solution)/shard_map/ppermute | solution.py:21
  4.0 23.7 %collective-permute-start.1 = (bf16[64,4096]{1,0:T(8,128)(2,1)}, bf16[64,4096]{1,0:T(8,128)(2,1)S(1)}, u32[]{:S(2)}, u32[]{:S(2)}) collective-permute-start(bf16[64,4096]{1,0:T(8,128)(2,1)} %bitcast.7), channel_id=1, source_target_pairs={{0,8},{2,10},{4,12},{6,14},{8,0},{10,2},{12,4},{14,6},{16,24},{18,... | collective-permute-start | bytes 1572872 | tf_op jit(solution)/shard_map/ppermute | solution.py:21
  5.6 47.8 %collective-permute-start.6 = (bf16[256,4096]{1,0:T(8,128)(2,1)}, bf16[256,4096]{1,0:T(8,128)(2,1)S(1)}, u32[]{:S(2)}, u32[]{:S(2)}) collective-permute-start(bf16[256,4096]{1,0:T(8,128)(2,1)} %mine.1), channel_id=1, source_target_pairs={{0,4},{2,6},{4,0},{6,2},{8,12},{10,14},{12,8},{14,10},{16,20},{18,... | collective-permute-start | bytes 6291464 | tf_op jit(solution)/shard_map/ppermute | solution.py:21
  27.7 11.5 %collective-permute-start.3 = (bf16[16,4608]{1,0:T(8,128)(2,1)S(1)}, bf16[16,4608]{1,0:T(8,128)(2,1)S(1)}, u32[]{:S(2)}, u32[]{:S(2)}) collective-permute-start(bf16[16,4608]{1,0:T(8,128)(2,1)S(1)} %pad_maximum_fusion), channel_id=1, source_target_pairs={{0,16},{2,18},{4,20},{6,22},{8,24},{10,26},{12,28},{14,30},{16,0},... | collective-permute-start | bytes 442376 | tf_op jit(solution)/shard_map/ppermute | solution.py:21
  29.1 10.2 %collective-permute-start.4 = (bf16[16,4608]{1,0:T(8,128)(2,1)S(1)}, bf16[16,4608]{1,0:T(8,128)(2,1)S(1)}, u32[]{:S(2)}, u32[]{:S(2)}) collective-permute-start(bf16[16,4608]{1,0:T(8,128)(2,1)S(1)} %pad_maximum_fusion), channel_id=1, source_target_pairs={{0,8},{2,10},{4,12},{6,14},{8,0},{10,2},{12,4},{14,6},{16,24},{18,... | collective-permute-start | bytes 442376 | tf_op jit(solution)/shard_map/ppermute | solution.py:21
  31.5 11.1 %collective-permute-start.5 = (bf16[16,4608]{1,0:T(8,128)(2,1)S(1)}, bf16[16,4608]{1,0:T(8,128)(2,1)S(1)}, u32[]{:S(2)}, u32[]{:S(2)}) collective-permute-start(bf16[16,4608]{1,0:T(8,128)(2,1)S(1)} %pad_maximum_fusion), channel_id=1, source_target_pairs={{0,24},{2,26},{4,28},{6,30},{8,16},{10,18},{12,20},{14,22},{16,8},... | collective-permute-start | bytes 442376 | tf_op jit(solution)/shard_map/ppermute | solution.py:21
  32.1 19.1 %collective-permute-start.2 = (bf16[64,4096]{1,0:T(8,128)(2,1)S(1)}, bf16[64,4096]{1,0:T(8,128)(2,1)S(1)}, u32[]{:S(2)}, u32[]{:S(2)}) collective-permute-start(bf16[64,4096]{1,0:T(8,128)(2,1)S(1)} %collective-permute-done), channel_id=1, source_target_pairs={{0,8},{2,10},{4,12},{6,14},{8,0},{10,2},{12,4},{14,6},{16,24},{18,... | collective-permute-start | bytes 1572872 | tf_op jit(solution)/shard_map/ppermute | solution.py:21
  39.2 14.2 %collective-permute-start.7 = (bf16[192,4096]{1,0:T(8,128)(2,1)S(1)}, bf16[192,4096]{1,0:T(8,128)(2,1)S(1)}, u32[]{:S(2)}, u32[]{:S(2)}) collective-permute-start(bf16[192,4096]{1,0:T(8,128)(2,1)S(1)} %constant_dynamic-update-slice_fusion.refs_0_), channel_id=1, source_target_pairs={{0,2},{2,0},{4,6},{6,4},{8,10},{10,8},{12,14},{14,12},{16,18},{18,... | collective-permute-start | bytes 4718600 | tf_op jit(solution)/shard_map/ppermute | solution.py:21
  51.2 2.2 %collective-permute-start.8 = (bf16[64,4096]{1,0:T(8,128)(2,1)S(1)}, bf16[64,4096]{1,0:T(8,128)(2,1)S(1)}, u32[]{:S(2)}, u32[]{:S(2)}) collective-permute-start(bf16[64,4096]{1,0:T(8,128)(2,1)S(1)} %collective-permute-done.2.refs_1_), channel_id=1, source_target_pairs={{0,2},{2,0},{4,6},{6,4},{8,10},{10,8},{12,14},{14,12},{16,18},{18,... | collective-permute-start | bytes 1572872 | tf_op jit(solution)/shard_map/ppermute | solution.py:21
  51.3 7.1 %copy-start.1 = (bf16[256,4096]{1,0:T(8,128)(2,1)S(1)}, bf16[256,4096]{1,0:T(8,128)(2,1)}, u32[]{:S(2)}) copy-start(bf16[256,4096]{1,0:T(8,128)(2,1)} %mine.1) | copy-start | bytes 6291460
  51.3 7.1 %collective-permute-start.10 = (bf16[64,4608]{1,0:T(8,128)(2,1)S(1)}, bf16[64,4608]{1,0:T(8,128)(2,1)S(1)}, u32[]{:S(2)}, u32[]{:S(2)}) collective-permute-start(bf16[64,4608]{1,0:T(8,128)(2,1)S(1)} %constant_dynamic-update-slice_fusion.3.refs_4_), channel_id=1, source_target_pairs={{0,2},{2,0},{4,6},{6,4},{8,10},{10,8},{12,14},{14,12},{16,18},{18,... | collective-permute-start | bytes 1769480 | tf_op jit(solution)/shard_map/ppermute | solution.py:21
  51.9 3.5 %collective-permute-start.9 = (s32[4]{0:T(128)S(1)}, s32[4]{0:T(128)S(1)}, u32[]{:S(2)}, u32[]{:S(2)}) collective-permute-start(s32[4]{0:T(128)S(1)} %pad_add_fusion.ids), channel_id=1, source_target_pairs={{0,4},{2,6},{4,0},{6,2},{8,12},{10,14},{12,8},{14,10},{16,20},{18,... | collective-permute-start | bytes 56 | tf_op jit(solution)/shard_map/ppermute | solution.py:21
  55.4 14.5 %collective-permute-start.12 = (f32[256,256]{1,0:T(8,128)S(1)}, f32[256,256]{1,0:T(8,128)S(1)}, u32[]{:S(2)}, u32[]{:S(2)}) collective-permute-start(f32[256,256]{1,0:T(8,128)S(1)} %get-tuple-element.39), channel_id=1, source_target_pairs={{0,4},{2,6},{4,0},{6,2},{8,12},{10,14},{12,8},{14,10},{16,20},{18,... | collective-permute-start | bytes 786440 | tf_op jit(solution)/shard_map/ppermute | solution.py:21
  56.9 13.0 %collective-permute-start.13 = (f32[256,256]{1,0:T(8,128)S(1)}, f32[256,256]{1,0:T(8,128)S(1)}, u32[]{:S(2)}, u32[]{:S(2)}) collective-permute-start(f32[256,256]{1,0:T(8,128)S(1)} %get-tuple-element.40), channel_id=1, source_target_pairs={{0,5},{1,4},{2,7},{3,6},{4,1},{5,0},{6,3},{7,2},{8,13},{9,12},{10,... | collective-permute-start | bytes 786440 | tf_op jit(solution)/shard_map/ppermute | solution.py:359
  62.4 9.5 %collective-permute-start.11 = (f32[272,256]{1,0:T(8,128)S(1)}, f32[272,256]{1,0:T(8,128)S(1)}, u32[]{:S(2)}, u32[]{:S(2)}) collective-permute-start(f32[272,256]{1,0:T(8,128)S(1)} %get-tuple-element.38), channel_id=1, source_target_pairs={{0,1},{1,0},{2,3},{3,2},{4,5},{5,4},{6,7},{7,6},{8,9},{9,8},{10,11... | collective-permute-start | bytes 835592 | tf_op jit(solution)/shard_map/ppermute | solution.py:24
  63.0 8.9 %collective-permute-start.14 = (f32[80,256]{1,0:T(8,128)S(1)}, f32[80,256]{1,0:T(8,128)S(1)}, u32[]{:S(2)}, u32[]{:S(2)}) collective-permute-start(f32[80,256]{1,0:T(8,128)S(1)} %get-tuple-element.41), channel_id=1, source_target_pairs={{0,4},{2,6},{4,0},{6,2},{8,12},{10,14},{12,8},{14,10},{16,20},{18,... | collective-permute-start | bytes 245768 | tf_op jit(solution)/shard_map/ppermute | solution.py:21
  64.7 7.2 %collective-permute-start.15 = (f32[16,256]{1,0:T(8,128)S(1)}, f32[16,256]{1,0:T(8,128)S(1)}, u32[]{:S(2)}, u32[]{:S(2)}) collective-permute-start(f32[16,256]{1,0:T(8,128)S(1)} %get-tuple-element.42), channel_id=1, source_target_pairs={{0,5},{1,4},{2,7},{3,6},{4,1},{5,0},{6,3},{7,2},{8,13},{9,12},{10,... | collective-permute-start | bytes 49160 | tf_op jit(solution)/shard_map/ppermute | solution.py:359

commit v6 on v5

--- a/solution.py
+++ b/solution.py
@@ -174,9 +174,9 @@
     return copies
 
 
-def base_kernel(rows_ref, *refs):
-    wide, (kept, sent, w, rows_in, w_sem, r_sem) = refs[:4], refs[4:]
-    copies = load_rows((rows_ref,), rows_in, r_sem) + gather_wide(wide, w, w_sem)
+def base_kernel(rows_in, *refs):
+    wide, (kept, sent, w, w_sem) = refs[:4], refs[4:]
+    copies = gather_wide(wide, w, w_sem)
     for c in copies:
         c.wait()
     sent[...] = dot_nt(rows_in[...], w[pl.ds(HALF, HALF), :])
@@ -188,13 +188,11 @@
     return pl.pallas_call(
         base_kernel,
         out_shape=[jax.ShapeDtypeStruct((rows, HALF), F32)] * 2,
-        in_specs=[IN_ANY] * (1 + len(wide)),
+        in_specs=[IN_VMEM] + [IN_ANY] * len(wide),
         out_specs=[IN_VMEM] * 2,
         scratch_shapes=[
             pltpu.VMEM((2 * HALF, features), BF16),
-            pltpu.VMEM((rows, features), BF16),
             pltpu.SemaphoreType.DMA((2 * DEPTH,)),
-            pltpu.SemaphoreType.DMA((1,)),
         ],
         compiler_params=pltpu.CompilerParams(vmem_limit_bytes=9 * MIB),
         cost_estimate=pl.CostEstimate(flops=0, bytes_accessed=0, transcendentals=0),
@@ -258,21 +256,22 @@
             to_x[pl.ds(rows, RANK), at] = m
             up_own[b] = up[b]
         else:
-            m_y[:RANK, at] = m
             m_xy[:, at] = m
+            for i in range(3):
+                part = m.astype(BF16)
+                m_y[pl.ds(i * RANK, RANK), at] = part
+                m = m - part.astype(F32)
             for i in range(2):
-                m_y[pl.ds((b % 2 * 2 + i + 1) * RANK, RANK), :] = up[
-                    b, :, pl.ds(i * HALF, HALF)
-                ].astype(F32)
+                m_y[pl.ds((b % 2 * 2 + i + 3) * RANK, RANK), :] = up[b, :, pl.ds(i * HALF, HALF)]
 
 
 def own_sums(scalars, mine, theirs, narrow, wide):
     rows, features = mine.shape
-    shapes = [(rows + RANK, HALF), (rows + RANK, HALF), (5 * RANK, HALF), (RANK, HALF)]
+    part, m_xy = ((rows + RANK, HALF), F32), ((RANK, HALF), F32)
+    shapes = [part, part, ((7 * RANK, HALF), BF16), m_xy, ((2, RANK, 2 * HALF), BF16)]
     return pl.pallas_call(
         own_kernel,
-        out_shape=[jax.ShapeDtypeStruct(s, F32) for s in shapes]
-        + [jax.ShapeDtypeStruct((2, RANK, 2 * HALF), BF16)],
+        out_shape=[jax.ShapeDtypeStruct(*s) for s in shapes],
         in_specs=[IN_SMEM] * 2 + [IN_ANY] * (2 + len(wide) + len(narrow)),
         out_specs=[IN_VMEM] * 5,
         scratch_shapes=[
@@ -307,13 +306,14 @@
 def final_kernel(kept, up_own, from_x, other, m_y, m_xy, out):
     _, z_low, y, _, _ = place()
     line = pl.ds(out.shape[0], RANK)
-    m = (kept[line, :] + from_x[line, :]) + (m_y[:RANK, :] + m_xy[...])
+    parts = [m_y[pl.ds(i * RANK, RANK), :].astype(F32) for i in range(3)]
+    m = (kept[line, :] + from_x[line, :]) + ((parts[0] + parts[1]) + parts[2] + m_xy[...])
     mid = m.T.astype(BF16)
     up = []
     for b in range(2):
         for i in range(UP_TILES):
-            lines = pl.ds((b * 2 + i // 2 + 1) * RANK, RANK)
-            got = m_y[lines, pl.ds(i % 2 * LANES, LANES)].astype(BF16)
+            lines = pl.ds((b * 2 + i // 2 + 3) * RANK, RANK)
+            got = m_y[lines, pl.ds(i % 2 * LANES, LANES)]
             up.append(up_own[b, :, pl.ds(i * LANES, LANES)] + got)
     for tile in range(2):
         cols = pl.ds(tile * LANES, LANES)
@@ -372,7 +372,7 @@
         w = jnp.concatenate([w0, w1, w2])
         v = over_tensor(w, 1)
         d3 = over_tensor(d0, 12)
-        w3, d2, d1, d3, ids = tie((w3, d2, d1, d3, ids))
+        d1, d2, d3, w3, ids = tie((d1, d2, d3, w3, ids))
         v3, ids_p = over_tensor(w3, 1), over_tensor(ids, 2)
         narrow = jnp.concatenate([d0, d1, d2, d3])
         narrow_v = over_tensor(narrow, 1)

time: 73.1 us -> 72.2 us (0.988)
  waiting for transfers between devices: 42.3 us -> 41.2 us
    ppermute x13, waiting for transfers between devices: 40.3 us -> 38.9 us  [over_tensor(): lax.ppermute(array, 'tensor', perm=[(i, i ^ flip) for i in range(tensor)])]
where the time goes in v6:
time: 72.2 us; the launch traced here: 72 us
  waiting for transfers between devices  41.2 us (57%)
  starting transfers between devices  20.9 us (29%)
  Pallas kernels  6.94 us (10%)
  other arithmetic  1.66 us (2%)
  local copies, waits for them, and re-layouts  1.21 us (2%)
    ppermute x13, waiting for transfers between devices, over_tensor(): lax.ppermute(array, 'tensor', perm=[(i, i ^ flip) for i in range(tensor)])  38.9 us
    ppermute x13, starting transfers between devices, over_tensor(): lax.ppermute(array, 'tensor', perm=[(i, i ^ flip) for i in range(tensor)])  17.3 us
    pallas_call x1, Pallas kernels, own_sums(): pl.pallas_call(own_kernel, out_shape=[jax.ShapeDtypeStruct(*s) for s in s...  4.23 us
    ppermute x2, starting transfers between devices, over_both(): return lax.ppermute(array, ('tensor', 'adapter'), perm=pairs)  3.05 us
    ppermute x2, waiting for transfers between devices, over_both(): return lax.ppermute(array, ('tensor', 'adapter'), perm=pairs)  2.29 us
    pallas_call x1, Pallas kernels, base_sums(): pl.pallas_call(base_kernel, out_shape=[jax.ShapeDtypeStruct((rows, HALF),...  1.68 us
  transfers between devices with their start and end apart: 16, of which 8 were waited for; matrix products, arithmetic and copies ran while one was open for 4% of the time, Pallas kernels for 8%

profile of v6, /device:TPU:0, one launch (start us, length us, event | category | flops | bytes accessed | tf_op | source)
XLA Modules:
  0.0 72.0 jit_solution(9742563679162583450)
XLA Ops:
  0.0 4.0 %collective-permute-start = (bf16[64,4096]{1,0:T(8,128)(2,1)}, bf16[64,4096]{1,0:T(8,128)(2,1)S(1)}, u32[]{:S(2)}, u32[]{:S(2)}) collective-permute-start(bf16[64,4096]{1,0:T(8,128)(2,1)} %bitcast.6), channel_id=1, source_target_pairs={{0,16},{2,18},{4,20},{6,22},{8,24},{10,26},{12,28},{14,30},{16,0},... | collective-permute-start | bytes 1572872 | tf_op jit(solution)/shard_map/ppermute | solution.py:21
  4.0 1.6 %collective-permute-start.1 = (bf16[64,4096]{1,0:T(8,128)(2,1)}, bf16[64,4096]{1,0:T(8,128)(2,1)S(1)}, u32[]{:S(2)}, u32[]{:S(2)}) collective-permute-start(bf16[64,4096]{1,0:T(8,128)(2,1)} %bitcast.7), channel_id=1, source_target_pairs={{0,8},{2,10},{4,12},{6,14},{8,0},{10,2},{12,4},{14,6},{16,24},{18,... | collective-permute-start | bytes 1572872 | tf_op jit(solution)/shard_map/ppermute | solution.py:21
  5.6 1.5 %collective-permute-start.6 = (bf16[256,4096]{1,0:T(8,128)(2,1)}, bf16[256,4096]{1,0:T(8,128)(2,1)S(1)}, u32[]{:S(2)}, u32[]{:S(2)}) collective-permute-start(bf16[256,4096]{1,0:T(8,128)(2,1)} %mine.1), channel_id=1, source_target_pairs={{0,4},{2,6},{4,0},{6,2},{8,12},{10,14},{12,8},{14,10},{16,20},{18,... | collective-permute-start | bytes 6291464 | tf_op jit(solution)/shard_map/ppermute | solution.py:21
  7.1 0.7 %pad_add_fusion.ids = s32[4]{0:T(128)S(1)} fusion(s32[2]{0:T(128)} %param.11, s32[2]{0:T(128)} %param.10), kind=kLoop, calls=%fused_computation.9 | loop fusion | flops 4 | bytes 32 | tf_op jit(solution)/shard_map/concatenate | solution.py:368
  7.9 0.9 %pad_maximum_fusion = bf16[16,4608]{1,0:T(8,128)(2,1)S(1)} fusion(bf16[16,512]{1,0:T(8,128)(2,1)S(1)} %dynamic-slice_bitcast_fusion, bf16[16,4096]{1,0:T(8,128)(2,1)} %bitcast.9), kind=kLoop, calls=%fused_computation | loop fusion | flops 294912 | bytes 294912 | tf_op jit(solution)/shard_map/concatenate | solution.py:367
  8.8 18.7 %collective-permute-done = bf16[64,4096]{1,0:T(8,128)(2,1)S(1)} collective-permute-done((bf16[64,4096]{1,0:T(8,128)(2,1)}, bf16[64,4096]{1,0:T(8,128)(2,1)S(1)}, u32[]{:S(2)}, u32[]{:S(2)}) %collective-permute-start) | collective-permute-done | bytes 524320 | tf_op jit(solution)/shard_map/ppermute | solution.py:21
  27.5 0.2 collective-permute-done.1
  27.7 1.5 %collective-permute-start.2 = (bf16[16,4608]{1,0:T(8,128)(2,1)S(1)}, bf16[16,4608]{1,0:T(8,128)(2,1)S(1)}, u32[]{:S(2)}, u32[]{:S(2)}) collective-permute-start(bf16[16,4608]{1,0:T(8,128)(2,1)S(1)} %pad_maximum_fusion), channel_id=1, source_target_pairs={{0,8},{2,10},{4,12},{6,14},{8,0},{10,2},{12,4},{14,6},{16,24},{18,... | collective-permute-start | bytes 442376 | tf_op jit(solution)/shard_map/ppermute | solution.py:21
  29.2 2.3 %collective-permute-start.3 = (bf16[16,4608]{1,0:T(8,128)(2,1)S(1)}, bf16[16,4608]{1,0:T(8,128)(2,1)S(1)}, u32[]{:S(2)}, u32[]{:S(2)}) collective-permute-start(bf16[16,4608]{1,0:T(8,128)(2,1)S(1)} %pad_maximum_fusion), channel_id=1, source_target_pairs={{0,16},{2,18},{4,20},{6,22},{8,24},{10,26},{12,28},{14,30},{16,0},... | collective-permute-start | bytes 442376 | tf_op jit(solution)/shard_map/ppermute | solution.py:21
  31.5 0.6 collective-permute-start.4
  32.1 0.7 collective-permute-start.5
  32.8 1.1 %constant_dynamic-update-slice_fusion.2 = bf16[192,4096]{1,0:T(8,128)(2,1)S(1)} fusion(bf16[64,4096]{1,0:T(8,128)(2,1)} %bitcast.8), kind=kLoop, calls=%fused_computation.3 | loop fusion | bytes 1048576
  33.9 1.7 %collective-permute-done.2 = bf16[16,4608]{1,0:T(8,128)(2,1)S(1)} collective-permute-done((bf16[16,4608]{1,0:T(8,128)(2,1)S(1)}, bf16[16,4608]{1,0:T(8,128)(2,1)S(1)}, u32[]{:S(2)}, u32[]{:S(2)}) %collective-permute-start.2) | collective-permute-done | bytes 147488 | tf_op jit(solution)/shard_map/ppermute | solution.py:21
  35.6 0.0 collective-permute-start.7
  35.7 7.6 %collective-permute-done.3 = bf16[16,4608]{1,0:T(8,128)(2,1)S(1)} collective-permute-done((bf16[16,4608]{1,0:T(8,128)(2,1)S(1)}, bf16[16,4608]{1,0:T(8,128)(2,1)S(1)}, u32[]{:S(2)}, u32[]{:S(2)}) %collective-permute-start.3) | collective-permute-done | bytes 147488 | tf_op jit(solution)/shard_map/ppermute | solution.py:21
  43.2 7.2 %collective-permute-done.5.refs_1_ = bf16[64,4096]{1,0:T(8,128)(2,1)S(1)} collective-permute-done((bf16[64,4096]{1,0:T(8,128)(2,1)S(1)}, bf16[64,4096]{1,0:T(8,128)(2,1)S(1)}, u32[]{:S(2)}, u32[]{:S(2)}) %collective-permute-start.5) | collective-permute-done | bytes 524320 | tf_op jit(solution)/shard_map/ppermute | solution.py:21
  50.4 0.0 collective-permute-start.8
  50.5 0.0 copy-start.1
  50.5 0.6 collective-permute-start.10
  51.0 1.6 %collective-permute-start.9 = (s32[4]{0:T(128)S(1)}, s32[4]{0:T(128)S(1)}, u32[]{:S(2)}, u32[]{:S(2)}) collective-permute-start(s32[4]{0:T(128)S(1)} %pad_add_fusion.ids), channel_id=1, source_target_pairs={{0,4},{2,6},{4,0},{6,2},{8,12},{10,14},{12,8},{14,10},{16,20},{18,... | collective-permute-start | bytes 56 | tf_op jit(solution)/shard_map/ppermute | solution.py:21
  52.6 0.0 collective-permute-done.6.rows_in.theirs
  52.6 1.7 %shard_map.64 = (f32[256,256]{1,0:T(8,128)S(1)}, f32[256,256]{1,0:T(8,128)S(1)}) custom-call(bf16[256,4096]{1,0:T(8,128)(2,1)S(1)} %collective-permute-done.6.rows_in.theirs, bf16[192,4096]{1,0:T(8,128)(2,1)S(1)} %constant_dynamic-update-slice_fusion.refs_0_, bf16[64,4096]{1,0:T(8,128)(2,1)S(1)} %collective-permute-done.5.refs_1_, ...), custom_call_target="tpu_custom_call" | custom-call | tf_op jit(solution)/shard_map/pallas_call | solution.py:188
  54.3 0.3 collective-permute-done.9.ids_p
  54.6 1.6 %collective-permute-start.12 = (f32[256,256]{1,0:T(8,128)S(1)}, f32[256,256]{1,0:T(8,128)S(1)}, u32[]{:S(2)}, u32[]{:S(2)}) collective-permute-start(f32[256,256]{1,0:T(8,128)S(1)} %get-tuple-element.39), channel_id=1, source_target_pairs={{0,4},{2,6},{4,0},{6,2},{8,12},{10,14},{12,8},{14,10},{16,20},{18,... | collective-permute-start | bytes 786440 | tf_op jit(solution)/shard_map/ppermute | solution.py:21
  56.2 1.4 %collective-permute-start.13 = (f32[256,256]{1,0:T(8,128)S(1)}, f32[256,256]{1,0:T(8,128)S(1)}, u32[]{:S(2)}, u32[]{:S(2)}) collective-permute-start(f32[256,256]{1,0:T(8,128)S(1)} %get-tuple-element.40), channel_id=1, source_target_pairs={{0,5},{1,4},{2,7},{3,6},{4,1},{5,0},{6,3},{7,2},{8,13},{9,12},{10,... | collective-permute-start | bytes 786440 | tf_op jit(solution)/shard_map/ppermute | solution.py:359
  57.6 4.2 %shard_map.65 = (f32[272,256]{1,0:T(8,128)S(1)}, f32[272,256]{1,0:T(8,128)S(1)}, bf16[112,256]{1,0:T(8,128)(2,1)S(1)}, f32[16,256]{1,0:T(8,128)S(1)}, bf16[2,16,512]{2,1,0:T(8,128)(2,1)S(1)}) custom-call(s32[4]{0:T(128)S(1)} %pad_add_fusion.ids, s32[4]{0:T(128)S(1)} %collective-permute-done.9.ids_p, bf16[256,4096]{1,0:T(8,128)(2,1)S(1)} %copy-done.1, ...), custom_call_target="tpu_custom_call" | custom-call | tf_op jit(solution)/shard_map/pallas_call | solution.py:272
  61.8 0.5 collective-permute-start.11
  62.4 1.4 %collective-permute-start.14 = (bf16[112,256]{1,0:T(8,128)(2,1)S(1)}, bf16[112,256]{1,0:T(8,128)(2,1)S(1)}, u32[]{:S(2)}, u32[]{:S(2)}) collective-permute-start(bf16[112,256]{1,0:T(8,128)(2,1)S(1)} %get-tuple-element.41), channel_id=1, source_target_pairs={{0,4},{2,6},{4,0},{6,2},{8,12},{10,14},{12,8},{14,10},{16,20},{18,... | collective-permute-start | bytes 172040 | tf_op jit(solution)/shard_map/ppermute | solution.py:21
  63.8 1.6 %collective-permute-start.15 = (f32[16,256]{1,0:T(8,128)S(1)}, f32[16,256]{1,0:T(8,128)S(1)}, u32[]{:S(2)}, u32[]{:S(2)}) collective-permute-start(f32[16,256]{1,0:T(8,128)S(1)} %get-tuple-element.42), channel_id=1, source_target_pairs={{0,5},{1,4},{2,7},{3,6},{4,1},{5,0},{6,3},{7,2},{8,13},{9,12},{10,... | collective-permute-start | bytes 49160 | tf_op jit(solution)/shard_map/ppermute | solution.py:359
  65.4 3.3 %collective-permute-done.12.a = f32[256,256]{1,0:T(8,128)S(1)} collective-permute-done((f32[256,256]{1,0:T(8,128)S(1)}, f32[256,256]{1,0:T(8,128)S(1)}, u32[]{:S(2)}, u32[]{:S(2)}) %collective-permute-start.12) | collective-permute-done | bytes 262176 | tf_op jit(solution)/shard_map/ppermute | solution.py:21
  68.7 2.3 %collective-permute-done.15.m_xy = f32[16,256]{1,0:T(8,128)S(1)} collective-permute-done((f32[16,256]{1,0:T(8,128)S(1)}, f32[16,256]{1,0:T(8,128)S(1)}, u32[]{:S(2)}, u32[]{:S(2)}) %collective-permute-start.15) | collective-permute-done | bytes 16416 | tf_op jit(solution)/shard_map/ppermute | solution.py:359
  71.0 1.0 %shard_map.67 = bf16[256,512]{1,0:T(8,128)(2,1)} custom-call(f32[272,256]{1,0:T(8,128)S(1)} %get-tuple-element.36.kept, bf16[2,16,512]{2,1,0:T(8,128)(2,1)S(1)} %get-tuple-element.37.up_own, f32[272,256]{1,0:T(8,128)S(1)} %collective-permute-done.11.from_x, f32[256,256]{1,0:T(8,128)S(1)} %shard_map.66.other, ...), custom_call_target="tpu_custom_call" | custom-call | tf_op jit(solution)/shard_map/pallas_call | solution.py:340
  (18 shorter events, 0.2 us)
Async XLA Ops:
  0.0 7.1 %copy-start = (bf16[1,16,1024]{2,1,0:T(8,128)(2,1)S(1)}, bf16[1,16,1024]{2,1,0:T(8,128)(2,1)}, u32[]{:S(2)}) copy-start(bf16[1,16,1024]{2,1,0:T(8,128)(2,1)} %param.9) | copy-start | bytes 98308
  0.0 27.5 %collective-permute-start = (bf16[64,4096]{1,0:T(8,128)(2,1)}, bf16[64,4096]{1,0:T(8,128)(2,1)S(1)}, u32[]{:S(2)}, u32[]{:S(2)}) collective-permute-start(bf16[64,4096]{1,0:T(8,128)(2,1)} %bitcast.6), channel_id=1, source_target_pairs={{0,16},{2,18},{4,20},{6,22},{8,24},{10,26},{12,28},{14,30},{16,0},... | collective-permute-start | bytes 1572872 | tf_op jit(solution)/shard_map/ppermute | solution.py:21
  4.0 23.7 %collective-permute-start.1 = (bf16[64,4096]{1,0:T(8,128)(2,1)}, bf16[64,4096]{1,0:T(8,128)(2,1)S(1)}, u32[]{:S(2)}, u32[]{:S(2)}) collective-permute-start(bf16[64,4096]{1,0:T(8,128)(2,1)} %bitcast.7), channel_id=1, source_target_pairs={{0,8},{2,10},{4,12},{6,14},{8,0},{10,2},{12,4},{14,6},{16,24},{18,... | collective-permute-start | bytes 1572872 | tf_op jit(solution)/shard_map/ppermute | solution.py:21
  5.6 47.0 %collective-permute-start.6 = (bf16[256,4096]{1,0:T(8,128)(2,1)}, bf16[256,4096]{1,0:T(8,128)(2,1)S(1)}, u32[]{:S(2)}, u32[]{:S(2)}) collective-permute-start(bf16[256,4096]{1,0:T(8,128)(2,1)} %mine.1), channel_id=1, source_target_pairs={{0,4},{2,6},{4,0},{6,2},{8,12},{10,14},{12,8},{14,10},{16,20},{18,... | collective-permute-start | bytes 6291464 | tf_op jit(solution)/shard_map/ppermute | solution.py:21
  27.7 7.9 %collective-permute-start.2 = (bf16[16,4608]{1,0:T(8,128)(2,1)S(1)}, bf16[16,4608]{1,0:T(8,128)(2,1)S(1)}, u32[]{:S(2)}, u32[]{:S(2)}) collective-permute-start(bf16[16,4608]{1,0:T(8,128)(2,1)S(1)} %pad_maximum_fusion), channel_id=1, source_target_pairs={{0,8},{2,10},{4,12},{6,14},{8,0},{10,2},{12,4},{14,6},{16,24},{18,... | collective-permute-start | bytes 442376 | tf_op jit(solution)/shard_map/ppermute | solution.py:21
  29.2 14.0 %collective-permute-start.3 = (bf16[16,4608]{1,0:T(8,128)(2,1)S(1)}, bf16[16,4608]{1,0:T(8,128)(2,1)S(1)}, u32[]{:S(2)}, u32[]{:S(2)}) collective-permute-start(bf16[16,4608]{1,0:T(8,128)(2,1)S(1)} %pad_maximum_fusion), channel_id=1, source_target_pairs={{0,16},{2,18},{4,20},{6,22},{8,24},{10,26},{12,28},{14,30},{16,0},... | collective-permute-start | bytes 442376 | tf_op jit(solution)/shard_map/ppermute | solution.py:21
  31.5 11.7 %collective-permute-start.4 = (bf16[16,4608]{1,0:T(8,128)(2,1)S(1)}, bf16[16,4608]{1,0:T(8,128)(2,1)S(1)}, u32[]{:S(2)}, u32[]{:S(2)}) collective-permute-start(bf16[16,4608]{1,0:T(8,128)(2,1)S(1)} %pad_maximum_fusion), channel_id=1, source_target_pairs={{0,24},{2,26},{4,28},{6,30},{8,16},{10,18},{12,20},{14,22},{16,8},... | collective-permute-start | bytes 442376 | tf_op jit(solution)/shard_map/ppermute | solution.py:21
  32.1 18.3 %collective-permute-start.5 = (bf16[64,4096]{1,0:T(8,128)(2,1)S(1)}, bf16[64,4096]{1,0:T(8,128)(2,1)S(1)}, u32[]{:S(2)}, u32[]{:S(2)}) collective-permute-start(bf16[64,4096]{1,0:T(8,128)(2,1)S(1)} %collective-permute-done), channel_id=1, source_target_pairs={{0,8},{2,10},{4,12},{6,14},{8,0},{10,2},{12,4},{14,6},{16,24},{18,... | collective-permute-start | bytes 1572872 | tf_op jit(solution)/shard_map/ppermute | solution.py:21
  35.6 17.0 %collective-permute-start.7 = (bf16[192,4096]{1,0:T(8,128)(2,1)S(1)}, bf16[192,4096]{1,0:T(8,128)(2,1)S(1)}, u32[]{:S(2)}, u32[]{:S(2)}) collective-permute-start(bf16[192,4096]{1,0:T(8,128)(2,1)S(1)} %constant_dynamic-update-slice_fusion.refs_0_), channel_id=1, source_target_pairs={{0,2},{2,0},{4,6},{6,4},{8,10},{10,8},{12,14},{14,12},{16,18},{18,... | collective-permute-start | bytes 4718600 | tf_op jit(solution)/shard_map/ppermute | solution.py:21
  50.4 2.2 %collective-permute-start.8 = (bf16[64,4096]{1,0:T(8,128)(2,1)S(1)}, bf16[64,4096]{1,0:T(8,128)(2,1)S(1)}, u32[]{:S(2)}, u32[]{:S(2)}) collective-permute-start(bf16[64,4096]{1,0:T(8,128)(2,1)S(1)} %collective-permute-done.5.refs_1_), channel_id=1, source_target_pairs={{0,2},{2,0},{4,6},{6,4},{8,10},{10,8},{12,14},{14,12},{16,18},{18,... | collective-permute-start | bytes 1572872 | tf_op jit(solution)/shard_map/ppermute | solution.py:21
  50.5 7.1 %copy-start.1 = (bf16[256,4096]{1,0:T(8,128)(2,1)S(1)}, bf16[256,4096]{1,0:T(8,128)(2,1)}, u32[]{:S(2)}) copy-start(bf16[256,4096]{1,0:T(8,128)(2,1)} %mine.1) | copy-start | bytes 6291460
  50.5 7.1 %collective-permute-start.10 = (bf16[64,4608]{1,0:T(8,128)(2,1)S(1)}, bf16[64,4608]{1,0:T(8,128)(2,1)S(1)}, u32[]{:S(2)}, u32[]{:S(2)}) collective-permute-start(bf16[64,4608]{1,0:T(8,128)(2,1)S(1)} %constant_dynamic-update-slice_fusion.3.refs_4_), channel_id=1, source_target_pairs={{0,2},{2,0},{4,6},{6,4},{8,10},{10,8},{12,14},{14,12},{16,18},{18,... | collective-permute-start | bytes 1769480 | tf_op jit(solution)/shard_map/ppermute | solution.py:21
  51.0 3.5 %collective-permute-start.9 = (s32[4]{0:T(128)S(1)}, s32[4]{0:T(128)S(1)}, u32[]{:S(2)}, u32[]{:S(2)}) collective-permute-start(s32[4]{0:T(128)S(1)} %pad_add_fusion.ids), channel_id=1, source_target_pairs={{0,4},{2,6},{4,0},{6,2},{8,12},{10,14},{12,8},{14,10},{16,20},{18,... | collective-permute-start | bytes 56 | tf_op jit(solution)/shard_map/ppermute | solution.py:21
  54.6 14.1 %collective-permute-start.12 = (f32[256,256]{1,0:T(8,128)S(1)}, f32[256,256]{1,0:T(8,128)S(1)}, u32[]{:S(2)}, u32[]{:S(2)}) collective-permute-start(f32[256,256]{1,0:T(8,128)S(1)} %get-tuple-element.39), channel_id=1, source_target_pairs={{0,4},{2,6},{4,0},{6,2},{8,12},{10,14},{12,8},{14,10},{16,20},{18,... | collective-permute-start | bytes 786440 | tf_op jit(solution)/shard_map/ppermute | solution.py:21
  56.2 12.5 %collective-permute-start.13 = (f32[256,256]{1,0:T(8,128)S(1)}, f32[256,256]{1,0:T(8,128)S(1)}, u32[]{:S(2)}, u32[]{:S(2)}) collective-permute-start(f32[256,256]{1,0:T(8,128)S(1)} %get-tuple-element.40), channel_id=1, source_target_pairs={{0,5},{1,4},{2,7},{3,6},{4,1},{5,0},{6,3},{7,2},{8,13},{9,12},{10,... | collective-permute-start | bytes 786440 | tf_op jit(solution)/shard_map/ppermute | solution.py:359
  61.8 9.1 %collective-permute-start.11 = (f32[272,256]{1,0:T(8,128)S(1)}, f32[272,256]{1,0:T(8,128)S(1)}, u32[]{:S(2)}, u32[]{:S(2)}) collective-permute-start(f32[272,256]{1,0:T(8,128)S(1)} %get-tuple-element.38), channel_id=1, source_target_pairs={{0,1},{1,0},{2,3},{3,2},{4,5},{5,4},{6,7},{7,6},{8,9},{9,8},{10,11... | collective-permute-start | bytes 835592 | tf_op jit(solution)/shard_map/ppermute | solution.py:24
  62.4 8.6 %collective-permute-start.14 = (bf16[112,256]{1,0:T(8,128)(2,1)S(1)}, bf16[112,256]{1,0:T(8,128)(2,1)S(1)}, u32[]{:S(2)}, u32[]{:S(2)}) collective-permute-start(bf16[112,256]{1,0:T(8,128)(2,1)S(1)} %get-tuple-element.41), channel_id=1, source_target_pairs={{0,4},{2,6},{4,0},{6,2},{8,12},{10,14},{12,8},{14,10},{16,20},{18,... | collective-permute-start | bytes 172040 | tf_op jit(solution)/shard_map/ppermute | solution.py:21
  63.8 7.2 %collective-permute-start.15 = (f32[16,256]{1,0:T(8,128)S(1)}, f32[16,256]{1,0:T(8,128)S(1)}, u32[]{:S(2)}, u32[]{:S(2)}) collective-permute-start(f32[16,256]{1,0:T(8,128)S(1)} %get-tuple-element.42), channel_id=1, source_target_pairs={{0,5},{1,4},{2,7},{3,6},{4,1},{5,0},{6,3},{7,2},{8,13},{9,12},{10,... | collective-permute-start | bytes 49160 | tf_op jit(solution)/shard_map/ppermute | solution.py:359

commit v7 on v6

--- a/solution.py
+++ b/solution.py
@@ -162,18 +162,6 @@
     return copies
 
 
-def load_rows(pieces, rows_in, sems):
-    at, copies = 0, []
-    for i, ref in enumerate(pieces):
-        copies.append(
-            pltpu.make_async_copy(ref, rows_in.at[pl.ds(at, ref.shape[0])], sems.at[i])
-        )
-        at += ref.shape[0]
-    for c in copies:
-        c.start()
-    return copies
-
-
 def base_kernel(rows_in, *refs):
     wide, (kept, sent, w, w_sem) = refs[:4], refs[4:]
     copies = gather_wide(wide, w, w_sem)
@@ -201,11 +189,11 @@
 
 def own_kernel(ids, ids_p, mine, theirs, *refs):
     wide, narrow, refs = refs[:4], refs[4:6], refs[6:]
-    kept, to_x, m_y, m_xy, up_own, w, d, up, rows_in, w_sem, d_sem, r_sem = refs
+    kept, to_x, m_y, m_xy, up_own, w, d, up, w_sem, d_sem = refs
     t = lax.axis_index("tensor")
     rows, features = mine.shape
     cols = pl.ds(0, features)
-    copies = load_rows((mine, theirs), rows_in, r_sem) + gather_wide(wide, w, w_sem)
+    copies = gather_wide(wide, w, w_sem)
 
     def fetch(b, ref, line):
         lines = pl.ds(line, RANK)
@@ -237,8 +225,8 @@
 
     for c in copies:
         c.wait()
-    to_x[:rows, :] = dot_nt(rows_in[pl.ds(0, rows), :], w[pl.ds(HALF, HALF), :])
-    kept[:rows, :] = dot_nt(rows_in[pl.ds(0, rows), :], w[pl.ds(0, HALF), :])
+    to_x[:rows, :] = dot_nt(mine[...], w[pl.ds(HALF, HALF), :])
+    kept[:rows, :] = dot_nt(mine[...], w[pl.ds(0, HALF), :])
     for b, here in enumerate(where):
 
         @pl.when(here)
@@ -248,7 +236,7 @@
 
     for b in range(4):
         at = pl.ds(b % 2 * BLK, BLK)
-        m = dot_nt(d[b], rows_in[pl.ds(b * BLK, BLK), :])
+        m = dot_nt(d[b], (mine if b < 2 else theirs)[at, :])
         limit = ids[2 + b] if b < 2 else ids_p[b]
         m = jnp.where(lax.broadcasted_iota(jnp.int32, m.shape, 1) < limit, m, 0.0)
         if b < 2:
@@ -272,18 +260,16 @@
     return pl.pallas_call(
         own_kernel,
         out_shape=[jax.ShapeDtypeStruct(*s) for s in shapes],
-        in_specs=[IN_SMEM] * 2 + [IN_ANY] * (2 + len(wide) + len(narrow)),
+        in_specs=[IN_SMEM] * 2 + [IN_VMEM] * 2 + [IN_ANY] * (len(wide) + len(narrow)),
         out_specs=[IN_VMEM] * 5,
         scratch_shapes=[
             pltpu.VMEM((2 * HALF, features), BF16),
             pltpu.VMEM((4, RANK, features), BF16),
             pltpu.VMEM((4, RANK, 2 * HALF), BF16),
-            pltpu.VMEM((2 * rows, features), BF16),
             pltpu.SemaphoreType.DMA((2 * DEPTH,)),
             pltpu.SemaphoreType.DMA((8,)),
-            pltpu.SemaphoreType.DMA((2,)),
         ],
-        compiler_params=pltpu.CompilerParams(vmem_limit_bytes=13 * MIB),
+        compiler_params=pltpu.CompilerParams(vmem_limit_bytes=9 * MIB),
         cost_estimate=pl.CostEstimate(flops=0, bytes_accessed=0, transcendentals=0),
     )(*scalars, mine, theirs, *wide, *narrow)
 
@@ -366,7 +352,7 @@
         half = lax.dynamic_slice_in_dim(up[0], lax.axis_index("adapter") * 2 * HALF, 2 * HALF, 1)
         d0 = jnp.concatenate([down, half], axis=1)
         ids = jnp.concatenate([chosen, live])
-        w2, w1, w0, d0 = tie((w2, w1, w0, d0))
+        w2, w0, d0 = tie((w2, w0, d0))
         w3 = over_tensor(w2, 4)
         d2, d1 = over_tensor(d0, 8), over_tensor(d0, 4)
         w = jnp.concatenate([w0, w1, w2])

time: 72.2 us -> 72 us (level)
  no operation moved by 1% of the time
where the time goes in v7:
time: 72 us; the launch traced here: 71.8 us
  waiting for transfers between devices  41.7 us (58%)
  starting transfers between devices  20.5 us (28%)
  Pallas kernels  6.61 us (9%)
  other arithmetic  1.66 us (2%)
  local copies, waits for them, and re-layouts  1.21 us (2%)
    ppermute x13, waiting for transfers between devices, over_tensor(): lax.ppermute(array, 'tensor', perm=[(i, i ^ flip) for i in range(tensor)])  39.5 us
    ppermute x13, starting transfers between devices, over_tensor(): lax.ppermute(array, 'tensor', perm=[(i, i ^ flip) for i in range(tensor)])  16.9 us
    pallas_call x1, Pallas kernels, own_sums(): pl.pallas_call(own_kernel, out_shape=[jax.ShapeDtypeStruct(*s) for s in s...  3.93 us
    ppermute x2, starting transfers between devices, over_both(): return lax.ppermute(array, ('tensor', 'adapter'), perm=pairs)  3.05 us
    ppermute x2, waiting for transfers between devices, over_both(): return lax.ppermute(array, ('tensor', 'adapter'), perm=pairs)  2.29 us
    pallas_call x1, Pallas kernels, base_sums(): pl.pallas_call(base_kernel, out_shape=[jax.ShapeDtypeStruct((rows, HALF),...  1.65 us
  transfers between devices with their start and end apart: 16, of which 8 were waited for; matrix products, arithmetic and copies ran while one was open for 4% of the time, Pallas kernels for 8%

profile of v7, /device:TPU:0, one launch (start us, length us, event | category | flops | bytes accessed | tf_op | source)
XLA Modules:
  0.0 71.8 jit_solution(2277382910823287015)
XLA Ops:
  0.0 4.0 %collective-permute-start = (bf16[64,4096]{1,0:T(8,128)(2,1)}, bf16[64,4096]{1,0:T(8,128)(2,1)S(1)}, u32[]{:S(2)}, u32[]{:S(2)}) collective-permute-start(bf16[64,4096]{1,0:T(8,128)(2,1)} %bitcast.6), channel_id=1, source_target_pairs={{0,16},{2,18},{4,20},{6,22},{8,24},{10,26},{12,28},{14,30},{16,0},... | collective-permute-start | bytes 1572872 | tf_op jit(solution)/shard_map/ppermute | solution.py:21
  4.0 1.6 %collective-permute-start.6 = (bf16[64,4096]{1,0:T(8,128)(2,1)}, bf16[64,4096]{1,0:T(8,128)(2,1)S(1)}, u32[]{:S(2)}, u32[]{:S(2)}) collective-permute-start(bf16[64,4096]{1,0:T(8,128)(2,1)} %bitcast.7), channel_id=1, source_target_pairs={{0,8},{2,10},{4,12},{6,14},{8,0},{10,2},{12,4},{14,6},{16,24},{18,... | collective-permute-start | bytes 1572872 | tf_op jit(solution)/shard_map/ppermute | solution.py:21
  5.6 1.5 %collective-permute-start.5 = (bf16[256,4096]{1,0:T(8,128)(2,1)}, bf16[256,4096]{1,0:T(8,128)(2,1)S(1)}, u32[]{:S(2)}, u32[]{:S(2)}) collective-permute-start(bf16[256,4096]{1,0:T(8,128)(2,1)} %mine.1), channel_id=1, source_target_pairs={{0,4},{2,6},{4,0},{6,2},{8,12},{10,14},{12,8},{14,10},{16,20},{18,... | collective-permute-start | bytes 6291464 | tf_op jit(solution)/shard_map/ppermute | solution.py:21
  7.1 0.7 %pad_add_fusion.ids = s32[4]{0:T(128)S(1)} fusion(s32[2]{0:T(128)} %param.11, s32[2]{0:T(128)} %param.10), kind=kLoop, calls=%fused_computation.9 | loop fusion | flops 4 | bytes 32 | tf_op jit(solution)/shard_map/concatenate | solution.py:354
  7.9 0.9 %pad_maximum_fusion = bf16[16,4608]{1,0:T(8,128)(2,1)S(1)} fusion(bf16[16,512]{1,0:T(8,128)(2,1)S(1)} %dynamic-slice_bitcast_fusion, bf16[16,4096]{1,0:T(8,128)(2,1)} %bitcast.9), kind=kLoop, calls=%fused_computation | loop fusion | flops 294912 | bytes 294912 | tf_op jit(solution)/shard_map/concatenate | solution.py:353
  8.8 18.7 %collective-permute-done = bf16[64,4096]{1,0:T(8,128)(2,1)S(1)} collective-permute-done((bf16[64,4096]{1,0:T(8,128)(2,1)}, bf16[64,4096]{1,0:T(8,128)(2,1)S(1)}, u32[]{:S(2)}, u32[]{:S(2)}) %collective-permute-start) | collective-permute-done | bytes 524320 | tf_op jit(solution)/shard_map/ppermute | solution.py:21
  27.5 0.7 %collective-permute-start.1 = (bf16[16,4608]{1,0:T(8,128)(2,1)S(1)}, bf16[16,4608]{1,0:T(8,128)(2,1)S(1)}, u32[]{:S(2)}, u32[]{:S(2)}) collective-permute-start(bf16[16,4608]{1,0:T(8,128)(2,1)S(1)} %pad_maximum_fusion), channel_id=1, source_target_pairs={{0,8},{2,10},{4,12},{6,14},{8,0},{10,2},{12,4},{14,6},{16,24},{18,... | collective-permute-start | bytes 442376 | tf_op jit(solution)/shard_map/ppermute | solution.py:21
  28.2 3.3 %collective-permute-start.2 = (bf16[16,4608]{1,0:T(8,128)(2,1)S(1)}, bf16[16,4608]{1,0:T(8,128)(2,1)S(1)}, u32[]{:S(2)}, u32[]{:S(2)}) collective-permute-start(bf16[16,4608]{1,0:T(8,128)(2,1)S(1)} %pad_maximum_fusion), channel_id=1, source_target_pairs={{0,16},{2,18},{4,20},{6,22},{8,24},{10,26},{12,28},{14,30},{16,0},... | collective-permute-start | bytes 442376 | tf_op jit(solution)/shard_map/ppermute | solution.py:21
  31.5 0.4 collective-permute-start.3
  31.9 1.1 %constant_dynamic-update-slice_fusion.2 = bf16[192,4096]{1,0:T(8,128)(2,1)S(1)} fusion(bf16[64,4096]{1,0:T(8,128)(2,1)} %bitcast.8), kind=kLoop, calls=%fused_computation.3 | loop fusion | bytes 1048576
  33.0 0.2 collective-permute-start.4
  33.3 1.9 %collective-permute-done.1 = bf16[16,4608]{1,0:T(8,128)(2,1)S(1)} collective-permute-done((bf16[16,4608]{1,0:T(8,128)(2,1)S(1)}, bf16[16,4608]{1,0:T(8,128)(2,1)S(1)}, u32[]{:S(2)}, u32[]{:S(2)}) %collective-permute-start.1) | collective-permute-done | bytes 147488 | tf_op jit(solution)/shard_map/ppermute | solution.py:21
  35.3 7.3 %collective-permute-done.2 = bf16[16,4608]{1,0:T(8,128)(2,1)S(1)} collective-permute-done((bf16[16,4608]{1,0:T(8,128)(2,1)S(1)}, bf16[16,4608]{1,0:T(8,128)(2,1)S(1)}, u32[]{:S(2)}, u32[]{:S(2)}) %collective-permute-start.2) | collective-permute-done | bytes 147488 | tf_op jit(solution)/shard_map/ppermute | solution.py:21
  42.6 7.6 %collective-permute-done.4.refs_1_ = bf16[64,4096]{1,0:T(8,128)(2,1)S(1)} collective-permute-done((bf16[64,4096]{1,0:T(8,128)(2,1)S(1)}, bf16[64,4096]{1,0:T(8,128)(2,1)S(1)}, u32[]{:S(2)}, u32[]{:S(2)}) %collective-permute-start.4) | collective-permute-done | bytes 524320 | tf_op jit(solution)/shard_map/ppermute | solution.py:21
  50.2 0.0 collective-permute-start.8
  50.3 0.0 copy-start.1
  50.3 0.6 collective-permute-start.10
  50.9 1.6 %collective-permute-start.9 = (s32[4]{0:T(128)S(1)}, s32[4]{0:T(128)S(1)}, u32[]{:S(2)}, u32[]{:S(2)}) collective-permute-start(s32[4]{0:T(128)S(1)} %pad_add_fusion.ids), channel_id=1, source_target_pairs={{0,4},{2,6},{4,0},{6,2},{8,12},{10,14},{12,8},{14,10},{16,20},{18,... | collective-permute-start | bytes 56 | tf_op jit(solution)/shard_map/ppermute | solution.py:21
  52.4 0.0 collective-permute-done.8.refs_3_
  52.4 0.0 collective-permute-done.7.refs_2_
  52.4 0.2 collective-permute-done.5.rows_in.theirs
  52.6 1.7 %shard_map.64 = (f32[256,256]{1,0:T(8,128)S(1)}, f32[256,256]{1,0:T(8,128)S(1)}) custom-call(bf16[256,4096]{1,0:T(8,128)(2,1)S(1)} %collective-permute-done.5.rows_in.theirs, bf16[192,4096]{1,0:T(8,128)(2,1)S(1)} %constant_dynamic-update-slice_fusion.refs_0_, bf16[64,4096]{1,0:T(8,128)(2,1)S(1)} %collective-permute-done.4.refs_1_, ...), custom_call_target="tpu_custom_call" | custom-call | tf_op jit(solution)/shard_map/pallas_call | solution.py:176
  54.3 0.1 collective-permute-done.9.ids_p
  54.4 1.6 %collective-permute-start.12 = (f32[256,256]{1,0:T(8,128)S(1)}, f32[256,256]{1,0:T(8,128)S(1)}, u32[]{:S(2)}, u32[]{:S(2)}) collective-permute-start(f32[256,256]{1,0:T(8,128)S(1)} %get-tuple-element.37), channel_id=1, source_target_pairs={{0,4},{2,6},{4,0},{6,2},{8,12},{10,14},{12,8},{14,10},{16,20},{18,... | collective-permute-start | bytes 786440 | tf_op jit(solution)/shard_map/ppermute | solution.py:21
  56.0 1.4 %collective-permute-start.13 = (f32[256,256]{1,0:T(8,128)S(1)}, f32[256,256]{1,0:T(8,128)S(1)}, u32[]{:S(2)}, u32[]{:S(2)}) collective-permute-start(f32[256,256]{1,0:T(8,128)S(1)} %get-tuple-element.38), channel_id=1, source_target_pairs={{0,5},{1,4},{2,7},{3,6},{4,1},{5,0},{6,3},{7,2},{8,13},{9,12},{10,... | collective-permute-start | bytes 786440 | tf_op jit(solution)/shard_map/ppermute | solution.py:345
  57.4 3.9 %shard_map.65 = (f32[272,256]{1,0:T(8,128)S(1)}, f32[272,256]{1,0:T(8,128)S(1)}, bf16[112,256]{1,0:T(8,128)(2,1)S(1)}, f32[16,256]{1,0:T(8,128)S(1)}, bf16[2,16,512]{2,1,0:T(8,128)(2,1)S(1)}) custom-call(s32[4]{0:T(128)S(1)} %pad_add_fusion.ids, s32[4]{0:T(128)S(1)} %collective-permute-done.9.ids_p, bf16[256,4096]{1,0:T(8,128)(2,1)S(1)} %copy-done.1, ...), custom_call_target="tpu_custom_call" | custom-call | tf_op jit(solution)/shard_map/pallas_call | solution.py:260
  61.3 0.6 collective-permute-start.11
  61.9 1.4 %collective-permute-start.14 = (bf16[112,256]{1,0:T(8,128)(2,1)S(1)}, bf16[112,256]{1,0:T(8,128)(2,1)S(1)}, u32[]{:S(2)}, u32[]{:S(2)}) collective-permute-start(bf16[112,256]{1,0:T(8,128)(2,1)S(1)} %get-tuple-element.39), channel_id=1, source_target_pairs={{0,4},{2,6},{4,0},{6,2},{8,12},{10,14},{12,8},{14,10},{16,20},{18,... | collective-permute-start | bytes 172040 | tf_op jit(solution)/shard_map/ppermute | solution.py:21
  63.3 1.6 %collective-permute-start.15 = (f32[16,256]{1,0:T(8,128)S(1)}, f32[16,256]{1,0:T(8,128)S(1)}, u32[]{:S(2)}, u32[]{:S(2)}) collective-permute-start(f32[16,256]{1,0:T(8,128)S(1)} %get-tuple-element.40), channel_id=1, source_target_pairs={{0,5},{1,4},{2,7},{3,6},{4,1},{5,0},{6,3},{7,2},{8,13},{9,12},{10,... | collective-permute-start | bytes 49160 | tf_op jit(solution)/shard_map/ppermute | solution.py:345
  64.9 3.6 %collective-permute-done.12.a = f32[256,256]{1,0:T(8,128)S(1)} collective-permute-done((f32[256,256]{1,0:T(8,128)S(1)}, f32[256,256]{1,0:T(8,128)S(1)}, u32[]{:S(2)}, u32[]{:S(2)}) %collective-permute-start.12) | collective-permute-done | bytes 262176 | tf_op jit(solution)/shard_map/ppermute | solution.py:21
  68.5 2.3 %collective-permute-done.15.m_xy = f32[16,256]{1,0:T(8,128)S(1)} collective-permute-done((f32[16,256]{1,0:T(8,128)S(1)}, f32[16,256]{1,0:T(8,128)S(1)}, u32[]{:S(2)}, u32[]{:S(2)}) %collective-permute-start.15) | collective-permute-done | bytes 16416 | tf_op jit(solution)/shard_map/ppermute | solution.py:345
  70.8 1.0 %shard_map.67 = bf16[256,512]{1,0:T(8,128)(2,1)} custom-call(f32[272,256]{1,0:T(8,128)S(1)} %get-tuple-element.34.kept, bf16[2,16,512]{2,1,0:T(8,128)(2,1)S(1)} %get-tuple-element.35.up_own, f32[272,256]{1,0:T(8,128)S(1)} %collective-permute-done.11.from_x, f32[256,256]{1,0:T(8,128)S(1)} %shard_map.66.other, ...), custom_call_target="tpu_custom_call" | custom-call | tf_op jit(solution)/shard_map/pallas_call | solution.py:326
  (18 shorter events, 0.2 us)
Async XLA Ops:
  0.0 7.1 %copy-start = (bf16[1,16,1024]{2,1,0:T(8,128)(2,1)S(1)}, bf16[1,16,1024]{2,1,0:T(8,128)(2,1)}, u32[]{:S(2)}) copy-start(bf16[1,16,1024]{2,1,0:T(8,128)(2,1)} %param.9) | copy-start | bytes 98308
  0.0 27.5 %collective-permute-start = (bf16[64,4096]{1,0:T(8,128)(2,1)}, bf16[64,4096]{1,0:T(8,128)(2,1)S(1)}, u32[]{:S(2)}, u32[]{:S(2)}) collective-permute-start(bf16[64,4096]{1,0:T(8,128)(2,1)} %bitcast.6), channel_id=1, source_target_pairs={{0,16},{2,18},{4,20},{6,22},{8,24},{10,26},{12,28},{14,30},{16,0},... | collective-permute-start | bytes 1572872 | tf_op jit(solution)/shard_map/ppermute | solution.py:21
  4.0 29.0 %collective-permute-start.6 = (bf16[64,4096]{1,0:T(8,128)(2,1)}, bf16[64,4096]{1,0:T(8,128)(2,1)S(1)}, u32[]{:S(2)}, u32[]{:S(2)}) collective-permute-start(bf16[64,4096]{1,0:T(8,128)(2,1)} %bitcast.7), channel_id=1, source_target_pairs={{0,8},{2,10},{4,12},{6,14},{8,0},{10,2},{12,4},{14,6},{16,24},{18,... | collective-permute-start | bytes 1572872 | tf_op jit(solution)/shard_map/ppermute | solution.py:21
  5.6 47.0 %collective-permute-start.5 = (bf16[256,4096]{1,0:T(8,128)(2,1)}, bf16[256,4096]{1,0:T(8,128)(2,1)S(1)}, u32[]{:S(2)}, u32[]{:S(2)}) collective-permute-start(bf16[256,4096]{1,0:T(8,128)(2,1)} %mine.1), channel_id=1, source_target_pairs={{0,4},{2,6},{4,0},{6,2},{8,12},{10,14},{12,8},{14,10},{16,20},{18,... | collective-permute-start | bytes 6291464 | tf_op jit(solution)/shard_map/ppermute | solution.py:21
  27.5 7.7 %collective-permute-start.1 = (bf16[16,4608]{1,0:T(8,128)(2,1)S(1)}, bf16[16,4608]{1,0:T(8,128)(2,1)S(1)}, u32[]{:S(2)}, u32[]{:S(2)}) collective-permute-start(bf16[16,4608]{1,0:T(8,128)(2,1)S(1)} %pad_maximum_fusion), channel_id=1, source_target_pairs={{0,8},{2,10},{4,12},{6,14},{8,0},{10,2},{12,4},{14,6},{16,24},{18,... | collective-permute-start | bytes 442376 | tf_op jit(solution)/shard_map/ppermute | solution.py:21
  28.2 14.4 %collective-permute-start.2 = (bf16[16,4608]{1,0:T(8,128)(2,1)S(1)}, bf16[16,4608]{1,0:T(8,128)(2,1)S(1)}, u32[]{:S(2)}, u32[]{:S(2)}) collective-permute-start(bf16[16,4608]{1,0:T(8,128)(2,1)S(1)} %pad_maximum_fusion), channel_id=1, source_target_pairs={{0,16},{2,18},{4,20},{6,22},{8,24},{10,26},{12,28},{14,30},{16,0},... | collective-permute-start | bytes 442376 | tf_op jit(solution)/shard_map/ppermute | solution.py:21
  31.5 11.1 %collective-permute-start.3 = (bf16[16,4608]{1,0:T(8,128)(2,1)S(1)}, bf16[16,4608]{1,0:T(8,128)(2,1)S(1)}, u32[]{:S(2)}, u32[]{:S(2)}) collective-permute-start(bf16[16,4608]{1,0:T(8,128)(2,1)S(1)} %pad_maximum_fusion), channel_id=1, source_target_pairs={{0,24},{2,26},{4,28},{6,30},{8,16},{10,18},{12,20},{14,22},{16,8},... | collective-permute-start | bytes 442376 | tf_op jit(solution)/shard_map/ppermute | solution.py:21
  33.0 17.2 %collective-permute-start.4 = (bf16[64,4096]{1,0:T(8,128)(2,1)S(1)}, bf16[64,4096]{1,0:T(8,128)(2,1)S(1)}, u32[]{:S(2)}, u32[]{:S(2)}) collective-permute-start(bf16[64,4096]{1,0:T(8,128)(2,1)S(1)} %collective-permute-done), channel_id=1, source_target_pairs={{0,8},{2,10},{4,12},{6,14},{8,0},{10,2},{12,4},{14,6},{16,24},{18,... | collective-permute-start | bytes 1572872 | tf_op jit(solution)/shard_map/ppermute | solution.py:21
  35.3 17.2 %collective-permute-start.7 = (bf16[192,4096]{1,0:T(8,128)(2,1)S(1)}, bf16[192,4096]{1,0:T(8,128)(2,1)S(1)}, u32[]{:S(2)}, u32[]{:S(2)}) collective-permute-start(bf16[192,4096]{1,0:T(8,128)(2,1)S(1)} %constant_dynamic-update-slice_fusion.refs_0_), channel_id=1, source_target_pairs={{0,2},{2,0},{4,6},{6,4},{8,10},{10,8},{12,14},{14,12},{16,18},{18,... | collective-permute-start | bytes 4718600 | tf_op jit(solution)/shard_map/ppermute | solution.py:21
  50.2 2.2 %collective-permute-start.8 = (bf16[64,4096]{1,0:T(8,128)(2,1)S(1)}, bf16[64,4096]{1,0:T(8,128)(2,1)S(1)}, u32[]{:S(2)}, u32[]{:S(2)}) collective-permute-start(bf16[64,4096]{1,0:T(8,128)(2,1)S(1)} %collective-permute-done.4.refs_1_), channel_id=1, source_target_pairs={{0,2},{2,0},{4,6},{6,4},{8,10},{10,8},{12,14},{14,12},{16,18},{18,... | collective-permute-start | bytes 1572872 | tf_op jit(solution)/shard_map/ppermute | solution.py:21
  50.3 7.1 %copy-start.1 = (bf16[256,4096]{1,0:T(8,128)(2,1)S(1)}, bf16[256,4096]{1,0:T(8,128)(2,1)}, u32[]{:S(2)}) copy-start(bf16[256,4096]{1,0:T(8,128)(2,1)} %mine.1) | copy-start | bytes 6291460
  50.3 7.1 %collective-permute-start.10 = (bf16[64,4608]{1,0:T(8,128)(2,1)S(1)}, bf16[64,4608]{1,0:T(8,128)(2,1)S(1)}, u32[]{:S(2)}, u32[]{:S(2)}) collective-permute-start(bf16[64,4608]{1,0:T(8,128)(2,1)S(1)} %constant_dynamic-update-slice_fusion.3.refs_4_), channel_id=1, source_target_pairs={{0,2},{2,0},{4,6},{6,4},{8,10},{10,8},{12,14},{14,12},{16,18},{18,... | collective-permute-start | bytes 1769480 | tf_op jit(solution)/shard_map/ppermute | solution.py:21
  50.9 3.5 %collective-permute-start.9 = (s32[4]{0:T(128)S(1)}, s32[4]{0:T(128)S(1)}, u32[]{:S(2)}, u32[]{:S(2)}) collective-permute-start(s32[4]{0:T(128)S(1)} %pad_add_fusion.ids), channel_id=1, source_target_pairs={{0,4},{2,6},{4,0},{6,2},{8,12},{10,14},{12,8},{14,10},{16,20},{18,... | collective-permute-start | bytes 56 | tf_op jit(solution)/shard_map/ppermute | solution.py:21
  54.4 14.1 %collective-permute-start.12 = (f32[256,256]{1,0:T(8,128)S(1)}, f32[256,256]{1,0:T(8,128)S(1)}, u32[]{:S(2)}, u32[]{:S(2)}) collective-permute-start(f32[256,256]{1,0:T(8,128)S(1)} %get-tuple-element.37), channel_id=1, source_target_pairs={{0,4},{2,6},{4,0},{6,2},{8,12},{10,14},{12,8},{14,10},{16,20},{18,... | collective-permute-start | bytes 786440 | tf_op jit(solution)/shard_map/ppermute | solution.py:21
  56.0 12.5 %collective-permute-start.13 = (f32[256,256]{1,0:T(8,128)S(1)}, f32[256,256]{1,0:T(8,128)S(1)}, u32[]{:S(2)}, u32[]{:S(2)}) collective-permute-start(f32[256,256]{1,0:T(8,128)S(1)} %get-tuple-element.38), channel_id=1, source_target_pairs={{0,5},{1,4},{2,7},{3,6},{4,1},{5,0},{6,3},{7,2},{8,13},{9,12},{10,... | collective-permute-start | bytes 786440 | tf_op jit(solution)/shard_map/ppermute | solution.py:345
  61.3 9.4 %collective-permute-start.11 = (f32[272,256]{1,0:T(8,128)S(1)}, f32[272,256]{1,0:T(8,128)S(1)}, u32[]{:S(2)}, u32[]{:S(2)}) collective-permute-start(f32[272,256]{1,0:T(8,128)S(1)} %get-tuple-element.36), channel_id=1, source_target_pairs={{0,1},{1,0},{2,3},{3,2},{4,5},{5,4},{6,7},{7,6},{8,9},{9,8},{10,11... | collective-permute-start | bytes 835592 | tf_op jit(solution)/shard_map/ppermute | solution.py:24
  61.9 8.9 %collective-permute-start.14 = (bf16[112,256]{1,0:T(8,128)(2,1)S(1)}, bf16[112,256]{1,0:T(8,128)(2,1)S(1)}, u32[]{:S(2)}, u32[]{:S(2)}) collective-permute-start(bf16[112,256]{1,0:T(8,128)(2,1)S(1)} %get-tuple-element.39), channel_id=1, source_target_pairs={{0,4},{2,6},{4,0},{6,2},{8,12},{10,14},{12,8},{14,10},{16,20},{18,... | collective-permute-start | bytes 172040 | tf_op jit(solution)/shard_map/ppermute | solution.py:21
  63.3 7.5 %collective-permute-start.15 = (f32[16,256]{1,0:T(8,128)S(1)}, f32[16,256]{1,0:T(8,128)S(1)}, u32[]{:S(2)}, u32[]{:S(2)}) collective-permute-start(f32[16,256]{1,0:T(8,128)S(1)} %get-tuple-element.40), channel_id=1, source_target_pairs={{0,5},{1,4},{2,7},{3,6},{4,1},{5,0},{6,3},{7,2},{8,13},{9,12},{10,... | collective-permute-start | bytes 49160 | tf_op jit(solution)/shard_map/ppermute | solution.py:345

commit v8 on v7

--- a/solution.py
+++ b/solution.py
@@ -365,7 +365,7 @@
         wide = (w, w3, v, v3)
         to_y, to_xy = base_sums(theirs, wide)
         to_y, to_xy, ids_p = tie((to_y, to_xy, ids_p))
-        other = add(over_tensor(to_y, 2), over_both(to_xy))
+        other = add(over_both(to_xy), over_tensor(to_y, 2))
         narrow = (narrow, narrow_v)
         kept, to_x, m_y, m_xy, up_own = own_sums(
             (ids, ids_p), hidden, theirs, narrow, wide

time: 72 us -> 71.5 us (level)
    ppermute x2, waiting for transfers between devices: 2.29 us -> 1.22 us  [over_both(): return lax.ppermute(array, ('tensor', 'adapter'), perm=pairs)]
    ppermute x2, starting transfers between devices: 3.05 us -> 3.93 us  [over_both(): return lax.ppermute(array, ('tensor', 'adapter'), perm=pairs)]
    ppermute x13, starting transfers between devices: 16.9 us -> 16 us  [over_tensor(): lax.ppermute(array, 'tensor', perm=[(i, i ^ flip) for i in range(tensor)])]
  transfers between devices with their start and end apart: 16 -> 16, of which waited for: 8 -> 9; matrix products, arithmetic and copies ran while one was open for 4% -> 4% of each run, Pallas kernels for 8% -> 8%
where the time goes in v8:
time: 71.5 us; the launch traced here: 71.3 us
  waiting for transfers between devices  41.4 us (58%)
  starting transfers between devices  20.5 us (29%)
  Pallas kernels  6.51 us (9%)
  other arithmetic  1.66 us (2%)
  local copies, waits for them, and re-layouts  1.21 us (2%)
    ppermute x13, waiting for transfers between devices, over_tensor(): lax.ppermute(array, 'tensor', perm=[(i, i ^ flip) for i in range(tensor)])  40.2 us
    ppermute x13, starting transfers between devices, over_tensor(): lax.ppermute(array, 'tensor', perm=[(i, i ^ flip) for i in range(tensor)])  16 us
    ppermute x2, starting transfers between devices, over_both(): return lax.ppermute(array, ('tensor', 'adapter'), perm=pairs)  3.93 us
    pallas_call x1, Pallas kernels, own_sums(): pl.pallas_call(own_kernel, out_shape=[jax.ShapeDtypeStruct(*s) for s in s...  3.83 us
    pallas_call x1, Pallas kernels, base_sums(): pl.pallas_call(base_kernel, out_shape=[jax.ShapeDtypeStruct((rows, HALF),...  1.65 us
  transfers between devices with their start and end apart: 16, of which 9 were waited for; matrix products, arithmetic and copies ran while one was open for 4% of the time, Pallas kernels for 8%

profile of v8, /device:TPU:0, one launch (start us, length us, event | category | flops | bytes accessed | tf_op | source)
XLA Modules:
  0.0 71.3 jit_solution(6167971980549244286)
XLA Ops:
  0.0 4.0 %collective-permute-start = (bf16[64,4096]{1,0:T(8,128)(2,1)}, bf16[64,4096]{1,0:T(8,128)(2,1)S(1)}, u32[]{:S(2)}, u32[]{:S(2)}) collective-permute-start(bf16[64,4096]{1,0:T(8,128)(2,1)} %bitcast.6), channel_id=1, source_target_pairs={{0,16},{2,18},{4,20},{6,22},{8,24},{10,26},{12,28},{14,30},{16,0},... | collective-permute-start | bytes 1572872 | tf_op jit(solution)/shard_map/ppermute | solution.py:21
  4.0 1.6 %collective-permute-start.6 = (bf16[64,4096]{1,0:T(8,128)(2,1)}, bf16[64,4096]{1,0:T(8,128)(2,1)S(1)}, u32[]{:S(2)}, u32[]{:S(2)}) collective-permute-start(bf16[64,4096]{1,0:T(8,128)(2,1)} %bitcast.7), channel_id=1, source_target_pairs={{0,8},{2,10},{4,12},{6,14},{8,0},{10,2},{12,4},{14,6},{16,24},{18,... | collective-permute-start | bytes 1572872 | tf_op jit(solution)/shard_map/ppermute | solution.py:21
  5.6 1.5 %collective-permute-start.5 = (bf16[256,4096]{1,0:T(8,128)(2,1)}, bf16[256,4096]{1,0:T(8,128)(2,1)S(1)}, u32[]{:S(2)}, u32[]{:S(2)}) collective-permute-start(bf16[256,4096]{1,0:T(8,128)(2,1)} %mine.1), channel_id=1, source_target_pairs={{0,4},{2,6},{4,0},{6,2},{8,12},{10,14},{12,8},{14,10},{16,20},{18,... | collective-permute-start | bytes 6291464 | tf_op jit(solution)/shard_map/ppermute | solution.py:21
  7.1 0.7 %pad_add_fusion.ids = s32[4]{0:T(128)S(1)} fusion(s32[2]{0:T(128)} %param.11, s32[2]{0:T(128)} %param.10), kind=kLoop, calls=%fused_computation.9 | loop fusion | flops 4 | bytes 32 | tf_op jit(solution)/shard_map/concatenate | solution.py:354
  7.9 0.9 %pad_maximum_fusion = bf16[16,4608]{1,0:T(8,128)(2,1)S(1)} fusion(bf16[16,512]{1,0:T(8,128)(2,1)S(1)} %dynamic-slice_bitcast_fusion, bf16[16,4096]{1,0:T(8,128)(2,1)} %bitcast.9), kind=kLoop, calls=%fused_computation | loop fusion | flops 294912 | bytes 294912 | tf_op jit(solution)/shard_map/concatenate | solution.py:353
  8.8 18.7 %collective-permute-done = bf16[64,4096]{1,0:T(8,128)(2,1)S(1)} collective-permute-done((bf16[64,4096]{1,0:T(8,128)(2,1)}, bf16[64,4096]{1,0:T(8,128)(2,1)S(1)}, u32[]{:S(2)}, u32[]{:S(2)}) %collective-permute-start) | collective-permute-done | bytes 524320 | tf_op jit(solution)/shard_map/ppermute | solution.py:21
  27.5 0.7 %collective-permute-start.1 = (bf16[16,4608]{1,0:T(8,128)(2,1)S(1)}, bf16[16,4608]{1,0:T(8,128)(2,1)S(1)}, u32[]{:S(2)}, u32[]{:S(2)}) collective-permute-start(bf16[16,4608]{1,0:T(8,128)(2,1)S(1)} %pad_maximum_fusion), channel_id=1, source_target_pairs={{0,8},{2,10},{4,12},{6,14},{8,0},{10,2},{12,4},{14,6},{16,24},{18,... | collective-permute-start | bytes 442376 | tf_op jit(solution)/shard_map/ppermute | solution.py:21
  28.2 3.3 %collective-permute-start.2 = (bf16[16,4608]{1,0:T(8,128)(2,1)S(1)}, bf16[16,4608]{1,0:T(8,128)(2,1)S(1)}, u32[]{:S(2)}, u32[]{:S(2)}) collective-permute-start(bf16[16,4608]{1,0:T(8,128)(2,1)S(1)} %pad_maximum_fusion), channel_id=1, source_target_pairs={{0,16},{2,18},{4,20},{6,22},{8,24},{10,26},{12,28},{14,30},{16,0},... | collective-permute-start | bytes 442376 | tf_op jit(solution)/shard_map/ppermute | solution.py:21
  31.5 0.4 collective-permute-start.3
  31.9 1.1 %constant_dynamic-update-slice_fusion.2 = bf16[192,4096]{1,0:T(8,128)(2,1)S(1)} fusion(bf16[64,4096]{1,0:T(8,128)(2,1)} %bitcast.8), kind=kLoop, calls=%fused_computation.3 | loop fusion | bytes 1048576
  33.0 0.0 collective-permute-done.6
  33.0 0.2 collective-permute-start.4
  33.3 1.9 %collective-permute-done.1 = bf16[16,4608]{1,0:T(8,128)(2,1)S(1)} collective-permute-done((bf16[16,4608]{1,0:T(8,128)(2,1)S(1)}, bf16[16,4608]{1,0:T(8,128)(2,1)S(1)}, u32[]{:S(2)}, u32[]{:S(2)}) %collective-permute-start.1) | collective-permute-done | bytes 147488 | tf_op jit(solution)/shard_map/ppermute | solution.py:21
  35.3 7.3 %collective-permute-done.2 = bf16[16,4608]{1,0:T(8,128)(2,1)S(1)} collective-permute-done((bf16[16,4608]{1,0:T(8,128)(2,1)S(1)}, bf16[16,4608]{1,0:T(8,128)(2,1)S(1)}, u32[]{:S(2)}, u32[]{:S(2)}) %collective-permute-start.2) | collective-permute-done | bytes 147488 | tf_op jit(solution)/shard_map/ppermute | solution.py:21
  42.6 0.0 collective-permute-done.3
  42.6 7.6 %collective-permute-done.4.refs_1_ = bf16[64,4096]{1,0:T(8,128)(2,1)S(1)} collective-permute-done((bf16[64,4096]{1,0:T(8,128)(2,1)S(1)}, bf16[64,4096]{1,0:T(8,128)(2,1)S(1)}, u32[]{:S(2)}, u32[]{:S(2)}) %collective-permute-start.4) | collective-permute-done | bytes 524320 | tf_op jit(solution)/shard_map/ppermute | solution.py:21
  50.3 0.0 copy-start.1
  50.3 0.6 collective-permute-start.10
  50.9 1.6 %collective-permute-start.9 = (s32[4]{0:T(128)S(1)}, s32[4]{0:T(128)S(1)}, u32[]{:S(2)}, u32[]{:S(2)}) collective-permute-start(s32[4]{0:T(128)S(1)} %pad_add_fusion.ids), channel_id=1, source_target_pairs={{0,4},{2,6},{4,0},{6,2},{8,12},{10,14},{12,8},{14,10},{16,20},{18,... | collective-permute-start | bytes 56 | tf_op jit(solution)/shard_map/ppermute | solution.py:21
  52.4 0.2 collective-permute-done.5.rows_in.theirs
  52.6 1.7 %shard_map.64 = (f32[256,256]{1,0:T(8,128)S(1)}, f32[256,256]{1,0:T(8,128)S(1)}) custom-call(bf16[256,4096]{1,0:T(8,128)(2,1)S(1)} %collective-permute-done.5.rows_in.theirs, bf16[192,4096]{1,0:T(8,128)(2,1)S(1)} %constant_dynamic-update-slice_fusion.refs_0_, bf16[64,4096]{1,0:T(8,128)(2,1)S(1)} %collective-permute-done.4.refs_1_, ...), custom_call_target="tpu_custom_call" | custom-call | tf_op jit(solution)/shard_map/pallas_call | solution.py:176
  54.3 0.1 collective-permute-done.9.ids_p
  54.4 2.5 %collective-permute-start.12 = (f32[256,256]{1,0:T(8,128)S(1)}, f32[256,256]{1,0:T(8,128)S(1)}, u32[]{:S(2)}, u32[]{:S(2)}) collective-permute-start(f32[256,256]{1,0:T(8,128)S(1)} %get-tuple-element.37), channel_id=1, source_target_pairs={{0,5},{1,4},{2,7},{3,6},{4,1},{5,0},{6,3},{7,2},{8,13},{9,12},{10,... | collective-permute-start | bytes 786440 | tf_op jit(solution)/shard_map/ppermute | solution.py:345
  56.9 0.5 collective-permute-start.13
  57.4 3.8 %shard_map.65 = (f32[272,256]{1,0:T(8,128)S(1)}, f32[272,256]{1,0:T(8,128)S(1)}, bf16[112,256]{1,0:T(8,128)(2,1)S(1)}, f32[16,256]{1,0:T(8,128)S(1)}, bf16[2,16,512]{2,1,0:T(8,128)(2,1)S(1)}) custom-call(s32[4]{0:T(128)S(1)} %pad_add_fusion.ids, s32[4]{0:T(128)S(1)} %collective-permute-done.9.ids_p, bf16[256,4096]{1,0:T(8,128)(2,1)S(1)} %copy-done.1, ...), custom_call_target="tpu_custom_call" | custom-call | tf_op jit(solution)/shard_map/pallas_call | solution.py:260
  61.2 0.6 collective-permute-start.11
  61.8 1.6 %collective-permute-start.14 = (bf16[112,256]{1,0:T(8,128)(2,1)S(1)}, bf16[112,256]{1,0:T(8,128)(2,1)S(1)}, u32[]{:S(2)}, u32[]{:S(2)}) collective-permute-start(bf16[112,256]{1,0:T(8,128)(2,1)S(1)} %get-tuple-element.39), channel_id=1, source_target_pairs={{0,4},{2,6},{4,0},{6,2},{8,12},{10,14},{12,8},{14,10},{16,20},{18,... | collective-permute-start | bytes 172040 | tf_op jit(solution)/shard_map/ppermute | solution.py:21
  63.4 1.4 %collective-permute-start.15 = (f32[16,256]{1,0:T(8,128)S(1)}, f32[16,256]{1,0:T(8,128)S(1)}, u32[]{:S(2)}, u32[]{:S(2)}) collective-permute-start(f32[16,256]{1,0:T(8,128)S(1)} %get-tuple-element.40), channel_id=1, source_target_pairs={{0,5},{1,4},{2,7},{3,6},{4,1},{5,0},{6,3},{7,2},{8,13},{9,12},{10,... | collective-permute-start | bytes 49160 | tf_op jit(solution)/shard_map/ppermute | solution.py:345
  64.8 4.2 %collective-permute-done.13.b = f32[256,256]{1,0:T(8,128)S(1)} collective-permute-done((f32[256,256]{1,0:T(8,128)S(1)}, f32[256,256]{1,0:T(8,128)S(1)}, u32[]{:S(2)}, u32[]{:S(2)}) %collective-permute-start.13) | collective-permute-done | bytes 262176 | tf_op jit(solution)/shard_map/ppermute | solution.py:21
  69.0 1.2 %collective-permute-done.15.m_xy = f32[16,256]{1,0:T(8,128)S(1)} collective-permute-done((f32[16,256]{1,0:T(8,128)S(1)}, f32[16,256]{1,0:T(8,128)S(1)}, u32[]{:S(2)}, u32[]{:S(2)}) %collective-permute-start.15) | collective-permute-done | bytes 16416 | tf_op jit(solution)/shard_map/ppermute | solution.py:345
  70.2 0.1 collective-permute-done.14.m_y
  70.3 1.0 %shard_map.67 = bf16[256,512]{1,0:T(8,128)(2,1)} custom-call(f32[272,256]{1,0:T(8,128)S(1)} %get-tuple-element.34.kept, bf16[2,16,512]{2,1,0:T(8,128)(2,1)S(1)} %get-tuple-element.35.up_own, f32[272,256]{1,0:T(8,128)S(1)} %collective-permute-done.11.from_x, f32[256,256]{1,0:T(8,128)S(1)} %shard_map.66.other, ...), custom_call_target="tpu_custom_call" | custom-call | tf_op jit(solution)/shard_map/pallas_call | solution.py:326
  (18 shorter events, 0.2 us)
Async XLA Ops:
  0.0 7.1 %copy-start = (bf16[1,16,1024]{2,1,0:T(8,128)(2,1)S(1)}, bf16[1,16,1024]{2,1,0:T(8,128)(2,1)}, u32[]{:S(2)}) copy-start(bf16[1,16,1024]{2,1,0:T(8,128)(2,1)} %param.9) | copy-start | bytes 98308
  0.0 27.5 %collective-permute-start = (bf16[64,4096]{1,0:T(8,128)(2,1)}, bf16[64,4096]{1,0:T(8,128)(2,1)S(1)}, u32[]{:S(2)}, u32[]{:S(2)}) collective-permute-start(bf16[64,4096]{1,0:T(8,128)(2,1)} %bitcast.6), channel_id=1, source_target_pairs={{0,16},{2,18},{4,20},{6,22},{8,24},{10,26},{12,28},{14,30},{16,0},... | collective-permute-start | bytes 1572872 | tf_op jit(solution)/shard_map/ppermute | solution.py:21
  4.0 29.0 %collective-permute-start.6 = (bf16[64,4096]{1,0:T(8,128)(2,1)}, bf16[64,4096]{1,0:T(8,128)(2,1)S(1)}, u32[]{:S(2)}, u32[]{:S(2)}) collective-permute-start(bf16[64,4096]{1,0:T(8,128)(2,1)} %bitcast.7), channel_id=1, source_target_pairs={{0,8},{2,10},{4,12},{6,14},{8,0},{10,2},{12,4},{14,6},{16,24},{18,... | collective-permute-start | bytes 1572872 | tf_op jit(solution)/shard_map/ppermute | solution.py:21
  5.6 47.0 %collective-permute-start.5 = (bf16[256,4096]{1,0:T(8,128)(2,1)}, bf16[256,4096]{1,0:T(8,128)(2,1)S(1)}, u32[]{:S(2)}, u32[]{:S(2)}) collective-permute-start(bf16[256,4096]{1,0:T(8,128)(2,1)} %mine.1), channel_id=1, source_target_pairs={{0,4},{2,6},{4,0},{6,2},{8,12},{10,14},{12,8},{14,10},{16,20},{18,... | collective-permute-start | bytes 6291464 | tf_op jit(solution)/shard_map/ppermute | solution.py:21
  27.5 7.7 %collective-permute-start.1 = (bf16[16,4608]{1,0:T(8,128)(2,1)S(1)}, bf16[16,4608]{1,0:T(8,128)(2,1)S(1)}, u32[]{:S(2)}, u32[]{:S(2)}) collective-permute-start(bf16[16,4608]{1,0:T(8,128)(2,1)S(1)} %pad_maximum_fusion), channel_id=1, source_target_pairs={{0,8},{2,10},{4,12},{6,14},{8,0},{10,2},{12,4},{14,6},{16,24},{18,... | collective-permute-start | bytes 442376 | tf_op jit(solution)/shard_map/ppermute | solution.py:21
  28.2 14.4 %collective-permute-start.2 = (bf16[16,4608]{1,0:T(8,128)(2,1)S(1)}, bf16[16,4608]{1,0:T(8,128)(2,1)S(1)}, u32[]{:S(2)}, u32[]{:S(2)}) collective-permute-start(bf16[16,4608]{1,0:T(8,128)(2,1)S(1)} %pad_maximum_fusion), channel_id=1, source_target_pairs={{0,16},{2,18},{4,20},{6,22},{8,24},{10,26},{12,28},{14,30},{16,0},... | collective-permute-start | bytes 442376 | tf_op jit(solution)/shard_map/ppermute | solution.py:21
  31.5 11.1 %collective-permute-start.3 = (bf16[16,4608]{1,0:T(8,128)(2,1)S(1)}, bf16[16,4608]{1,0:T(8,128)(2,1)S(1)}, u32[]{:S(2)}, u32[]{:S(2)}) collective-permute-start(bf16[16,4608]{1,0:T(8,128)(2,1)S(1)} %pad_maximum_fusion), channel_id=1, source_target_pairs={{0,24},{2,26},{4,28},{6,30},{8,16},{10,18},{12,20},{14,22},{16,8},... | collective-permute-start | bytes 442376 | tf_op jit(solution)/shard_map/ppermute | solution.py:21
  33.0 17.2 %collective-permute-start.4 = (bf16[64,4096]{1,0:T(8,128)(2,1)S(1)}, bf16[64,4096]{1,0:T(8,128)(2,1)S(1)}, u32[]{:S(2)}, u32[]{:S(2)}) collective-permute-start(bf16[64,4096]{1,0:T(8,128)(2,1)S(1)} %collective-permute-done), channel_id=1, source_target_pairs={{0,8},{2,10},{4,12},{6,14},{8,0},{10,2},{12,4},{14,6},{16,24},{18,... | collective-permute-start | bytes 1572872 | tf_op jit(solution)/shard_map/ppermute | solution.py:21
  35.3 17.2 %collective-permute-start.7 = (bf16[192,4096]{1,0:T(8,128)(2,1)S(1)}, bf16[192,4096]{1,0:T(8,128)(2,1)S(1)}, u32[]{:S(2)}, u32[]{:S(2)}) collective-permute-start(bf16[192,4096]{1,0:T(8,128)(2,1)S(1)} %constant_dynamic-update-slice_fusion.refs_0_), channel_id=1, source_target_pairs={{0,2},{2,0},{4,6},{6,4},{8,10},{10,8},{12,14},{14,12},{16,18},{18,... | collective-permute-start | bytes 4718600 | tf_op jit(solution)/shard_map/ppermute | solution.py:21
  50.2 2.2 %collective-permute-start.8 = (bf16[64,4096]{1,0:T(8,128)(2,1)S(1)}, bf16[64,4096]{1,0:T(8,128)(2,1)S(1)}, u32[]{:S(2)}, u32[]{:S(2)}) collective-permute-start(bf16[64,4096]{1,0:T(8,128)(2,1)S(1)} %collective-permute-done.4.refs_1_), channel_id=1, source_target_pairs={{0,2},{2,0},{4,6},{6,4},{8,10},{10,8},{12,14},{14,12},{16,18},{18,... | collective-permute-start | bytes 1572872 | tf_op jit(solution)/shard_map/ppermute | solution.py:21
  50.3 7.1 %copy-start.1 = (bf16[256,4096]{1,0:T(8,128)(2,1)S(1)}, bf16[256,4096]{1,0:T(8,128)(2,1)}, u32[]{:S(2)}) copy-start(bf16[256,4096]{1,0:T(8,128)(2,1)} %mine.1) | copy-start | bytes 6291460
  50.3 7.1 %collective-permute-start.10 = (bf16[64,4608]{1,0:T(8,128)(2,1)S(1)}, bf16[64,4608]{1,0:T(8,128)(2,1)S(1)}, u32[]{:S(2)}, u32[]{:S(2)}) collective-permute-start(bf16[64,4608]{1,0:T(8,128)(2,1)S(1)} %constant_dynamic-update-slice_fusion.3.refs_4_), channel_id=1, source_target_pairs={{0,2},{2,0},{4,6},{6,4},{8,10},{10,8},{12,14},{14,12},{16,18},{18,... | collective-permute-start | bytes 1769480 | tf_op jit(solution)/shard_map/ppermute | solution.py:21
  50.9 3.5 %collective-permute-start.9 = (s32[4]{0:T(128)S(1)}, s32[4]{0:T(128)S(1)}, u32[]{:S(2)}, u32[]{:S(2)}) collective-permute-start(s32[4]{0:T(128)S(1)} %pad_add_fusion.ids), channel_id=1, source_target_pairs={{0,4},{2,6},{4,0},{6,2},{8,12},{10,14},{12,8},{14,10},{16,20},{18,... | collective-permute-start | bytes 56 | tf_op jit(solution)/shard_map/ppermute | solution.py:21
  54.4 10.4 %collective-permute-start.12 = (f32[256,256]{1,0:T(8,128)S(1)}, f32[256,256]{1,0:T(8,128)S(1)}, u32[]{:S(2)}, u32[]{:S(2)}) collective-permute-start(f32[256,256]{1,0:T(8,128)S(1)} %get-tuple-element.37), channel_id=1, source_target_pairs={{0,5},{1,4},{2,7},{3,6},{4,1},{5,0},{6,3},{7,2},{8,13},{9,12},{10,... | collective-permute-start | bytes 786440 | tf_op jit(solution)/shard_map/ppermute | solution.py:345
  56.9 12.1 %collective-permute-start.13 = (f32[256,256]{1,0:T(8,128)S(1)}, f32[256,256]{1,0:T(8,128)S(1)}, u32[]{:S(2)}, u32[]{:S(2)}) collective-permute-start(f32[256,256]{1,0:T(8,128)S(1)} %get-tuple-element.38), channel_id=1, source_target_pairs={{0,4},{2,6},{4,0},{6,2},{8,12},{10,14},{12,8},{14,10},{16,20},{18,... | collective-permute-start | bytes 786440 | tf_op jit(solution)/shard_map/ppermute | solution.py:21
  61.2 9.1 %collective-permute-start.11 = (f32[272,256]{1,0:T(8,128)S(1)}, f32[272,256]{1,0:T(8,128)S(1)}, u32[]{:S(2)}, u32[]{:S(2)}) collective-permute-start(f32[272,256]{1,0:T(8,128)S(1)} %get-tuple-element.36), channel_id=1, source_target_pairs={{0,1},{1,0},{2,3},{3,2},{4,5},{5,4},{6,7},{7,6},{8,9},{9,8},{10,11... | collective-permute-start | bytes 835592 | tf_op jit(solution)/shard_map/ppermute | solution.py:24
  61.8 8.5 %collective-permute-start.14 = (bf16[112,256]{1,0:T(8,128)(2,1)S(1)}, bf16[112,256]{1,0:T(8,128)(2,1)S(1)}, u32[]{:S(2)}, u32[]{:S(2)}) collective-permute-start(bf16[112,256]{1,0:T(8,128)(2,1)S(1)} %get-tuple-element.39), channel_id=1, source_target_pairs={{0,4},{2,6},{4,0},{6,2},{8,12},{10,14},{12,8},{14,10},{16,20},{18,... | collective-permute-start | bytes 172040 | tf_op jit(solution)/shard_map/ppermute | solution.py:21
  63.4 6.9 %collective-permute-start.15 = (f32[16,256]{1,0:T(8,128)S(1)}, f32[16,256]{1,0:T(8,128)S(1)}, u32[]{:S(2)}, u32[]{:S(2)}) collective-permute-start(f32[16,256]{1,0:T(8,128)S(1)} %get-tuple-element.40), channel_id=1, source_target_pairs={{0,5},{1,4},{2,7},{3,6},{4,1},{5,0},{6,3},{7,2},{8,13},{9,12},{10,... | collective-permute-start | bytes 49160 | tf_op jit(solution)/shard_map/ppermute | solution.py:345

commit v9 on v8

--- a/solution.py
+++ b/solution.py
@@ -358,7 +358,7 @@
         w = jnp.concatenate([w0, w1, w2])
         v = over_tensor(w, 1)
         d3 = over_tensor(d0, 12)
-        d1, d2, d3, w3, ids = tie((d1, d2, d3, w3, ids))
+        d1, d2, d3, w3 = tie((d1, d2, d3, w3))
         v3, ids_p = over_tensor(w3, 1), over_tensor(ids, 2)
         narrow = jnp.concatenate([d0, d1, d2, d3])
         narrow_v = over_tensor(narrow, 1)

time: 71.5 us -> 71.6 us (level)
  transfers between devices with their start and end apart: 16 -> 16, of which waited for: 9 -> 8; matrix products, arithmetic and copies ran while one was open for 4% -> 3% of each run, Pallas kernels for 8% -> 8%
where the time goes in v9:
time: 71.6 us; the launch traced here: 71.4 us
  waiting for transfers between devices  42.1 us (59%)
  starting transfers between devices  20.5 us (29%)
  Pallas kernels  6.52 us (9%)
  local copies, waits for them, and re-layouts  1.22 us (2%)
  other arithmetic  0.99 us (1%)
    ppermute x13, waiting for transfers between devices, over_tensor(): lax.ppermute(array, 'tensor', perm=[(i, i ^ flip) for i in range(tensor)])  40.8 us
    ppermute x13, starting transfers between devices, over_tensor(): lax.ppermute(array, 'tensor', perm=[(i, i ^ flip) for i in range(tensor)])  16 us
    ppermute x2, starting transfers between devices, over_both(): return lax.ppermute(array, ('tensor', 'adapter'), perm=pairs)  3.93 us
    pallas_call x1, Pallas kernels, own_sums(): pl.pallas_call(own_kernel, out_shape=[jax.ShapeDtypeStruct(*s) for s in s...  3.83 us
    pallas_call x1, Pallas kernels, base_sums(): pl.pallas_call(base_kernel, out_shape=[jax.ShapeDtypeStruct((rows, HALF),...  1.65 us
  transfers between devices with their start and end apart: 16, of which 8 were waited for; matrix products, arithmetic and copies ran while one was open for 3% of the time, Pallas kernels for 8%

profile of v9, /device:TPU:0, one launch (start us, length us, event | category | flops | bytes accessed | tf_op | source)
XLA Modules:
  0.0 71.4 jit_solution(5140831558047023422)
XLA Ops:
  0.0 4.0 %collective-permute-start.1 = (bf16[64,4096]{1,0:T(8,128)(2,1)}, bf16[64,4096]{1,0:T(8,128)(2,1)S(1)}, u32[]{:S(2)}, u32[]{:S(2)}) collective-permute-start(bf16[64,4096]{1,0:T(8,128)(2,1)} %bitcast.6), channel_id=1, source_target_pairs={{0,16},{2,18},{4,20},{6,22},{8,24},{10,26},{12,28},{14,30},{16,0},... | collective-permute-start | bytes 1572872 | tf_op jit(solution)/shard_map/ppermute | solution.py:21
  4.0 1.6 %collective-permute-start.2 = (bf16[64,4096]{1,0:T(8,128)(2,1)}, bf16[64,4096]{1,0:T(8,128)(2,1)S(1)}, u32[]{:S(2)}, u32[]{:S(2)}) collective-permute-start(bf16[64,4096]{1,0:T(8,128)(2,1)} %bitcast.7), channel_id=1, source_target_pairs={{0,8},{2,10},{4,12},{6,14},{8,0},{10,2},{12,4},{14,6},{16,24},{18,... | collective-permute-start | bytes 1572872 | tf_op jit(solution)/shard_map/ppermute | solution.py:21
  5.6 1.5 %collective-permute-start = (bf16[256,4096]{1,0:T(8,128)(2,1)}, bf16[256,4096]{1,0:T(8,128)(2,1)S(1)}, u32[]{:S(2)}, u32[]{:S(2)}) collective-permute-start(bf16[256,4096]{1,0:T(8,128)(2,1)} %mine.1), channel_id=1, source_target_pairs={{0,4},{2,6},{4,0},{6,2},{8,12},{10,14},{12,8},{14,10},{16,20},{18,... | collective-permute-start | bytes 6291464 | tf_op jit(solution)/shard_map/ppermute | solution.py:21
  7.1 0.9 %pad_maximum_fusion = bf16[16,4608]{1,0:T(8,128)(2,1)S(1)} fusion(bf16[16,512]{1,0:T(8,128)(2,1)S(1)} %dynamic-slice_bitcast_fusion, bf16[16,4096]{1,0:T(8,128)(2,1)} %bitcast.9), kind=kLoop, calls=%fused_computation | loop fusion | flops 294912 | bytes 294912 | tf_op jit(solution)/shard_map/concatenate | solution.py:353
  8.1 19.5 %collective-permute-done.1 = bf16[64,4096]{1,0:T(8,128)(2,1)S(1)} collective-permute-done((bf16[64,4096]{1,0:T(8,128)(2,1)}, bf16[64,4096]{1,0:T(8,128)(2,1)S(1)}, u32[]{:S(2)}, u32[]{:S(2)}) %collective-permute-start.1) | collective-permute-done | bytes 524320 | tf_op jit(solution)/shard_map/ppermute | solution.py:21
  27.5 0.7 %collective-permute-start.3 = (bf16[16,4608]{1,0:T(8,128)(2,1)S(1)}, bf16[16,4608]{1,0:T(8,128)(2,1)S(1)}, u32[]{:S(2)}, u32[]{:S(2)}) collective-permute-start(bf16[16,4608]{1,0:T(8,128)(2,1)S(1)} %pad_maximum_fusion), channel_id=1, source_target_pairs={{0,8},{2,10},{4,12},{6,14},{8,0},{10,2},{12,4},{14,6},{16,24},{18,... | collective-permute-start | bytes 442376 | tf_op jit(solution)/shard_map/ppermute | solution.py:21
  28.2 3.3 %collective-permute-start.4 = (bf16[16,4608]{1,0:T(8,128)(2,1)S(1)}, bf16[16,4608]{1,0:T(8,128)(2,1)S(1)}, u32[]{:S(2)}, u32[]{:S(2)}) collective-permute-start(bf16[16,4608]{1,0:T(8,128)(2,1)S(1)} %pad_maximum_fusion), channel_id=1, source_target_pairs={{0,16},{2,18},{4,20},{6,22},{8,24},{10,26},{12,28},{14,30},{16,0},... | collective-permute-start | bytes 442376 | tf_op jit(solution)/shard_map/ppermute | solution.py:21
  31.5 0.4 collective-permute-start.5
  31.9 1.1 %constant_dynamic-update-slice_fusion.2 = bf16[192,4096]{1,0:T(8,128)(2,1)S(1)} fusion(bf16[64,4096]{1,0:T(8,128)(2,1)} %bitcast.8), kind=kLoop, calls=%fused_computation.3 | loop fusion | bytes 1048576
  33.0 0.0 copy-start.2
  33.0 0.0 copy-start.3
  33.0 0.2 collective-permute-start.6
  33.4 1.9 %collective-permute-done.3 = bf16[16,4608]{1,0:T(8,128)(2,1)S(1)} collective-permute-done((bf16[16,4608]{1,0:T(8,128)(2,1)S(1)}, bf16[16,4608]{1,0:T(8,128)(2,1)S(1)}, u32[]{:S(2)}, u32[]{:S(2)}) %collective-permute-start.3) | collective-permute-done | bytes 147488 | tf_op jit(solution)/shard_map/ppermute | solution.py:21
  35.2 0.0 collective-permute-start.7
  35.2 7.4 %collective-permute-done.4 = bf16[16,4608]{1,0:T(8,128)(2,1)S(1)} collective-permute-done((bf16[16,4608]{1,0:T(8,128)(2,1)S(1)}, bf16[16,4608]{1,0:T(8,128)(2,1)S(1)}, u32[]{:S(2)}, u32[]{:S(2)}) %collective-permute-start.4) | collective-permute-done | bytes 147488 | tf_op jit(solution)/shard_map/ppermute | solution.py:21
  42.6 0.0 collective-permute-done.5
  42.6 7.6 %collective-permute-done.6.refs_1_ = bf16[64,4096]{1,0:T(8,128)(2,1)S(1)} collective-permute-done((bf16[64,4096]{1,0:T(8,128)(2,1)S(1)}, bf16[64,4096]{1,0:T(8,128)(2,1)S(1)}, u32[]{:S(2)}, u32[]{:S(2)}) %collective-permute-start.6) | collective-permute-done | bytes 524320 | tf_op jit(solution)/shard_map/ppermute | solution.py:21
  50.3 0.6 collective-permute-start.10
  50.8 0.1 pad_add_fusion.ids
  50.9 1.6 %collective-permute-start.9 = (s32[4]{0:T(128)S(1)}, s32[4]{0:T(128)S(1)}, u32[]{:S(2)}, u32[]{:S(2)}) collective-permute-start(s32[4]{0:T(128)S(1)} %pad_add_fusion.ids), channel_id=1, source_target_pairs={{0,4},{2,6},{4,0},{6,2},{8,12},{10,14},{12,8},{14,10},{16,20},{18,... | collective-permute-start | bytes 56 | tf_op jit(solution)/shard_map/ppermute | solution.py:21
  52.5 0.1 collective-permute-done.rows_in.theirs
  52.6 1.7 %shard_map.64 = (f32[256,256]{1,0:T(8,128)S(1)}, f32[256,256]{1,0:T(8,128)S(1)}) custom-call(bf16[256,4096]{1,0:T(8,128)(2,1)S(1)} %collective-permute-done.rows_in.theirs, bf16[192,4096]{1,0:T(8,128)(2,1)S(1)} %constant_dynamic-update-slice_fusion.refs_0_, bf16[64,4096]{1,0:T(8,128)(2,1)S(1)} %collective-permute-done.6.refs_1_, ...), custom_call_target="tpu_custom_call" | custom-call | tf_op jit(solution)/shard_map/pallas_call | solution.py:176
  54.3 0.2 collective-permute-done.9.ids_p
  54.5 2.5 %collective-permute-start.12 = (f32[256,256]{1,0:T(8,128)S(1)}, f32[256,256]{1,0:T(8,128)S(1)}, u32[]{:S(2)}, u32[]{:S(2)}) collective-permute-start(f32[256,256]{1,0:T(8,128)S(1)} %get-tuple-element.35), channel_id=1, source_target_pairs={{0,5},{1,4},{2,7},{3,6},{4,1},{5,0},{6,3},{7,2},{8,13},{9,12},{10,... | collective-permute-start | bytes 786440 | tf_op jit(solution)/shard_map/ppermute | solution.py:345
  57.0 0.5 collective-permute-start.13
  57.5 3.8 %shard_map.65 = (f32[272,256]{1,0:T(8,128)S(1)}, f32[272,256]{1,0:T(8,128)S(1)}, bf16[112,256]{1,0:T(8,128)(2,1)S(1)}, f32[16,256]{1,0:T(8,128)S(1)}, bf16[2,16,512]{2,1,0:T(8,128)(2,1)S(1)}) custom-call(s32[4]{0:T(128)S(1)} %pad_add_fusion.ids, s32[4]{0:T(128)S(1)} %collective-permute-done.9.ids_p, bf16[256,4096]{1,0:T(8,128)(2,1)S(1)} %copy-done.1, ...), custom_call_target="tpu_custom_call" | custom-call | tf_op jit(solution)/shard_map/pallas_call | solution.py:260
  61.3 0.6 collective-permute-start.11
  61.9 1.6 %collective-permute-start.14 = (bf16[112,256]{1,0:T(8,128)(2,1)S(1)}, bf16[112,256]{1,0:T(8,128)(2,1)S(1)}, u32[]{:S(2)}, u32[]{:S(2)}) collective-permute-start(bf16[112,256]{1,0:T(8,128)(2,1)S(1)} %get-tuple-element.37), channel_id=1, source_target_pairs={{0,4},{2,6},{4,0},{6,2},{8,12},{10,14},{12,8},{14,10},{16,20},{18,... | collective-permute-start | bytes 172040 | tf_op jit(solution)/shard_map/ppermute | solution.py:21
  63.5 1.4 %collective-permute-start.15 = (f32[16,256]{1,0:T(8,128)S(1)}, f32[16,256]{1,0:T(8,128)S(1)}, u32[]{:S(2)}, u32[]{:S(2)}) collective-permute-start(f32[16,256]{1,0:T(8,128)S(1)} %get-tuple-element.38), channel_id=1, source_target_pairs={{0,5},{1,4},{2,7},{3,6},{4,1},{5,0},{6,3},{7,2},{8,13},{9,12},{10,... | collective-permute-start | bytes 49160 | tf_op jit(solution)/shard_map/ppermute | solution.py:345
  64.9 4.2 %collective-permute-done.13.b = f32[256,256]{1,0:T(8,128)S(1)} collective-permute-done((f32[256,256]{1,0:T(8,128)S(1)}, f32[256,256]{1,0:T(8,128)S(1)}, u32[]{:S(2)}, u32[]{:S(2)}) %collective-permute-start.13) | collective-permute-done | bytes 262176 | tf_op jit(solution)/shard_map/ppermute | solution.py:21
  69.1 1.3 %collective-permute-done.15.m_xy = f32[16,256]{1,0:T(8,128)S(1)} collective-permute-done((f32[16,256]{1,0:T(8,128)S(1)}, f32[16,256]{1,0:T(8,128)S(1)}, u32[]{:S(2)}, u32[]{:S(2)}) %collective-permute-start.15) | collective-permute-done | bytes 16416 | tf_op jit(solution)/shard_map/ppermute | solution.py:345
  70.4 1.0 %shard_map.67 = bf16[256,512]{1,0:T(8,128)(2,1)} custom-call(f32[272,256]{1,0:T(8,128)S(1)} %get-tuple-element.32.kept, bf16[2,16,512]{2,1,0:T(8,128)(2,1)S(1)} %get-tuple-element.33.up_own, f32[272,256]{1,0:T(8,128)S(1)} %collective-permute-done.11.from_x, f32[256,256]{1,0:T(8,128)S(1)} %shard_map.66.other, ...), custom_call_target="tpu_custom_call" | custom-call | tf_op jit(solution)/shard_map/pallas_call | solution.py:326
  (22 shorter events, 0.2 us)
Async XLA Ops:
  0.0 7.1 %copy-start = (bf16[1,16,1024]{2,1,0:T(8,128)(2,1)S(1)}, bf16[1,16,1024]{2,1,0:T(8,128)(2,1)}, u32[]{:S(2)}) copy-start(bf16[1,16,1024]{2,1,0:T(8,128)(2,1)} %param.9) | copy-start | bytes 98308
  0.0 27.5 %collective-permute-start.1 = (bf16[64,4096]{1,0:T(8,128)(2,1)}, bf16[64,4096]{1,0:T(8,128)(2,1)S(1)}, u32[]{:S(2)}, u32[]{:S(2)}) collective-permute-start(bf16[64,4096]{1,0:T(8,128)(2,1)} %bitcast.6), channel_id=1, source_target_pairs={{0,16},{2,18},{4,20},{6,22},{8,24},{10,26},{12,28},{14,30},{16,0},... | collective-permute-start | bytes 1572872 | tf_op jit(solution)/shard_map/ppermute | solution.py:21
  4.0 29.0 %collective-permute-start.2 = (bf16[64,4096]{1,0:T(8,128)(2,1)}, bf16[64,4096]{1,0:T(8,128)(2,1)S(1)}, u32[]{:S(2)}, u32[]{:S(2)}) collective-permute-start(bf16[64,4096]{1,0:T(8,128)(2,1)} %bitcast.7), channel_id=1, source_target_pairs={{0,8},{2,10},{4,12},{6,14},{8,0},{10,2},{12,4},{14,6},{16,24},{18,... | collective-permute-start | bytes 1572872 | tf_op jit(solution)/shard_map/ppermute | solution.py:21
  5.6 47.0 %collective-permute-start = (bf16[256,4096]{1,0:T(8,128)(2,1)}, bf16[256,4096]{1,0:T(8,128)(2,1)S(1)}, u32[]{:S(2)}, u32[]{:S(2)}) collective-permute-start(bf16[256,4096]{1,0:T(8,128)(2,1)} %mine.1), channel_id=1, source_target_pairs={{0,4},{2,6},{4,0},{6,2},{8,12},{10,14},{12,8},{14,10},{16,20},{18,... | collective-permute-start | bytes 6291464 | tf_op jit(solution)/shard_map/ppermute | solution.py:21
  27.5 7.7 %collective-permute-start.3 = (bf16[16,4608]{1,0:T(8,128)(2,1)S(1)}, bf16[16,4608]{1,0:T(8,128)(2,1)S(1)}, u32[]{:S(2)}, u32[]{:S(2)}) collective-permute-start(bf16[16,4608]{1,0:T(8,128)(2,1)S(1)} %pad_maximum_fusion), channel_id=1, source_target_pairs={{0,8},{2,10},{4,12},{6,14},{8,0},{10,2},{12,4},{14,6},{16,24},{18,... | collective-permute-start | bytes 442376 | tf_op jit(solution)/shard_map/ppermute | solution.py:21
  28.2 14.4 %collective-permute-start.4 = (bf16[16,4608]{1,0:T(8,128)(2,1)S(1)}, bf16[16,4608]{1,0:T(8,128)(2,1)S(1)}, u32[]{:S(2)}, u32[]{:S(2)}) collective-permute-start(bf16[16,4608]{1,0:T(8,128)(2,1)S(1)} %pad_maximum_fusion), channel_id=1, source_target_pairs={{0,16},{2,18},{4,20},{6,22},{8,24},{10,26},{12,28},{14,30},{16,0},... | collective-permute-start | bytes 442376 | tf_op jit(solution)/shard_map/ppermute | solution.py:21
  31.5 11.1 %collective-permute-start.5 = (bf16[16,4608]{1,0:T(8,128)(2,1)S(1)}, bf16[16,4608]{1,0:T(8,128)(2,1)S(1)}, u32[]{:S(2)}, u32[]{:S(2)}) collective-permute-start(bf16[16,4608]{1,0:T(8,128)(2,1)S(1)} %pad_maximum_fusion), channel_id=1, source_target_pairs={{0,24},{2,26},{4,28},{6,30},{8,16},{10,18},{12,20},{14,22},{16,8},... | collective-permute-start | bytes 442376 | tf_op jit(solution)/shard_map/ppermute | solution.py:21
  33.0 17.9 %copy-start.2 = (s32[2]{0:T(128)S(1)}, s32[2]{0:T(128)}, u32[]{:S(2)}) copy-start(s32[2]{0:T(128)} %param.11) | copy-start | bytes 28
  33.0 17.9 %copy-start.3 = (s32[2]{0:T(128)S(1)}, s32[2]{0:T(128)}, u32[]{:S(2)}) copy-start(s32[2]{0:T(128)} %param.10) | copy-start | bytes 28
  33.0 17.2 %collective-permute-start.6 = (bf16[64,4096]{1,0:T(8,128)(2,1)S(1)}, bf16[64,4096]{1,0:T(8,128)(2,1)S(1)}, u32[]{:S(2)}, u32[]{:S(2)}) collective-permute-start(bf16[64,4096]{1,0:T(8,128)(2,1)S(1)} %collective-permute-done.1), channel_id=1, source_target_pairs={{0,8},{2,10},{4,12},{6,14},{8,0},{10,2},{12,4},{14,6},{16,24},{18,... | collective-permute-start | bytes 1572872 | tf_op jit(solution)/shard_map/ppermute | solution.py:21
  35.2 17.3 %collective-permute-start.7 = (bf16[192,4096]{1,0:T(8,128)(2,1)S(1)}, bf16[192,4096]{1,0:T(8,128)(2,1)S(1)}, u32[]{:S(2)}, u32[]{:S(2)}) collective-permute-start(bf16[192,4096]{1,0:T(8,128)(2,1)S(1)} %constant_dynamic-update-slice_fusion.refs_0_), channel_id=1, source_target_pairs={{0,2},{2,0},{4,6},{6,4},{8,10},{10,8},{12,14},{14,12},{16,18},{18,... | collective-permute-start | bytes 4718600 | tf_op jit(solution)/shard_map/ppermute | solution.py:21
  50.2 2.3 %collective-permute-start.8 = (bf16[64,4096]{1,0:T(8,128)(2,1)S(1)}, bf16[64,4096]{1,0:T(8,128)(2,1)S(1)}, u32[]{:S(2)}, u32[]{:S(2)}) collective-permute-start(bf16[64,4096]{1,0:T(8,128)(2,1)S(1)} %collective-permute-done.6.refs_1_), channel_id=1, source_target_pairs={{0,2},{2,0},{4,6},{6,4},{8,10},{10,8},{12,14},{14,12},{16,18},{18,... | collective-permute-start | bytes 1572872 | tf_op jit(solution)/shard_map/ppermute | solution.py:21
  50.3 7.2 %collective-permute-start.10 = (bf16[64,4608]{1,0:T(8,128)(2,1)S(1)}, bf16[64,4608]{1,0:T(8,128)(2,1)S(1)}, u32[]{:S(2)}, u32[]{:S(2)}) collective-permute-start(bf16[64,4608]{1,0:T(8,128)(2,1)S(1)} %constant_dynamic-update-slice_fusion.3.refs_4_), channel_id=1, source_target_pairs={{0,2},{2,0},{4,6},{6,4},{8,10},{10,8},{12,14},{14,12},{16,18},{18,... | collective-permute-start | bytes 1769480 | tf_op jit(solution)/shard_map/ppermute | solution.py:21
  50.9 6.6 %copy-start.1 = (bf16[256,4096]{1,0:T(8,128)(2,1)S(1)}, bf16[256,4096]{1,0:T(8,128)(2,1)}, u32[]{:S(2)}) copy-start(bf16[256,4096]{1,0:T(8,128)(2,1)} %mine.1) | copy-start | bytes 6291460
  50.9 3.6 %collective-permute-start.9 = (s32[4]{0:T(128)S(1)}, s32[4]{0:T(128)S(1)}, u32[]{:S(2)}, u32[]{:S(2)}) collective-permute-start(s32[4]{0:T(128)S(1)} %pad_add_fusion.ids), channel_id=1, source_target_pairs={{0,4},{2,6},{4,0},{6,2},{8,12},{10,14},{12,8},{14,10},{16,20},{18,... | collective-permute-start | bytes 56 | tf_op jit(solution)/shard_map/ppermute | solution.py:21
  54.5 10.4 %collective-permute-start.12 = (f32[256,256]{1,0:T(8,128)S(1)}, f32[256,256]{1,0:T(8,128)S(1)}, u32[]{:S(2)}, u32[]{:S(2)}) collective-permute-start(f32[256,256]{1,0:T(8,128)S(1)} %get-tuple-element.35), channel_id=1, source_target_pairs={{0,5},{1,4},{2,7},{3,6},{4,1},{5,0},{6,3},{7,2},{8,13},{9,12},{10,... | collective-permute-start | bytes 786440 | tf_op jit(solution)/shard_map/ppermute | solution.py:345
  57.0 12.1 %collective-permute-start.13 = (f32[256,256]{1,0:T(8,128)S(1)}, f32[256,256]{1,0:T(8,128)S(1)}, u32[]{:S(2)}, u32[]{:S(2)}) collective-permute-start(f32[256,256]{1,0:T(8,128)S(1)} %get-tuple-element.36), channel_id=1, source_target_pairs={{0,4},{2,6},{4,0},{6,2},{8,12},{10,14},{12,8},{14,10},{16,20},{18,... | collective-permute-start | bytes 786440 | tf_op jit(solution)/shard_map/ppermute | solution.py:21
  61.3 9.0 %collective-permute-start.11 = (f32[272,256]{1,0:T(8,128)S(1)}, f32[272,256]{1,0:T(8,128)S(1)}, u32[]{:S(2)}, u32[]{:S(2)}) collective-permute-start(f32[272,256]{1,0:T(8,128)S(1)} %get-tuple-element.34), channel_id=1, source_target_pairs={{0,1},{1,0},{2,3},{3,2},{4,5},{5,4},{6,7},{7,6},{8,9},{9,8},{10,11... | collective-permute-start | bytes 835592 | tf_op jit(solution)/shard_map/ppermute | solution.py:24
  61.9 8.5 %collective-permute-start.14 = (bf16[112,256]{1,0:T(8,128)(2,1)S(1)}, bf16[112,256]{1,0:T(8,128)(2,1)S(1)}, u32[]{:S(2)}, u32[]{:S(2)}) collective-permute-start(bf16[112,256]{1,0:T(8,128)(2,1)S(1)} %get-tuple-element.37), channel_id=1, source_target_pairs={{0,4},{2,6},{4,0},{6,2},{8,12},{10,14},{12,8},{14,10},{16,20},{18,... | collective-permute-start | bytes 172040 | tf_op jit(solution)/shard_map/ppermute | solution.py:21
  63.5 6.9 %collective-permute-start.15 = (f32[16,256]{1,0:T(8,128)S(1)}, f32[16,256]{1,0:T(8,128)S(1)}, u32[]{:S(2)}, u32[]{:S(2)}) collective-permute-start(f32[16,256]{1,0:T(8,128)S(1)} %get-tuple-element.38), channel_id=1, source_target_pairs={{0,5},{1,4},{2,7},{3,6},{4,1},{5,0},{6,3},{7,2},{8,13},{9,12},{10,... | collective-permute-start | bytes 49160 | tf_op jit(solution)/shard_map/ppermute | solution.py:345
